TPU v7x, 512 devices: a whole 4x4x16 slice. The times are simulated.
512 devices in a mesh: segment: 4 (over y), expert: 32 (over z, core), cuts: 4 (over x).
Axes of the slice: x: 4, y: 4, z: 16, core: 2. Of those that a mesh axis runs over, the one named last changes fastest.
Arguments:
- activations: bfloat16 [4, 4096, 3072], P('segment', 'expert', 'cuts'), may hold values from -6 to 6
- pred_routes: int32 [4, 4096, 2], P('segment', 'expert'), may hold values from 0 to 7, all different within a row; in each aligned block of 128 rows (0 to 127, 128 to 255, ..., all dimensions but the last counted through in order) at most 48 rows name the same one
- true_routes: int32 [4, 4096, 2], P('segment', 'expert'), may hold values from 0 to 7, all different within a row
- gate_scores: float32 [4, 4096, 2], P('segment', 'expert'), may hold values from 0.05 to 1
- mis_rows: int32 [4, 256], P('segment', 'expert'), may hold values from 0 to 127, as said below
- mis_count: int32 [4, 32], P('segment', 'expert'), may hold values from 4 to 8, as said below
- w_up: bfloat16 [4, 32, 3072, 1024], P('segment', 'expert', 'cuts'), may hold values from -0.109375 to 0.109375
- w_down: bfloat16 [4, 32, 1024, 3072], P('segment', 'expert', None, 'cuts'), may hold values from -0.1875 to 0.1875
Outputs:
- mixed: bfloat16 [4, 4096, 3072], P('segment', 'expert', 'cuts')
Inputs may be any that keep to these rules, and one draw needn't show every extreme that they name: `pred_routes`: two different experts a token. In the rows of one device no expert is named more than 48 times, a bound that some block reaches. `true_routes`: two different experts a token. `mis_rows`: the 8 entries of each device are distinct local row indices of its own 128 tokens. `mis_count`: in every section some device uses all 8 entries.
All inputs are finite; a program needn't handle non-finite values.
Results may differ from a plain program's by a relative error of at most 0.017.
Values may be sent and summed in bfloat16 or wider, within the bound.
No kernel may reach another device: no remote copies, remote signals or barrier semaphores. Data moves between devices by JAX's collectives and lax.ppermute only.
A program may use at most 64 MiB of HBM per device.

v0:
```python
import jax
import jax.numpy as jnp
from jax import lax
from jax.sharding import PartitionSpec as P

EXP_FLIGHT = 2
EXPERT_ROW_LIMIT = 48
LISTED_ROW_LIMIT = 8


def passed_along(value, axis, by):
    count = lax.axis_size(axis)
    return lax.ppermute(value, axis, [(i, (i + by) % count) for i in range(count)])


def place_rows(routes, allowed, row_limit):
    flat_routes = routes.reshape(-1)
    usable = jnp.repeat(allowed, routes.shape[1]) & (flat_routes < EXP_FLIGHT)
    onehot = (
        (flat_routes[:, None] == jnp.arange(EXP_FLIGHT, dtype=jnp.int32)[None, :]) & usable[:, None]
    ).astype(jnp.int32)
    earlier = jnp.cumsum(onehot, axis=0) - onehot
    position = jnp.sum(earlier * onehot, axis=1)
    destination = jnp.where(usable, flat_routes * row_limit + position, -1)
    return destination.reshape(routes.shape)


def slot_matrix(destination, total, values):
    slot_ids = jnp.arange(total, dtype=jnp.int32)
    matched = destination[None, :, :] == slot_ids[:, None, None]
    return jnp.sum(jnp.where(matched, values[None, :, :], 0.0), axis=2)


def spread_rows(destination, row_limit, arrived_rows, holders_per):
    ones_map = jnp.ones(destination.shape, jnp.float32)
    picker = slot_matrix(destination, EXP_FLIGHT * row_limit, ones_map).astype(jnp.bfloat16)
    packed = jnp.dot(picker, arrived_rows, preferred_element_type=jnp.float32).astype(jnp.bfloat16)
    packed = packed.reshape(EXP_FLIGHT, row_limit, arrived_rows.shape[1])
    return jnp.repeat(packed, holders_per, axis=0)


def shards(activations, pred_routes, true_routes, gate_scores, mis_rows, mis_count, w_up, w_down):
    arrived = passed_along(activations, "segment", 1)
    arrived_rows = arrived[0]
    tok_rows = arrived_rows.shape[0]
    holders = lax.axis_size("expert")
    holders_per = holders // EXP_FLIGHT
    predicted = pred_routes[0]
    correct = true_routes[0]
    scores = gate_scores[0]
    gate = scores / jnp.sum(scores, axis=1, keepdims=True)
    listing = mis_rows[0]
    in_use = jnp.arange(listing.shape[0], dtype=jnp.int32) < mis_count[0, 0]
    listed = jnp.any(
        (jnp.arange(tok_rows, dtype=jnp.int32)[:, None] == listing[None, :]) & in_use[None, :],
        axis=1,
    )
    destinations = [
        place_rows(predicted, jnp.logical_not(listed), EXPERT_ROW_LIMIT),
        place_rows(correct, listed, LISTED_ROW_LIMIT),
    ]
    expert_row_limits = [EXPERT_ROW_LIMIT, LISTED_ROW_LIMIT]
    routed_in = lax.all_to_all(
        spread_rows(destinations[0], EXPERT_ROW_LIMIT, arrived_rows, holders_per),
        "expert",
        split_axis=0,
        concat_axis=0,
        tiled=True,
    )
    resent_in = lax.all_to_all(
        spread_rows(destinations[1], LISTED_ROW_LIMIT, arrived_rows, holders_per),
        "expert",
        split_axis=0,
        concat_axis=0,
        tiled=True,
    )
    incoming = jnp.concatenate([routed_in, resent_in], axis=1)
    slot_count = incoming.shape[1]
    rows_in = incoming.reshape(holders * slot_count, incoming.shape[2])
    partial_value = jnp.dot(rows_in, w_up[0, 0], preferred_element_type=jnp.float32)
    rounded_portion = lax.optimization_barrier(partial_value.astype(jnp.bfloat16)).astype(
        jnp.float32
    )
    hidden = lax.psum(rounded_portion.astype(jnp.bfloat16), "cuts").astype(jnp.float32)
    active = jax.nn.gelu(hidden).astype(jnp.bfloat16)
    expert_part = jnp.dot(active, w_down[0, 0], preferred_element_type=jnp.float32).astype(
        jnp.bfloat16
    )
    returned = lax.all_to_all(
        expert_part.reshape(holders, slot_count, expert_part.shape[1]),
        "expert",
        split_axis=0,
        concat_axis=0,
        tiled=True,
    )
    summed = (
        returned.astype(jnp.float32)
        .reshape(EXP_FLIGHT, holders_per, slot_count, returned.shape[2])
        .sum(axis=1)
    )
    mixed = arrived_rows.astype(jnp.float32)
    offset = 0
    for destination, row_limit in zip(destinations, expert_row_limits):
        weights_map = slot_matrix(destination, EXP_FLIGHT * row_limit, gate)
        piece_rows = summed[:, offset : offset + row_limit].reshape(
            EXP_FLIGHT * row_limit, summed.shape[2]
        )
        mixed = mixed + jnp.dot(
            weights_map.T,
            piece_rows,
            precision=lax.Precision.HIGHEST,
            preferred_element_type=jnp.float32,
        )
        offset = offset + row_limit
    return mixed.astype(jnp.bfloat16)[None]


def solution(mesh):
    placed = (
        P("segment", "expert", "cuts"),
        P("segment", "expert", None),
        P("segment", "expert", None),
        P("segment", "expert", None),
        P("segment", "expert"),
        P("segment", "expert"),
        P("segment", "expert", "cuts", None),
        P("segment", "expert", None, "cuts"),
    )
    return jax.shard_map(
        shards,
        mesh=mesh,
        in_specs=placed,
        out_specs=P("segment", "expert", "cuts"),
        check_vma=False,
    )
```

profile of v0, /device:TPU:6, one launch (start us, length us, event | category | flops | bytes accessed | tf_op | source)
XLA Modules:
  0.0 429.4 jit_solution(8370300831960138314)
XLA Ops:
  6.5 3.6 collective-permute-start
  10.1 0.8 copy.44
  11.9 0.7 fusion.21
  13.2 0.6 reduce-window.16
  13.9 0.2 slice_reduce_fusion
  14.6 0.7 fusion.29
  15.3 0.7 reduce_sum.78
  16.0 0.7 divide_bitcast_fusion
  16.9 0.8 copy.41
  18.0 0.8 broadcast_in_dim.99
  18.8 15.5 %all-to-all-start.1 = ((bf16[32,8,768]{2,1,0:T(8,128)(2,1)}), bf16[32,8,768]{2,1,0:T(8,128)(2,1)S(1)}, u32[]{:S(2)}, u32[]{:S(2)}) async-start(bf16[32,8,768]{2,1,0:T(8,128)(2,1)} %bitcast.11), calls=%async_computation.1 | async-start | bytes 786432 | tf_op jit(solution)/shard_map/all_to_all | solution.py:70
  34.7 0.6 reduce-window.14
  35.4 0.2 slice_reduce_fusion.1
  36.1 0.7 fusion.28
  36.8 0.2 convolution_convert_fusion.1
  37.0 25.5 %all-to-all-done.1 = bf16[32,8,768]{2,1,0:T(8,128)(2,1)S(1)} async-done(((bf16[32,8,768]{2,1,0:T(8,128)(2,1)}), bf16[32,8,768]{2,1,0:T(8,128)(2,1)S(1)}, u32[]{:S(2)}, u32[]{:S(2)}) %all-to-all-start.1) | async-done | bytes 393248 | tf_op jit(solution)/shard_map/all_to_all | solution.py:70
  62.7 115.7 %all_to_all.15 = bf16[32,48,768]{2,1,0:T(8,128)(2,1)S(1)} all-to-all(bf16[32,48,768]{2,1,0:T(8,128)(2,1)S(1)} %bitcast.83), channel_id=1, replica_groups=mesh['segment'=4,'expert'=32,'cuts'=4] {'expert'}, dimensions={0} | all-to-all | bytes 4718592 | tf_op jit(solution)/shard_map/all_to_all | solution.py:63
  178.5 4.5 %convolution_convert_fusion = bf16[1792,1024]{1,0:T(8,128)(2,1)} fusion(bf16[1792,768]{1,0:T(8,128)(2,1)S(1)} %bitcast.84, bf16[1,1,768,1024]{3,2,1,0:T(8,128)(2,1)S(1)} %copy-done), kind=kOutput, calls=%fused_computation.11 | convolution fusion | flops 2820407296 | bytes 7995392 | tf_op jit(solution)/shard_map/dot_general | solution.py:80
  183.1 88.9 %all-reduce.2.cloned.1.call-done = bf16[1792,1024]{1,0:T(8,128)(2,1)} async-done(((bf16[1792,1024]{1,0:T(8,128)(2,1)}), bf16[1792,1024]{1,0:T(8,128)(2,1)}) %all-reduce.2.cloned.1.call-update) | async-done | bytes 3670032 | tf_op jit(solution)/shard_map/psum | solution.py:84
  272.0 6.7 %fusion.8 = bf16[1792,768]{1,0:T(8,128)(2,1)S(1)} fusion(bf16[1792,1024]{1,0:T(8,128)(2,1)} %all-reduce.2.cloned.1.call-done, bf16[1,1,1024,768]{3,2,1,0:T(8,128)(2,1)S(1)} %copy-done.1), kind=kOutput, calls=%fused_computation.13 | convolution fusion | flops 2838298624 | bytes 7995392 | tf_op jit(solution)/shard_map/dot_general | solution.py:86
  278.7 141.7 %all_to_all.16 = bf16[32,56,768]{2,1,0:T(8,128)(2,1)S(1)} all-to-all(bf16[32,56,768]{2,1,0:T(8,128)(2,1)S(1)} %bitcast.85), channel_id=1, replica_groups=mesh['segment'=4,'expert'=32,'cuts'=4] {'expert'}, dimensions={0} | all-to-all | bytes 5505024 | tf_op jit(solution)/shard_map/all_to_all | solution.py:89
  420.4 0.4 convert_reduce_fusion
  420.8 0.5 fusion.34
  421.3 1.2 fusion.14
  (45 shorter events, 3.2 us)
Async XLA Ops:
  6.5 172.0 %copy-start = (bf16[1,1,768,1024]{3,2,1,0:T(8,128)(2,1)S(1)}, bf16[1,1,768,1024]{3,2,1,0:T(8,128)(2,1)}, u32[]{:S(2)}) copy-start(bf16[1,1,768,1024]{3,2,1,0:T(8,128)(2,1)} %param.14) | copy-start | bytes 4718596
  6.5 11.3 %collective-permute-start = (bf16[1,128,768]{2,1,0:T(8,128)(2,1)}, bf16[1,128,768]{2,1,0:T(8,128)(2,1)S(1)}, u32[]{:S(2)}, u32[]{:S(2)}) collective-permute-start(bf16[1,128,768]{2,1,0:T(8,128)(2,1)} %param.8), channel_id=1, source_target_pairs={{0,128},{128,256},{256,384},{384,0},{1,129},{129,257},{257,385},{3... | collective-permute-start | bytes 589832 | tf_op jit(solution)/shard_map/ppermute | solution.py:13
  18.8 43.7 %all-to-all-start.1 = ((bf16[32,8,768]{2,1,0:T(8,128)(2,1)}), bf16[32,8,768]{2,1,0:T(8,128)(2,1)S(1)}, u32[]{:S(2)}, u32[]{:S(2)}) async-start(bf16[32,8,768]{2,1,0:T(8,128)(2,1)} %bitcast.11), calls=%async_computation.1 | async-start | bytes 786432 | tf_op jit(solution)/shard_map/all_to_all | solution.py:70
  34.3 237.7 %all-reduce.2.cloned.1.call-start = ((), (), s32[]{:S(2)}) async-start(), calls=%async_computation.3 | async-start | bytes 7340032 | tf_op jit(solution)/shard_map/psum | solution.py:84
  183.1 89.0 %copy-start.1 = (bf16[1,1,1024,768]{3,2,1,0:T(8,128)(2,1)S(1)}, bf16[1,1,1024,768]{3,2,1,0:T(8,128)(2,1)}, u32[]{:S(2)}) copy-start(bf16[1,1,1024,768]{3,2,1,0:T(8,128)(2,1)} %param.15) | copy-start | bytes 4718596
Sparse Core Ops, SparseCore 0:
  183.2 88.7 all-reduce.1
where the time goes:
time: 433 us; the launch traced here: 429 us
  blocking collectives  257 us (59%)
  waiting for transfers between devices  114 us (26%)
  starting transfers between devices  19.1 us (4%)
  between operations  14.3 us (3%)
  matrix products  13.3 us (3%)
  other arithmetic  5.99 us (1%)
  local copies, waits for them, and re-layouts  4.93 us (1%)
    all_to_all x1, blocking collectives, shards(): lax.all_to_all(expert_part.reshape(holders, slot_count, expert_part.shape...  142 us
    all_to_all x1, blocking collectives, shards(): lax.all_to_all(spread_rows(destinations[0], EXPERT_ROW_LIMIT, arrived_row...  116 us
    psum x1, waiting for transfers between devices, shards(): lax.psum(rounded_portion.astype(jnp.bfloat16), 'cuts').astype(jnp.float32)  88.9 us
    all_to_all x1, waiting for transfers between devices, shards(): lax.all_to_all(spread_rows(destinations[1], LISTED_ROW_LIMIT, arrived_row...  25.5 us
    all_to_all x1, starting transfers between devices, shards(): lax.all_to_all(spread_rows(destinations[1], LISTED_ROW_LIMIT, arrived_row...  15.5 us
  transfers between devices with their start and end apart: 3, of which 2 were waited for; matrix products, arithmetic and copies ran while one was open for 2% of the time, Pallas kernels for 0%

commit v1 on v0

v1 whole, which is shorter than its diff:
```python
import jax
import jax.numpy as jnp
from jax import lax
from jax.sharding import PartitionSpec as P

EXP_FLIGHT = 2
ROW_LIMIT = 56
CHUNK_GROUPS = ((0,), (3,), (2,), (1,))


def moved(value, axis, targets):
    return lax.ppermute(value, axis, list(enumerate(targets)))


def along_chips(value, by):
    count = lax.axis_size("expert")
    return moved(value, "expert", [(j + 2 * by) % count for j in range(count)])


def swapped_chips(value, mask):
    return moved(value, "expert", [j ^ (2 * mask) for j in range(lax.axis_size("expert"))])


def other_core(value):
    return moved(value, "expert", [j ^ 1 for j in range(lax.axis_size("expert"))])


def along_cuts(value, by):
    count = lax.axis_size("cuts")
    return moved(value, "cuts", [(i + by) % count for i in range(count)])


def cut_sum(blocks):
    from_left = along_cuts(blocks[1], 1)
    from_right = along_cuts(blocks[3], 3)
    from_far = along_cuts(blocks[2], 2)
    return sum(part.astype(jnp.float32) for part in (blocks[0], from_left, from_right, from_far))


def cut_gather(own):
    from_right = along_cuts(own, 3)
    from_far = along_cuts(own, 2)
    from_left = along_cuts(own, 1)
    return [own, from_right, from_far, from_left]


def shards(activations, pred_routes, true_routes, gate_scores, mis_rows, mis_count, w_up, w_down):
    arrived = lax.ppermute(activations, "segment", [(i, (i + 1) % 4) for i in range(4)])[0]
    tok_rows, width = arrived.shape
    up, down = w_up[0, 0], w_down[0, 0]
    chip = lax.axis_index("expert") // 2
    cut = lax.axis_index("cuts")
    half = chip // 8
    low = (chip % 8) < 4

    scores = gate_scores[0]
    gate = scores / jnp.sum(scores, axis=1, keepdims=True)
    listing = mis_rows[0]
    in_use = jnp.arange(listing.shape[0], dtype=jnp.int32) < mis_count[0, 0]
    listed = jnp.any(
        (jnp.arange(tok_rows, dtype=jnp.int32)[:, None] == listing[None, :]) & in_use[None, :],
        axis=1,
    )
    routes = jnp.where(listed[:, None], true_routes[0], pred_routes[0])
    order = jnp.stack([half, 1 - half])
    named = routes[None, :, :] == order[:, None, None]
    chosen = jnp.any(named, axis=2)
    factor = jnp.sum(jnp.where(named, gate[None], 0.0), axis=2)
    before = jnp.arange(tok_rows)[:, None] < jnp.arange(tok_rows)[None, :]
    position = jnp.dot(
        chosen.astype(jnp.bfloat16), before.astype(jnp.bfloat16), preferred_element_type=jnp.float32
    ).astype(jnp.int32)
    picked = (
        position[:, None, :] == jnp.arange(ROW_LIMIT, dtype=jnp.int32)[None, :, None]
    ) & chosen[:, None, :]
    picker = picked.astype(jnp.bfloat16).reshape(2 * ROW_LIMIT, tok_rows)
    weights = jnp.where(picked, factor[:, None, :], 0.0).reshape(2 * ROW_LIMIT, tok_rows)

    packed = jnp.dot(picker, arrived, preferred_element_type=jnp.float32).astype(jnp.bfloat16)
    same, other = packed[:ROW_LIMIT], packed[ROW_LIMIT:]
    ahead = jnp.where(low, same, other)
    behind = jnp.where(low, other, same)

    sources = [
        same,
        along_chips(ahead, 4),
        along_chips(other, 8),
        along_chips(behind, -4),
    ]
    ring = jnp.stack(sources + sources[:3])
    chunk = lax.dynamic_slice_in_dim(ring, cut, 4, axis=0)

    def hidden_part(m):
        rows = chunk if m == 0 else swapped_chips(chunk, m)
        both = jnp.concatenate([rows, other_core(rows)], axis=1)
        flat = both.reshape(8 * ROW_LIMIT, width)
        part = jnp.dot(flat, up, preferred_element_type=jnp.float32).astype(jnp.bfloat16)
        return part.reshape(4, 2 * ROW_LIMIT, up.shape[1])

    total = jnp.zeros((4, ROW_LIMIT, width), jnp.float32)
    for group in CHUNK_GROUPS:
        parts = jnp.concatenate([hidden_part(m) for m in group], axis=1)
        hidden = cut_sum([parts[b] for b in range(4)])
        active = jax.nn.gelu(hidden).astype(jnp.bfloat16)
        gathered = jnp.stack(cut_gather(active)).reshape(4 * len(group) * 2 * ROW_LIMIT, up.shape[1])
        out = jnp.dot(gathered, down, preferred_element_type=jnp.float32).astype(jnp.bfloat16)
        out = out.reshape(4, len(group), 2, ROW_LIMIT, width)
        for at, m in enumerate(group):
            both = out[:, at, 0].astype(jnp.float32) + other_core(out[:, at, 1]).astype(jnp.float32)
            if m == 0:
                total = total + both
            else:
                total = total + swapped_chips(both.astype(jnp.bfloat16), m).astype(jnp.float32)

    rounded = total.astype(jnp.bfloat16)
    ring = jnp.concatenate([rounded, rounded[:3]])
    aligned = lax.dynamic_slice_in_dim(ring, (4 - cut) % 4, 4, axis=0)
    home = aligned[0].astype(jnp.float32)
    from_ahead = along_chips(aligned[1], -4).astype(jnp.float32)
    from_far = along_chips(aligned[2], 8).astype(jnp.float32)
    from_behind = along_chips(aligned[3], 4).astype(jnp.float32)
    same_sum = home + jnp.where(low, from_ahead, from_behind)
    other_sum = from_far + jnp.where(low, from_behind, from_ahead)
    spread = jnp.dot(
        weights.T,
        jnp.concatenate([same_sum, other_sum]),
        precision=lax.Precision.HIGHEST,
        preferred_element_type=jnp.float32,
    )
    return (arrived.astype(jnp.float32) + spread).astype(jnp.bfloat16)[None]


def solution(mesh):
    placed = (
        P("segment", "expert", "cuts"),
        P("segment", "expert", None),
        P("segment", "expert", None),
        P("segment", "expert", None),
        P("segment", "expert"),
        P("segment", "expert"),
        P("segment", "expert", "cuts", None),
        P("segment", "expert", None, "cuts"),
    )
    return jax.shard_map(
        shards,
        mesh=mesh,
        in_specs=placed,
        out_specs=P("segment", "expert", "cuts"),
        check_vma=False,
    )
```

time: 433 us -> 248 us (0.57)
  the two profiles are of different devices: /device:TPU:6 before, /device:TPU:32 now
where the time goes in v1:
time: 248 us; the launch traced here: 247 us
  starting transfers between devices  169 us (68%)
  waiting for transfers between devices  61 us (25%)
  matrix products  8.55 us (3%)
  other arithmetic  6.25 us (3%)
    ppermute x44, starting transfers between devices, moved(): return lax.ppermute(value, axis, list(enumerate(targets)))  165 us
    ppermute x44, waiting for transfers between devices, moved(): return lax.ppermute(value, axis, list(enumerate(targets)))  57 us
  transfers between devices with their start and end apart: 45, of which 11 were waited for; matrix products, arithmetic and copies ran while one was open for 5% of the time, Pallas kernels for 0%

profile of v1, /device:TPU:32, one launch (start us, length us, event | category | flops | bytes accessed | tf_op | source)
XLA Modules:
  0.0 247.0 jit_solution(16111764700093374812)
XLA Ops:
  6.1 4.0 %collective-permute-done = bf16[1,128,768]{2,1,0:T(8,128)(2,1)S(1)} collective-permute-done((bf16[1,128,768]{2,1,0:T(8,128)(2,1)}, bf16[1,128,768]{2,1,0:T(8,128)(2,1)S(1)}, u32[]{:S(2)}, u32[]{:S(2)}) %collective-permute-start) | collective-permute-done | bytes 196640 | tf_op jit(solution)/shard_map/ppermute | solution.py:48
  10.4 9.1 %collective-permute-start.1 = (bf16[56,768]{1,0:T(8,128)(2,1)S(1)}, bf16[56,768]{1,0:T(8,128)(2,1)S(1)}, u32[]{:S(2)}, u32[]{:S(2)}) collective-permute-start(bf16[56,768]{1,0:T(8,128)(2,1)S(1)} %get-tuple-element.24), channel_id=1, source_target_pairs={{0,32},{4,36},{8,40},{12,44},{16,48},{20,52},{24,56},{28,60},{32,6... | collective-permute-start | bytes 258056 | tf_op jit(solution)/shard_map/ppermute | solution.py:12
  19.5 10.0 %collective-permute-start.2 = (bf16[56,768]{1,0:T(8,128)(2,1)S(1)}, bf16[56,768]{1,0:T(8,128)(2,1)S(1)}, u32[]{:S(2)}, u32[]{:S(2)}) collective-permute-start(bf16[56,768]{1,0:T(8,128)(2,1)S(1)} %get-tuple-element.23), channel_id=1, source_target_pairs={{0,64},{4,68},{8,72},{12,76},{16,80},{20,84},{24,88},{28,92},{32,9... | collective-permute-start | bytes 258056 | tf_op jit(solution)/shard_map/ppermute | solution.py:12
  29.5 5.5 %collective-permute-start.3 = (bf16[56,768]{1,0:T(8,128)(2,1)S(1)}, bf16[56,768]{1,0:T(8,128)(2,1)S(1)}, u32[]{:S(2)}, u32[]{:S(2)}) collective-permute-start(bf16[56,768]{1,0:T(8,128)(2,1)S(1)} %get-tuple-element.22), channel_id=1, source_target_pairs={{0,96},{4,100},{8,104},{12,108},{16,112},{20,116},{24,120},{28,124... | collective-permute-start | bytes 258056 | tf_op jit(solution)/shard_map/ppermute | solution.py:12
  35.8 5.4 %collective-permute-done.3 = bf16[56,768]{1,0:T(8,128)(2,1)S(1)} collective-permute-done((bf16[56,768]{1,0:T(8,128)(2,1)S(1)}, bf16[56,768]{1,0:T(8,128)(2,1)S(1)}, u32[]{:S(2)}, u32[]{:S(2)}) %collective-permute-start.3) | collective-permute-done | bytes 86048 | tf_op jit(solution)/shard_map/ppermute | solution.py:12
  43.2 4.3 %collective-permute-start.32 = (bf16[4,56,768]{2,1,0:T(8,128)(2,1)S(1)}, bf16[4,56,768]{2,1,0:T(8,128)(2,1)S(1)}, u32[]{:S(2)}, u32[]{:S(2)}) collective-permute-start(bf16[4,56,768]{2,1,0:T(8,128)(2,1)S(1)} %constant_dynamic-slice_fusion), channel_id=1, source_target_pairs={{0,8},{4,12},{8,0},{12,4},{16,24},{20,28},{24,16},{28,20},{32,40},... | collective-permute-start | bytes 1032200 | tf_op jit(solution)/shard_map/ppermute | solution.py:12
  47.5 5.7 %collective-permute-start.22 = (bf16[4,56,768]{2,1,0:T(8,128)(2,1)S(1)}, bf16[4,56,768]{2,1,0:T(8,128)(2,1)S(1)}, u32[]{:S(2)}, u32[]{:S(2)}) collective-permute-start(bf16[4,56,768]{2,1,0:T(8,128)(2,1)S(1)} %constant_dynamic-slice_fusion), channel_id=1, source_target_pairs={{0,16},{4,20},{8,24},{12,28},{16,0},{20,4},{24,8},{28,12},{32,48},... | collective-permute-start | bytes 1032200 | tf_op jit(solution)/shard_map/ppermute | solution.py:12
  56.2 4.9 %collective-permute-start.7 = (bf16[112,1024]{1,0:T(8,128)(2,1)S(1)}, bf16[112,1024]{1,0:T(8,128)(2,1)S(1)}, u32[]{:S(2)}, u32[]{:S(2)}) collective-permute-start(bf16[112,1024]{1,0:T(8,128)(2,1)S(1)} %get-tuple-element.6), channel_id=1, source_target_pairs={{0,2},{1,3},{2,0},{3,1},{4,6},{5,7},{6,4},{7,5},{8,10},{9,11},{10,... | collective-permute-start | bytes 688136 | tf_op jit(solution)/shard_map/ppermute | solution.py:12
  67.1 9.4 %collective-permute-done.22 = bf16[4,56,768]{2,1,0:T(8,128)(2,1)S(1)} collective-permute-done((bf16[4,56,768]{2,1,0:T(8,128)(2,1)S(1)}, bf16[4,56,768]{2,1,0:T(8,128)(2,1)S(1)}, u32[]{:S(2)}, u32[]{:S(2)}) %collective-permute-start.22) | collective-permute-done | bytes 344096 | tf_op jit(solution)/shard_map/ppermute | solution.py:12
  78.4 4.7 %collective-permute-done.12 = bf16[4,56,768]{2,1,0:T(8,128)(2,1)S(1)} collective-permute-done((bf16[4,56,768]{2,1,0:T(8,128)(2,1)S(1)}, bf16[4,56,768]{2,1,0:T(8,128)(2,1)S(1)}, u32[]{:S(2)}, u32[]{:S(2)}) %collective-permute-start.12) | collective-permute-done | bytes 344096 | tf_op jit(solution)/shard_map/ppermute | solution.py:12
  91.2 4.6 %collective-permute-start.9 = (bf16[112,1024]{1,0:T(8,128)(2,1)S(1)}, bf16[112,1024]{1,0:T(8,128)(2,1)S(1)}, u32[]{:S(2)}, u32[]{:S(2)}) collective-permute-start(bf16[112,1024]{1,0:T(8,128)(2,1)S(1)} %fusion.54), channel_id=1, source_target_pairs={{0,2},{1,3},{2,0},{3,1},{4,6},{5,7},{6,4},{7,5},{8,10},{9,11},{10,... | collective-permute-start | bytes 688136 | tf_op jit(solution)/shard_map/ppermute | solution.py:12
  103.6 4.7 %collective-permute-start.35 = (bf16[112,1024]{1,0:T(8,128)(2,1)S(1)}, bf16[112,1024]{1,0:T(8,128)(2,1)S(1)}, u32[]{:S(2)}, u32[]{:S(2)}) collective-permute-start(bf16[112,1024]{1,0:T(8,128)(2,1)S(1)} %get-tuple-element.16), channel_id=1, source_target_pairs={{0,3},{1,0},{2,1},{3,2},{4,7},{5,4},{6,5},{7,6},{8,11},{9,8},{10,9... | collective-permute-start | bytes 688136 | tf_op jit(solution)/shard_map/ppermute | solution.py:12
  111.4 4.2 %collective-permute-start.26 = (bf16[112,1024]{1,0:T(8,128)(2,1)S(1)}, bf16[112,1024]{1,0:T(8,128)(2,1)S(1)}, u32[]{:S(2)}, u32[]{:S(2)}) collective-permute-start(bf16[112,1024]{1,0:T(8,128)(2,1)S(1)} %get-tuple-element.12), channel_id=1, source_target_pairs={{0,2},{1,3},{2,0},{3,1},{4,6},{5,7},{6,4},{7,5},{8,10},{9,11},{10,... | collective-permute-start | bytes 688136 | tf_op jit(solution)/shard_map/ppermute | solution.py:12
  126.3 4.5 %collective-permute-start.15 = (bf16[112,1024]{1,0:T(8,128)(2,1)S(1)}, bf16[112,1024]{1,0:T(8,128)(2,1)S(1)}, u32[]{:S(2)}, u32[]{:S(2)}) collective-permute-start(bf16[112,1024]{1,0:T(8,128)(2,1)S(1)} %get-tuple-element.10), channel_id=1, source_target_pairs={{0,3},{1,0},{2,1},{3,2},{4,7},{5,4},{6,5},{7,6},{8,11},{9,8},{10,9... | collective-permute-start | bytes 688136 | tf_op jit(solution)/shard_map/ppermute | solution.py:12
  137.8 6.0 %collective-permute-start.38 = (bf16[112,1024]{1,0:T(8,128)(2,1)S(1)}, bf16[112,1024]{1,0:T(8,128)(2,1)S(1)}, u32[]{:S(2)}, u32[]{:S(2)}) collective-permute-start(bf16[112,1024]{1,0:T(8,128)(2,1)S(1)} %fusion.78), channel_id=1, source_target_pairs={{0,2},{1,3},{2,0},{3,1},{4,6},{5,7},{6,4},{7,5},{8,10},{9,11},{10,... | collective-permute-start | bytes 688136 | tf_op jit(solution)/shard_map/ppermute | solution.py:12
  145.8 3.9 %collective-permute-start.29 = (bf16[112,1024]{1,0:T(8,128)(2,1)S(1)}, bf16[112,1024]{1,0:T(8,128)(2,1)S(1)}, u32[]{:S(2)}, u32[]{:S(2)}) collective-permute-start(bf16[112,1024]{1,0:T(8,128)(2,1)S(1)} %fusion.70), channel_id=1, source_target_pairs={{0,1},{1,2},{2,3},{3,0},{4,5},{5,6},{6,7},{7,4},{8,9},{9,10},{10,1... | collective-permute-start | bytes 688136 | tf_op jit(solution)/shard_map/ppermute | solution.py:12
  159.8 4.5 %collective-permute-start.18 = (bf16[112,1024]{1,0:T(8,128)(2,1)S(1)}, bf16[112,1024]{1,0:T(8,128)(2,1)S(1)}, u32[]{:S(2)}, u32[]{:S(2)}) collective-permute-start(bf16[112,1024]{1,0:T(8,128)(2,1)S(1)} %fusion.62), channel_id=1, source_target_pairs={{0,2},{1,3},{2,0},{3,1},{4,6},{5,7},{6,4},{7,5},{8,10},{9,11},{10,... | collective-permute-start | bytes 688136 | tf_op jit(solution)/shard_map/ppermute | solution.py:12
  179.8 5.8 %collective-permute-start.31 = (bf16[4,56,768]{2,1,0:T(8,128)(2,1)S(1)}, bf16[4,56,768]{2,1,0:T(8,128)(2,1)}, u32[]{:S(2)}, u32[]{:S(2)}) collective-permute-start(bf16[4,56,768]{2,1,0:T(8,128)(2,1)S(1)} %fusion.41), channel_id=1, source_target_pairs={{0,16},{4,20},{8,24},{12,28},{16,0},{20,4},{24,8},{28,12},{32,48},... | collective-permute-start | bytes 1032200 | tf_op jit(solution)/shard_map/ppermute | solution.py:12
  188.6 5.5 %collective-permute-done.41 = bf16[4,56,768]{2,1,0:T(8,128)(2,1)} collective-permute-done((bf16[4,56,768]{2,1,0:T(8,128)(2,1)S(1)}, bf16[4,56,768]{2,1,0:T(8,128)(2,1)}, u32[]{:S(2)}, u32[]{:S(2)}) %collective-permute-start.41) | collective-permute-done | bytes 344096 | tf_op jit(solution)/shard_map/ppermute | solution.py:12
  194.1 14.7 %collective-permute-done.31 = bf16[4,56,768]{2,1,0:T(8,128)(2,1)} collective-permute-done((bf16[4,56,768]{2,1,0:T(8,128)(2,1)S(1)}, bf16[4,56,768]{2,1,0:T(8,128)(2,1)}, u32[]{:S(2)}, u32[]{:S(2)}) %collective-permute-start.31) | collective-permute-done | bytes 344096 | tf_op jit(solution)/shard_map/ppermute | solution.py:12
  208.8 6.8 %collective-permute-done.21 = bf16[4,56,768]{2,1,0:T(8,128)(2,1)} collective-permute-done((bf16[4,56,768]{2,1,0:T(8,128)(2,1)}, bf16[4,56,768]{2,1,0:T(8,128)(2,1)}, u32[]{:S(2)}, u32[]{:S(2)}) %collective-permute-start.21) | collective-permute-done | bytes 344096 | tf_op jit(solution)/shard_map/ppermute | solution.py:12
  217.3 7.1 %collective-permute-start.43 = (bf16[56,768]{1,0:T(8,128)(2,1)S(1)}, bf16[56,768]{1,0:T(8,128)(2,1)S(1)}, u32[]{:S(2)}, u32[]{:S(2)}) collective-permute-start(bf16[56,768]{1,0:T(8,128)(2,1)S(1)} %get-tuple-element.18), channel_id=1, source_target_pairs={{0,32},{4,36},{8,40},{12,44},{16,48},{20,52},{24,56},{28,60},{32,6... | collective-permute-start | bytes 258056 | tf_op jit(solution)/shard_map/ppermute | solution.py:12
  227.0 11.8 %collective-permute-start.44 = (bf16[56,768]{1,0:T(8,128)(2,1)S(1)}, bf16[56,768]{1,0:T(8,128)(2,1)S(1)}, u32[]{:S(2)}, u32[]{:S(2)}) collective-permute-start(bf16[56,768]{1,0:T(8,128)(2,1)S(1)} %get-tuple-element.17), channel_id=1, source_target_pairs={{0,64},{4,68},{8,72},{12,76},{16,80},{20,84},{24,88},{28,92},{32,9... | collective-permute-start | bytes 258056 | tf_op jit(solution)/shard_map/ppermute | solution.py:12
  239.0 6.7 %collective-permute-done.44 = bf16[56,768]{1,0:T(8,128)(2,1)S(1)} collective-permute-done((bf16[56,768]{1,0:T(8,128)(2,1)S(1)}, bf16[56,768]{1,0:T(8,128)(2,1)S(1)}, u32[]{:S(2)}, u32[]{:S(2)}) %collective-permute-start.44) | collective-permute-done | bytes 86048 | tf_op jit(solution)/shard_map/ppermute | solution.py:12
  (132 shorter events, 91.2 us)
Async XLA Ops:
  10.4 24.6 %collective-permute-start.1 = (bf16[56,768]{1,0:T(8,128)(2,1)S(1)}, bf16[56,768]{1,0:T(8,128)(2,1)S(1)}, u32[]{:S(2)}, u32[]{:S(2)}) collective-permute-start(bf16[56,768]{1,0:T(8,128)(2,1)S(1)} %get-tuple-element.24), channel_id=1, source_target_pairs={{0,32},{4,36},{8,40},{12,44},{16,48},{20,52},{24,56},{28,60},{32,6... | collective-permute-start | bytes 258056 | tf_op jit(solution)/shard_map/ppermute | solution.py:12
  43.2 21.0 %collective-permute-start.32 = (bf16[4,56,768]{2,1,0:T(8,128)(2,1)S(1)}, bf16[4,56,768]{2,1,0:T(8,128)(2,1)S(1)}, u32[]{:S(2)}, u32[]{:S(2)}) collective-permute-start(bf16[4,56,768]{2,1,0:T(8,128)(2,1)S(1)} %constant_dynamic-slice_fusion), channel_id=1, source_target_pairs={{0,8},{4,12},{8,0},{12,4},{16,24},{20,28},{24,16},{28,20},{32,40},... | collective-permute-start | bytes 1032200 | tf_op jit(solution)/shard_map/ppermute | solution.py:12
  47.5 28.9 %collective-permute-start.22 = (bf16[4,56,768]{2,1,0:T(8,128)(2,1)S(1)}, bf16[4,56,768]{2,1,0:T(8,128)(2,1)S(1)}, u32[]{:S(2)}, u32[]{:S(2)}) collective-permute-start(bf16[4,56,768]{2,1,0:T(8,128)(2,1)S(1)} %constant_dynamic-slice_fusion), channel_id=1, source_target_pairs={{0,16},{4,20},{8,24},{12,28},{16,0},{20,4},{24,8},{28,12},{32,48},... | collective-permute-start | bytes 1032200 | tf_op jit(solution)/shard_map/ppermute | solution.py:12
  53.3 29.8 %collective-permute-start.12 = (bf16[4,56,768]{2,1,0:T(8,128)(2,1)S(1)}, bf16[4,56,768]{2,1,0:T(8,128)(2,1)S(1)}, u32[]{:S(2)}, u32[]{:S(2)}) collective-permute-start(bf16[4,56,768]{2,1,0:T(8,128)(2,1)S(1)} %constant_dynamic-slice_fusion), channel_id=1, source_target_pairs={{0,24},{4,28},{8,16},{12,20},{16,8},{20,12},{24,0},{28,4},{32,56},... | collective-permute-start | bytes 1032200 | tf_op jit(solution)/shard_map/ppermute | solution.py:12
  56.2 28.8 %collective-permute-start.7 = (bf16[112,1024]{1,0:T(8,128)(2,1)S(1)}, bf16[112,1024]{1,0:T(8,128)(2,1)S(1)}, u32[]{:S(2)}, u32[]{:S(2)}) collective-permute-start(bf16[112,1024]{1,0:T(8,128)(2,1)S(1)} %get-tuple-element.6), channel_id=1, source_target_pairs={{0,2},{1,3},{2,0},{3,1},{4,6},{5,7},{6,4},{7,5},{8,10},{9,11},{10,... | collective-permute-start | bytes 688136 | tf_op jit(solution)/shard_map/ppermute | solution.py:12
  61.2 26.3 %collective-permute-start.6 = (bf16[112,1024]{1,0:T(8,128)(2,1)S(1)}, bf16[112,1024]{1,0:T(8,128)(2,1)S(1)}, u32[]{:S(2)}, u32[]{:S(2)}) collective-permute-start(bf16[112,1024]{1,0:T(8,128)(2,1)S(1)} %get-tuple-element.7), channel_id=1, source_target_pairs={{0,3},{1,0},{2,1},{3,2},{4,7},{5,4},{6,5},{7,6},{8,11},{9,8},{10,9... | collective-permute-start | bytes 688136 | tf_op jit(solution)/shard_map/ppermute | solution.py:12
  64.3 23.2 %collective-permute-start.5 = (bf16[112,1024]{1,0:T(8,128)(2,1)S(1)}, bf16[112,1024]{1,0:T(8,128)(2,1)S(1)}, u32[]{:S(2)}, u32[]{:S(2)}) collective-permute-start(bf16[112,1024]{1,0:T(8,128)(2,1)S(1)} %get-tuple-element.5), channel_id=1, source_target_pairs={{0,1},{1,2},{2,3},{3,0},{4,5},{5,6},{6,7},{7,4},{8,9},{9,10},{10,1... | collective-permute-start | bytes 688136 | tf_op jit(solution)/shard_map/ppermute | solution.py:12
  76.5 19.4 %collective-permute-start.33 = (bf16[4,56,768]{2,1,0:T(8,128)(2,1)S(1)}, bf16[4,56,768]{2,1,0:T(8,128)(2,1)S(1)}, u32[]{:S(2)}, u32[]{:S(2)}) collective-permute-start(bf16[4,56,768]{2,1,0:T(8,128)(2,1)S(1)} %collective-permute-done.32), channel_id=1, source_target_pairs={{0,4},{4,0},{8,12},{12,8},{16,20},{20,16},{24,28},{28,24},{32,36},... | collective-permute-start | bytes 1032200 | tf_op jit(solution)/shard_map/ppermute | solution.py:12
  83.1 17.0 %collective-permute-start.23 = (bf16[4,56,768]{2,1,0:T(8,128)(2,1)S(1)}, bf16[4,56,768]{2,1,0:T(8,128)(2,1)S(1)}, u32[]{:S(2)}, u32[]{:S(2)}) collective-permute-start(bf16[4,56,768]{2,1,0:T(8,128)(2,1)S(1)} %collective-permute-done.22), channel_id=1, source_target_pairs={{0,4},{4,0},{8,12},{12,8},{16,20},{20,16},{24,28},{28,24},{32,36},... | collective-permute-start | bytes 1032200 | tf_op jit(solution)/shard_map/ppermute | solution.py:12
  85.1 18.5 %collective-permute-start.13 = (bf16[4,56,768]{2,1,0:T(8,128)(2,1)S(1)}, bf16[4,56,768]{2,1,0:T(8,128)(2,1)S(1)}, u32[]{:S(2)}, u32[]{:S(2)}) collective-permute-start(bf16[4,56,768]{2,1,0:T(8,128)(2,1)S(1)} %collective-permute-done.12), channel_id=1, source_target_pairs={{0,4},{4,0},{8,12},{12,8},{16,20},{20,16},{24,28},{28,24},{32,36},... | collective-permute-start | bytes 1032200 | tf_op jit(solution)/shard_map/ppermute | solution.py:12
  87.8 21.5 %collective-permute-start.10 = (bf16[112,1024]{1,0:T(8,128)(2,1)S(1)}, bf16[112,1024]{1,0:T(8,128)(2,1)S(1)}, u32[]{:S(2)}, u32[]{:S(2)}) collective-permute-start(bf16[112,1024]{1,0:T(8,128)(2,1)S(1)} %fusion.54), channel_id=1, source_target_pairs={{0,1},{1,2},{2,3},{3,0},{4,5},{5,6},{6,7},{7,4},{8,9},{9,10},{10,1... | collective-permute-start | bytes 688136 | tf_op jit(solution)/shard_map/ppermute | solution.py:12
  91.2 20.2 %collective-permute-start.9 = (bf16[112,1024]{1,0:T(8,128)(2,1)S(1)}, bf16[112,1024]{1,0:T(8,128)(2,1)S(1)}, u32[]{:S(2)}, u32[]{:S(2)}) collective-permute-start(bf16[112,1024]{1,0:T(8,128)(2,1)S(1)} %fusion.54), channel_id=1, source_target_pairs={{0,2},{1,3},{2,0},{3,1},{4,6},{5,7},{6,4},{7,5},{8,10},{9,11},{10,... | collective-permute-start | bytes 688136 | tf_op jit(solution)/shard_map/ppermute | solution.py:12
  95.8 19.7 %collective-permute-start.8 = (bf16[112,1024]{1,0:T(8,128)(2,1)S(1)}, bf16[112,1024]{1,0:T(8,128)(2,1)S(1)}, u32[]{:S(2)}, u32[]{:S(2)}) collective-permute-start(bf16[112,1024]{1,0:T(8,128)(2,1)S(1)} %fusion.54), channel_id=1, source_target_pairs={{0,3},{1,0},{2,1},{3,2},{4,7},{5,4},{6,5},{7,6},{8,11},{9,8},{10,9... | collective-permute-start | bytes 688136 | tf_op jit(solution)/shard_map/ppermute | solution.py:12
  100.2 19.3 %collective-permute-start.36 = (bf16[112,1024]{1,0:T(8,128)(2,1)S(1)}, bf16[112,1024]{1,0:T(8,128)(2,1)S(1)}, u32[]{:S(2)}, u32[]{:S(2)}) collective-permute-start(bf16[112,1024]{1,0:T(8,128)(2,1)S(1)} %get-tuple-element.15), channel_id=1, source_target_pairs={{0,2},{1,3},{2,0},{3,1},{4,6},{5,7},{6,4},{7,5},{8,10},{9,11},{10,... | collective-permute-start | bytes 688136 | tf_op jit(solution)/shard_map/ppermute | solution.py:12
  103.6 18.9 %collective-permute-start.35 = (bf16[112,1024]{1,0:T(8,128)(2,1)S(1)}, bf16[112,1024]{1,0:T(8,128)(2,1)S(1)}, u32[]{:S(2)}, u32[]{:S(2)}) collective-permute-start(bf16[112,1024]{1,0:T(8,128)(2,1)S(1)} %get-tuple-element.16), channel_id=1, source_target_pairs={{0,3},{1,0},{2,1},{3,2},{4,7},{5,4},{6,5},{7,6},{8,11},{9,8},{10,9... | collective-permute-start | bytes 688136 | tf_op jit(solution)/shard_map/ppermute | solution.py:12
  109.3 17.0 %collective-permute-start.34 = (bf16[112,1024]{1,0:T(8,128)(2,1)S(1)}, bf16[112,1024]{1,0:T(8,128)(2,1)S(1)}, u32[]{:S(2)}, u32[]{:S(2)}) collective-permute-start(bf16[112,1024]{1,0:T(8,128)(2,1)S(1)} %get-tuple-element.14), channel_id=1, source_target_pairs={{0,1},{1,2},{2,3},{3,0},{4,5},{5,6},{6,7},{7,4},{8,9},{9,10},{10,1... | collective-permute-start | bytes 688136 | tf_op jit(solution)/shard_map/ppermute | solution.py:12
  111.4 19.7 %collective-permute-start.26 = (bf16[112,1024]{1,0:T(8,128)(2,1)S(1)}, bf16[112,1024]{1,0:T(8,128)(2,1)S(1)}, u32[]{:S(2)}, u32[]{:S(2)}) collective-permute-start(bf16[112,1024]{1,0:T(8,128)(2,1)S(1)} %get-tuple-element.12), channel_id=1, source_target_pairs={{0,2},{1,3},{2,0},{3,1},{4,6},{5,7},{6,4},{7,5},{8,10},{9,11},{10,... | collective-permute-start | bytes 688136 | tf_op jit(solution)/shard_map/ppermute | solution.py:12
  115.6 17.5 %collective-permute-start.25 = (bf16[112,1024]{1,0:T(8,128)(2,1)S(1)}, bf16[112,1024]{1,0:T(8,128)(2,1)S(1)}, u32[]{:S(2)}, u32[]{:S(2)}) collective-permute-start(bf16[112,1024]{1,0:T(8,128)(2,1)S(1)} %get-tuple-element.13), channel_id=1, source_target_pairs={{0,3},{1,0},{2,1},{3,2},{4,7},{5,4},{6,5},{7,6},{8,11},{9,8},{10,9... | collective-permute-start | bytes 688136 | tf_op jit(solution)/shard_map/ppermute | solution.py:12
  126.3 17.5 %collective-permute-start.15 = (bf16[112,1024]{1,0:T(8,128)(2,1)S(1)}, bf16[112,1024]{1,0:T(8,128)(2,1)S(1)}, u32[]{:S(2)}, u32[]{:S(2)}) collective-permute-start(bf16[112,1024]{1,0:T(8,128)(2,1)S(1)} %get-tuple-element.10), channel_id=1, source_target_pairs={{0,3},{1,0},{2,1},{3,2},{4,7},{5,4},{6,5},{7,6},{8,11},{9,8},{10,9... | collective-permute-start | bytes 688136 | tf_op jit(solution)/shard_map/ppermute | solution.py:12
  133.1 55.5 %collective-permute-start.11 = (bf16[4,56,768]{2,1,0:T(8,128)(2,1)S(1)}, bf16[4,56,768]{2,1,0:T(8,128)(2,1)}, u32[]{:S(2)}, u32[]{:S(2)}) collective-permute-start(bf16[4,56,768]{2,1,0:T(8,128)(2,1)S(1)} %slice_bitcast_fusion.6), channel_id=1, source_target_pairs={{0,4},{4,0},{8,12},{12,8},{16,20},{20,16},{24,28},{28,24},{32,36},... | collective-permute-start | bytes 1032200 | tf_op jit(solution)/shard_map/ppermute | solution.py:12
  179.8 29.0 %collective-permute-start.31 = (bf16[4,56,768]{2,1,0:T(8,128)(2,1)S(1)}, bf16[4,56,768]{2,1,0:T(8,128)(2,1)}, u32[]{:S(2)}, u32[]{:S(2)}) collective-permute-start(bf16[4,56,768]{2,1,0:T(8,128)(2,1)S(1)} %fusion.41), channel_id=1, source_target_pairs={{0,16},{4,20},{8,24},{12,28},{16,0},{20,4},{24,8},{28,12},{32,48},... | collective-permute-start | bytes 1032200 | tf_op jit(solution)/shard_map/ppermute | solution.py:12
  186.5 29.1 %collective-permute-start.21 = (bf16[4,56,768]{2,1,0:T(8,128)(2,1)}, bf16[4,56,768]{2,1,0:T(8,128)(2,1)}, u32[]{:S(2)}, u32[]{:S(2)}) collective-permute-start(bf16[4,56,768]{2,1,0:T(8,128)(2,1)} %fusion.42), channel_id=1, source_target_pairs={{0,24},{4,28},{8,16},{12,20},{16,8},{20,12},{24,0},{28,4},{32,56},... | collective-permute-start | bytes 1032200 | tf_op jit(solution)/shard_map/ppermute | solution.py:12
  217.3 21.7 %collective-permute-start.43 = (bf16[56,768]{1,0:T(8,128)(2,1)S(1)}, bf16[56,768]{1,0:T(8,128)(2,1)S(1)}, u32[]{:S(2)}, u32[]{:S(2)}) collective-permute-start(bf16[56,768]{1,0:T(8,128)(2,1)S(1)} %get-tuple-element.18), channel_id=1, source_target_pairs={{0,32},{4,36},{8,40},{12,44},{16,48},{20,52},{24,56},{28,60},{32,6... | collective-permute-start | bytes 258056 | tf_op jit(solution)/shard_map/ppermute | solution.py:12
  227.0 18.7 %collective-permute-start.44 = (bf16[56,768]{1,0:T(8,128)(2,1)S(1)}, bf16[56,768]{1,0:T(8,128)(2,1)S(1)}, u32[]{:S(2)}, u32[]{:S(2)}) collective-permute-start(bf16[56,768]{1,0:T(8,128)(2,1)S(1)} %get-tuple-element.17), channel_id=1, source_target_pairs={{0,64},{4,68},{8,72},{12,76},{16,80},{20,84},{24,88},{28,92},{32,9... | collective-permute-start | bytes 258056 | tf_op jit(solution)/shard_map/ppermute | solution.py:12
  (24 other events, 358.1 us)

commit v2 on v1

--- a/solution.py
+++ b/solution.py
@@ -5,7 +5,7 @@
 
 EXP_FLIGHT = 2
 ROW_LIMIT = 56
-CHUNK_GROUPS = ((0,), (3,), (2,), (1,))
+CHUNK_GROUPS = ((2, 3), (0, 1))
 
 
 def moved(value, axis, targets):
@@ -37,17 +37,20 @@
     return sum(part.astype(jnp.float32) for part in (blocks[0], from_left, from_right, from_far))
 
 
-def cut_gather(own):
-    from_right = along_cuts(own, 3)
-    from_far = along_cuts(own, 2)
-    from_left = along_cuts(own, 1)
-    return [own, from_right, from_far, from_left]
+def back_home(value, step):
+    targets = []
+    for j in range(lax.axis_size("expert")):
+        for c in range(4):
+            home = [j, (j - 8) % 32, j ^ 20, (j + 8) % 32][c]
+            targets.append(home * 4 + (c + step) % 4)
+    return moved(value, ("expert", "cuts"), targets)
 
 
 def shards(activations, pred_routes, true_routes, gate_scores, mis_rows, mis_count, w_up, w_down):
     arrived = lax.ppermute(activations, "segment", [(i, (i + 1) % 4) for i in range(4)])[0]
     tok_rows, width = arrived.shape
-    up, down = w_up[0, 0], w_down[0, 0]
+    up = w_up[0, 0]
+    downs = lax.all_gather(w_down[0, 0], "cuts")
     chip = lax.axis_index("expert") // 2
     cut = lax.axis_index("cuts")
     half = chip // 8
@@ -84,7 +87,7 @@
     sources = [
         same,
         along_chips(ahead, 4),
-        along_chips(other, 8),
+        swapped_chips(other, 10),
         along_chips(behind, -4),
     ]
     ring = jnp.stack(sources + sources[:3])
@@ -102,25 +105,28 @@
         parts = jnp.concatenate([hidden_part(m) for m in group], axis=1)
         hidden = cut_sum([parts[b] for b in range(4)])
         active = jax.nn.gelu(hidden).astype(jnp.bfloat16)
-        gathered = jnp.stack(cut_gather(active)).reshape(4 * len(group) * 2 * ROW_LIMIT, up.shape[1])
-        out = jnp.dot(gathered, down, preferred_element_type=jnp.float32).astype(jnp.bfloat16)
+        out = jnp.stack(
+            [jnp.dot(active, downs[f], preferred_element_type=jnp.float32) for f in range(4)]
+        ).astype(jnp.bfloat16)
         out = out.reshape(4, len(group), 2, ROW_LIMIT, width)
+        both = out[:, :, 0].astype(jnp.float32) + other_core(out[:, :, 1]).astype(jnp.float32)
         for at, m in enumerate(group):
-            both = out[:, at, 0].astype(jnp.float32) + other_core(out[:, at, 1]).astype(jnp.float32)
             if m == 0:
-                total = total + both
+                total = total + both[:, at]
             else:
-                total = total + swapped_chips(both.astype(jnp.bfloat16), m).astype(jnp.float32)
+                total = total + swapped_chips(both[:, at].astype(jnp.bfloat16), m).astype(jnp.float32)
 
     rounded = total.astype(jnp.bfloat16)
     ring = jnp.concatenate([rounded, rounded[:3]])
-    aligned = lax.dynamic_slice_in_dim(ring, (4 - cut) % 4, 4, axis=0)
-    home = aligned[0].astype(jnp.float32)
-    from_ahead = along_chips(aligned[1], -4).astype(jnp.float32)
-    from_far = along_chips(aligned[2], 8).astype(jnp.float32)
-    from_behind = along_chips(aligned[3], 4).astype(jnp.float32)
-    same_sum = home + jnp.where(low, from_ahead, from_behind)
-    other_sum = from_far + jnp.where(low, from_behind, from_ahead)
+    slices = lax.dynamic_slice_in_dim(ring, cut, 4, axis=0)
+    same_sum = jnp.zeros((ROW_LIMIT, width), jnp.float32)
+    other_sum = same_sum
+    for step in range(4):
+        part = back_home(slices[step], step).astype(jnp.float32)
+        source = (cut - step) % 4
+        is_same = (source == 0) | ((source == 1) & low) | ((source == 3) & ~low)
+        same_sum = same_sum + jnp.where(is_same, part, 0.0)
+        other_sum = other_sum + jnp.where(is_same, 0.0, part)
     spread = jnp.dot(
         weights.T,
         jnp.concatenate([same_sum, other_sum]),

time: 248 us -> 236 us (0.952)
  starting transfers between devices: 169 us -> 105 us
  waiting for transfers between devices: 61 us -> 93.4 us
  between operations: 1.71 us -> 14.8 us
  matrix products: 8.55 us -> 14 us
    ppermute x44 -> x25, starting transfers between devices: 165 us -> 102 us  [moved(): return lax.ppermute(value, axis, list(enumerate(targets)))]
    ppermute x44 -> x25, waiting for transfers between devices: 57 us -> 87.5 us  [moved(): return lax.ppermute(value, axis, list(enumerate(targets)))]
    dot_general x4 -> x8, matrix products: 3.5 us -> 8.92 us  [shards(): jnp.dot(active, downs[f], preferred_element_type=jnp.float32)]
  transfers between devices with their start and end apart: 45 -> 27, of which waited for: 11 -> 13; matrix products, arithmetic and copies ran while one was open for 5% -> 5% of each run, Pallas kernels for 0% -> 0%
where the time goes in v2:
time: 236 us; the launch traced here: 235 us
  starting transfers between devices  105 us (44%)
  waiting for transfers between devices  93.4 us (40%)
  between operations  14.8 us (6%)
  matrix products  14 us (6%)
  other arithmetic  5.69 us (2%)
    ppermute x25, starting transfers between devices, moved(): return lax.ppermute(value, axis, list(enumerate(targets)))  102 us
    ppermute x25, waiting for transfers between devices, moved(): return lax.ppermute(value, axis, list(enumerate(targets)))  87.5 us
    dot_general x8, matrix products, shards(): jnp.dot(active, downs[f], preferred_element_type=jnp.float32)  8.92 us
    ppermute x1, waiting for transfers between devices, shards(): lax.ppermute(activations, 'segment', [(i, (i + 1) % 4) for i in range(4)])  5.18 us
  transfers between devices with their start and end apart: 27, of which 13 were waited for; matrix products, arithmetic and copies ran while one was open for 5% of the time, Pallas kernels for 0%

profile of v2, /device:TPU:32, one launch (start us, length us, event | category | flops | bytes accessed | tf_op | source)
XLA Modules:
  0.0 235.1 jit_solution(6204681380249416406)
XLA Ops:
  7.6 3.5 %collective-permute-start = (bf16[1,128,768]{2,1,0:T(8,128)(2,1)S(1)}, bf16[1,128,768]{2,1,0:T(8,128)(2,1)S(1)}, u32[]{:S(2)}, u32[]{:S(2)}) collective-permute-start(bf16[1,128,768]{2,1,0:T(8,128)(2,1)S(1)} %copy-done.7), channel_id=1, source_target_pairs={{0,128},{128,256},{256,384},{384,0},{1,129},{129,257},{257,385},{3... | collective-permute-start | bytes 589832 | tf_op jit(solution)/shard_map/ppermute | solution.py:50
  12.2 5.2 %collective-permute-done = bf16[1,128,768]{2,1,0:T(8,128)(2,1)S(1)} collective-permute-done((bf16[1,128,768]{2,1,0:T(8,128)(2,1)S(1)}, bf16[1,128,768]{2,1,0:T(8,128)(2,1)S(1)}, u32[]{:S(2)}, u32[]{:S(2)}) %collective-permute-start) | collective-permute-done | bytes 196640 | tf_op jit(solution)/shard_map/ppermute | solution.py:50
  17.6 9.1 %collective-permute-start.1 = (bf16[56,768]{1,0:T(8,128)(2,1)S(1)}, bf16[56,768]{1,0:T(8,128)(2,1)S(1)}, u32[]{:S(2)}, u32[]{:S(2)}) collective-permute-start(bf16[56,768]{1,0:T(8,128)(2,1)S(1)} %get-tuple-element.21), channel_id=1, source_target_pairs={{0,32},{4,36},{8,40},{12,44},{16,48},{20,52},{24,56},{28,60},{32,6... | collective-permute-start | bytes 258056 | tf_op jit(solution)/shard_map/ppermute | solution.py:12
  26.7 9.1 %collective-permute-start.2 = (bf16[56,768]{1,0:T(8,128)(2,1)S(1)}, bf16[56,768]{1,0:T(8,128)(2,1)S(1)}, u32[]{:S(2)}, u32[]{:S(2)}) collective-permute-start(bf16[56,768]{1,0:T(8,128)(2,1)S(1)} %get-tuple-element.20), channel_id=1, source_target_pairs={{0,80},{4,84},{8,88},{12,92},{16,64},{20,68},{24,72},{28,76},{32,1... | collective-permute-start | bytes 258056 | tf_op jit(solution)/shard_map/ppermute | solution.py:12
  35.9 5.5 %collective-permute-start.3 = (bf16[56,768]{1,0:T(8,128)(2,1)S(1)}, bf16[56,768]{1,0:T(8,128)(2,1)S(1)}, u32[]{:S(2)}, u32[]{:S(2)}) collective-permute-start(bf16[56,768]{1,0:T(8,128)(2,1)S(1)} %get-tuple-element.19), channel_id=1, source_target_pairs={{0,96},{4,100},{8,104},{12,108},{16,112},{20,116},{24,120},{28,124... | collective-permute-start | bytes 258056 | tf_op jit(solution)/shard_map/ppermute | solution.py:12
  41.4 4.5 %collective-permute-done.2 = bf16[56,768]{1,0:T(8,128)(2,1)S(1)} collective-permute-done((bf16[56,768]{1,0:T(8,128)(2,1)S(1)}, bf16[56,768]{1,0:T(8,128)(2,1)S(1)}, u32[]{:S(2)}, u32[]{:S(2)}) %collective-permute-start.2) | collective-permute-done | bytes 86048 | tf_op jit(solution)/shard_map/ppermute | solution.py:12
  45.8 2.8 %collective-permute-done.3 = bf16[56,768]{1,0:T(8,128)(2,1)S(1)} collective-permute-done((bf16[56,768]{1,0:T(8,128)(2,1)S(1)}, bf16[56,768]{1,0:T(8,128)(2,1)S(1)}, u32[]{:S(2)}, u32[]{:S(2)}) %collective-permute-start.3) | collective-permute-done | bytes 86048 | tf_op jit(solution)/shard_map/ppermute | solution.py:12
  50.6 6.3 %collective-permute-start.6 = (bf16[4,56,768]{2,1,0:T(8,128)(2,1)S(1)}, bf16[4,56,768]{2,1,0:T(8,128)(2,1)S(1)}, u32[]{:S(2)}, u32[]{:S(2)}) collective-permute-start(bf16[4,56,768]{2,1,0:T(8,128)(2,1)S(1)} %constant_dynamic-slice_fusion), channel_id=1, source_target_pairs={{0,24},{4,28},{8,16},{12,20},{16,8},{20,12},{24,0},{28,4},{32,56},... | collective-permute-start | bytes 1032200 | tf_op jit(solution)/shard_map/ppermute | solution.py:12
  60.8 13.0 %collective-permute-done.4 = bf16[4,56,768]{2,1,0:T(8,128)(2,1)S(1)} collective-permute-done((bf16[4,56,768]{2,1,0:T(8,128)(2,1)S(1)}, bf16[4,56,768]{2,1,0:T(8,128)(2,1)S(1)}, u32[]{:S(2)}, u32[]{:S(2)}) %collective-permute-start.4) | collective-permute-done | bytes 344096 | tf_op jit(solution)/shard_map/ppermute | solution.py:12
  75.8 7.5 %collective-permute-done.6 = bf16[4,56,768]{2,1,0:T(8,128)(2,1)S(1)} collective-permute-done((bf16[4,56,768]{2,1,0:T(8,128)(2,1)S(1)}, bf16[4,56,768]{2,1,0:T(8,128)(2,1)S(1)}, u32[]{:S(2)}, u32[]{:S(2)}) %collective-permute-start.6) | collective-permute-done | bytes 344096 | tf_op jit(solution)/shard_map/ppermute | solution.py:12
  90.6 4.9 %collective-permute-start.10 = (bf16[224,1024]{1,0:T(8,128)(2,1)S(1)}, bf16[224,1024]{1,0:T(8,128)(2,1)S(1)}, u32[]{:S(2)}, u32[]{:S(2)}) collective-permute-start(bf16[224,1024]{1,0:T(8,128)(2,1)S(1)} %get-tuple-element.6), channel_id=1, source_target_pairs={{0,2},{1,3},{2,0},{3,1},{4,6},{5,7},{6,4},{7,5},{8,10},{9,11},{10,... | collective-permute-start | bytes 1376264 | tf_op jit(solution)/shard_map/ppermute | solution.py:12
  95.5 2.5 %collective-permute-start.8 = (bf16[224,1024]{1,0:T(8,128)(2,1)S(1)}, bf16[224,1024]{1,0:T(8,128)(2,1)S(1)}, u32[]{:S(2)}, u32[]{:S(2)}) collective-permute-start(bf16[224,1024]{1,0:T(8,128)(2,1)S(1)} %get-tuple-element.5), channel_id=1, source_target_pairs={{0,1},{1,2},{2,3},{3,0},{4,5},{5,6},{6,7},{7,4},{8,9},{9,10},{10,1... | collective-permute-start | bytes 1376264 | tf_op jit(solution)/shard_map/ppermute | solution.py:12
  98.0 4.6 %collective-permute-start.9 = (bf16[224,1024]{1,0:T(8,128)(2,1)S(1)}, bf16[224,1024]{1,0:T(8,128)(2,1)S(1)}, u32[]{:S(2)}, u32[]{:S(2)}) collective-permute-start(bf16[224,1024]{1,0:T(8,128)(2,1)S(1)} %get-tuple-element.7), channel_id=1, source_target_pairs={{0,3},{1,0},{2,1},{3,2},{4,7},{5,4},{6,5},{7,6},{8,11},{9,8},{10,9... | collective-permute-start | bytes 1376264 | tf_op jit(solution)/shard_map/ppermute | solution.py:12
  105.6 5.1 %collective-permute-start.18 = (bf16[224,1024]{1,0:T(8,128)(2,1)S(1)}, bf16[224,1024]{1,0:T(8,128)(2,1)S(1)}, u32[]{:S(2)}, u32[]{:S(2)}) collective-permute-start(bf16[224,1024]{1,0:T(8,128)(2,1)S(1)} %get-tuple-element.10), channel_id=1, source_target_pairs={{0,3},{1,0},{2,1},{3,2},{4,7},{5,4},{6,5},{7,6},{8,11},{9,8},{10,9... | collective-permute-start | bytes 1376264 | tf_op jit(solution)/shard_map/ppermute | solution.py:12
  112.6 3.8 %collective-permute-done.8 = bf16[224,1024]{1,0:T(8,128)(2,1)S(1)} collective-permute-done((bf16[224,1024]{1,0:T(8,128)(2,1)S(1)}, bf16[224,1024]{1,0:T(8,128)(2,1)S(1)}, u32[]{:S(2)}, u32[]{:S(2)}) %collective-permute-start.8) | collective-permute-done | bytes 458784 | tf_op jit(solution)/shard_map/ppermute | solution.py:12
  118.6 8.4 %collective-permute-done.17 = bf16[224,1024]{1,0:T(8,128)(2,1)S(1)} collective-permute-done((bf16[224,1024]{1,0:T(8,128)(2,1)S(1)}, bf16[224,1024]{1,0:T(8,128)(2,1)S(1)}, u32[]{:S(2)}, u32[]{:S(2)}) %collective-permute-start.17) | collective-permute-done | bytes 458784 | tf_op jit(solution)/shard_map/ppermute | solution.py:12
  127.1 8.9 %collective-permute-done.19 = bf16[224,1024]{1,0:T(8,128)(2,1)S(1)} collective-permute-done((bf16[224,1024]{1,0:T(8,128)(2,1)S(1)}, bf16[224,1024]{1,0:T(8,128)(2,1)S(1)}, u32[]{:S(2)}, u32[]{:S(2)}) %collective-permute-start.19) | collective-permute-done | bytes 458784 | tf_op jit(solution)/shard_map/ppermute | solution.py:12
  156.9 6.3 %collective-permute-start.21 = (bf16[4,56,768]{2,1,0:T(8,128)(2,1)}, bf16[4,56,768]{2,1,0:T(8,128)(2,1)}, u32[]{:S(2)}, u32[]{:S(2)}) collective-permute-start(bf16[4,56,768]{2,1,0:T(8,128)(2,1)} %fusion.131), channel_id=1, source_target_pairs={{0,8},{4,12},{8,0},{12,4},{16,24},{20,28},{24,16},{28,20},{32,40},... | collective-permute-start | bytes 1032200 | tf_op jit(solution)/shard_map/ppermute | solution.py:12
  163.4 13.7 %collective-permute-done.12 = bf16[4,56,768]{2,1,0:T(8,128)(2,1)} collective-permute-done((bf16[4,56,768]{2,1,0:T(8,128)(2,1)}, bf16[4,56,768]{2,1,0:T(8,128)(2,1)}, u32[]{:S(2)}, u32[]{:S(2)}) %collective-permute-start.12) | collective-permute-done | bytes 344096 | tf_op jit(solution)/shard_map/ppermute | solution.py:12
  177.1 7.1 %collective-permute-done.13 = bf16[4,56,768]{2,1,0:T(8,128)(2,1)} collective-permute-done((bf16[4,56,768]{2,1,0:T(8,128)(2,1)S(1)}, bf16[4,56,768]{2,1,0:T(8,128)(2,1)}, u32[]{:S(2)}, u32[]{:S(2)}) %collective-permute-start.13) | collective-permute-done | bytes 344096 | tf_op jit(solution)/shard_map/ppermute | solution.py:12
  186.4 8.4 %collective-permute-start.23 = (bf16[56,768]{1,0:T(8,128)(2,1)S(1)}, bf16[56,768]{1,0:T(8,128)(2,1)S(1)}, u32[]{:S(2)}, u32[]{:S(2)}) collective-permute-start(bf16[56,768]{1,0:T(8,128)(2,1)S(1)} %get-tuple-element.17), channel_id=1, source_target_pairs={{0,1},{1,98},{2,83},{3,32},{4,5},{5,102},{6,87},{7,36},{8,9},{9,10... | collective-permute-start | bytes 258056 | tf_op jit(solution)/shard_map/ppermute | solution.py:12
  194.8 8.2 %collective-permute-start.24 = (bf16[56,768]{1,0:T(8,128)(2,1)S(1)}, bf16[56,768]{1,0:T(8,128)(2,1)S(1)}, u32[]{:S(2)}, u32[]{:S(2)}) collective-permute-start(bf16[56,768]{1,0:T(8,128)(2,1)S(1)} %get-tuple-element.16), channel_id=1, source_target_pairs={{0,2},{1,99},{2,80},{3,33},{4,6},{5,103},{6,84},{7,37},{8,10},{9,1... | collective-permute-start | bytes 258056 | tf_op jit(solution)/shard_map/ppermute | solution.py:12
  203.0 6.9 %collective-permute-start.25 = (bf16[56,768]{1,0:T(8,128)(2,1)S(1)}, bf16[56,768]{1,0:T(8,128)(2,1)S(1)}, u32[]{:S(2)}, u32[]{:S(2)}) collective-permute-start(bf16[56,768]{1,0:T(8,128)(2,1)S(1)} %get-tuple-element.15), channel_id=1, source_target_pairs={{0,3},{1,96},{2,81},{3,34},{4,7},{5,100},{6,85},{7,38},{8,11},{9,1... | collective-permute-start | bytes 258056 | tf_op jit(solution)/shard_map/ppermute | solution.py:12
  210.2 16.8 %collective-permute-done.24 = bf16[56,768]{1,0:T(8,128)(2,1)S(1)} collective-permute-done((bf16[56,768]{1,0:T(8,128)(2,1)S(1)}, bf16[56,768]{1,0:T(8,128)(2,1)S(1)}, u32[]{:S(2)}, u32[]{:S(2)}) %collective-permute-start.24) | collective-permute-done | bytes 86048 | tf_op jit(solution)/shard_map/ppermute | solution.py:12
  (106 shorter events, 48.3 us)
Async XLA Ops:
  6.5 130.8 %all-gather.3.cloned.1.call-start = ((), (), s32[]{:S(2)}) async-start(), calls=%async_computation | async-start | bytes 7864320 | tf_op jit(solution)/shard_map/all_gather | solution.py:53
  7.6 9.8 %collective-permute-start = (bf16[1,128,768]{2,1,0:T(8,128)(2,1)S(1)}, bf16[1,128,768]{2,1,0:T(8,128)(2,1)S(1)}, u32[]{:S(2)}, u32[]{:S(2)}) collective-permute-start(bf16[1,128,768]{2,1,0:T(8,128)(2,1)S(1)} %copy-done.7), channel_id=1, source_target_pairs={{0,128},{128,256},{256,384},{384,0},{1,129},{129,257},{257,385},{3... | collective-permute-start | bytes 589832 | tf_op jit(solution)/shard_map/ppermute | solution.py:50
  17.6 23.7 %collective-permute-start.1 = (bf16[56,768]{1,0:T(8,128)(2,1)S(1)}, bf16[56,768]{1,0:T(8,128)(2,1)S(1)}, u32[]{:S(2)}, u32[]{:S(2)}) collective-permute-start(bf16[56,768]{1,0:T(8,128)(2,1)S(1)} %get-tuple-element.21), channel_id=1, source_target_pairs={{0,32},{4,36},{8,40},{12,44},{16,48},{20,52},{24,56},{28,60},{32,6... | collective-permute-start | bytes 258056 | tf_op jit(solution)/shard_map/ppermute | solution.py:12
  26.7 19.1 %collective-permute-start.2 = (bf16[56,768]{1,0:T(8,128)(2,1)S(1)}, bf16[56,768]{1,0:T(8,128)(2,1)S(1)}, u32[]{:S(2)}, u32[]{:S(2)}) collective-permute-start(bf16[56,768]{1,0:T(8,128)(2,1)S(1)} %get-tuple-element.20), channel_id=1, source_target_pairs={{0,80},{4,84},{8,88},{12,92},{16,64},{20,68},{24,72},{28,76},{32,1... | collective-permute-start | bytes 258056 | tf_op jit(solution)/shard_map/ppermute | solution.py:12
  35.9 12.7 %collective-permute-start.3 = (bf16[56,768]{1,0:T(8,128)(2,1)S(1)}, bf16[56,768]{1,0:T(8,128)(2,1)S(1)}, u32[]{:S(2)}, u32[]{:S(2)}) collective-permute-start(bf16[56,768]{1,0:T(8,128)(2,1)S(1)} %get-tuple-element.19), channel_id=1, source_target_pairs={{0,96},{4,100},{8,104},{12,108},{16,112},{20,116},{24,120},{28,124... | collective-permute-start | bytes 258056 | tf_op jit(solution)/shard_map/ppermute | solution.py:12
  48.7 25.2 %collective-permute-start.4 = (bf16[4,56,768]{2,1,0:T(8,128)(2,1)S(1)}, bf16[4,56,768]{2,1,0:T(8,128)(2,1)S(1)}, u32[]{:S(2)}, u32[]{:S(2)}) collective-permute-start(bf16[4,56,768]{2,1,0:T(8,128)(2,1)S(1)} %constant_dynamic-slice_fusion), channel_id=1, source_target_pairs={{0,16},{4,20},{8,24},{12,28},{16,0},{20,4},{24,8},{28,12},{32,48},... | collective-permute-start | bytes 1032200 | tf_op jit(solution)/shard_map/ppermute | solution.py:12
  50.6 32.6 %collective-permute-start.6 = (bf16[4,56,768]{2,1,0:T(8,128)(2,1)S(1)}, bf16[4,56,768]{2,1,0:T(8,128)(2,1)S(1)}, u32[]{:S(2)}, u32[]{:S(2)}) collective-permute-start(bf16[4,56,768]{2,1,0:T(8,128)(2,1)S(1)} %constant_dynamic-slice_fusion), channel_id=1, source_target_pairs={{0,24},{4,28},{8,16},{12,20},{16,8},{20,12},{24,0},{28,4},{32,56},... | collective-permute-start | bytes 1032200 | tf_op jit(solution)/shard_map/ppermute | solution.py:12
  57.0 28.3 %collective-permute-start.15 = (bf16[4,56,768]{2,1,0:T(8,128)(2,1)S(1)}, bf16[4,56,768]{2,1,0:T(8,128)(2,1)S(1)}, u32[]{:S(2)}, u32[]{:S(2)}) collective-permute-start(bf16[4,56,768]{2,1,0:T(8,128)(2,1)S(1)} %constant_dynamic-slice_fusion), channel_id=1, source_target_pairs={{0,8},{4,12},{8,0},{12,4},{16,24},{20,28},{24,16},{28,20},{32,40},... | collective-permute-start | bytes 1032200 | tf_op jit(solution)/shard_map/ppermute | solution.py:12
  58.9 28.7 %collective-permute-start.14 = (bf16[4,56,768]{2,1,0:T(8,128)(2,1)S(1)}, bf16[4,56,768]{2,1,0:T(8,128)(2,1)S(1)}, u32[]{:S(2)}, u32[]{:S(2)}) collective-permute-start(bf16[4,56,768]{2,1,0:T(8,128)(2,1)S(1)} %constant_dynamic-slice_fusion), channel_id=1, source_target_pairs={{0,4},{4,0},{8,12},{12,8},{16,20},{20,16},{24,28},{28,24},{32,36},... | collective-permute-start | bytes 1032200 | tf_op jit(solution)/shard_map/ppermute | solution.py:12
  73.9 14.7 %collective-permute-start.5 = (bf16[4,56,768]{2,1,0:T(8,128)(2,1)S(1)}, bf16[4,56,768]{2,1,0:T(8,128)(2,1)S(1)}, u32[]{:S(2)}, u32[]{:S(2)}) collective-permute-start(bf16[4,56,768]{2,1,0:T(8,128)(2,1)S(1)} %collective-permute-done.4), channel_id=1, source_target_pairs={{0,4},{4,0},{8,12},{12,8},{16,20},{20,16},{24,28},{28,24},{32,36},... | collective-permute-start | bytes 1032200 | tf_op jit(solution)/shard_map/ppermute | solution.py:12
  85.3 17.3 %collective-permute-start.16 = (bf16[4,56,768]{2,1,0:T(8,128)(2,1)S(1)}, bf16[4,56,768]{2,1,0:T(8,128)(2,1)S(1)}, u32[]{:S(2)}, u32[]{:S(2)}) collective-permute-start(bf16[4,56,768]{2,1,0:T(8,128)(2,1)S(1)} %collective-permute-done.15), channel_id=1, source_target_pairs={{0,4},{4,0},{8,12},{12,8},{16,20},{20,16},{24,28},{28,24},{32,36},... | collective-permute-start | bytes 1032200 | tf_op jit(solution)/shard_map/ppermute | solution.py:12
  90.6 20.1 %collective-permute-start.10 = (bf16[224,1024]{1,0:T(8,128)(2,1)S(1)}, bf16[224,1024]{1,0:T(8,128)(2,1)S(1)}, u32[]{:S(2)}, u32[]{:S(2)}) collective-permute-start(bf16[224,1024]{1,0:T(8,128)(2,1)S(1)} %get-tuple-element.6), channel_id=1, source_target_pairs={{0,2},{1,3},{2,0},{3,1},{4,6},{5,7},{6,4},{7,5},{8,10},{9,11},{10,... | collective-permute-start | bytes 1376264 | tf_op jit(solution)/shard_map/ppermute | solution.py:12
  95.5 20.9 %collective-permute-start.8 = (bf16[224,1024]{1,0:T(8,128)(2,1)S(1)}, bf16[224,1024]{1,0:T(8,128)(2,1)S(1)}, u32[]{:S(2)}, u32[]{:S(2)}) collective-permute-start(bf16[224,1024]{1,0:T(8,128)(2,1)S(1)} %get-tuple-element.5), channel_id=1, source_target_pairs={{0,1},{1,2},{2,3},{3,0},{4,5},{5,6},{6,7},{7,4},{8,9},{9,10},{10,1... | collective-permute-start | bytes 1376264 | tf_op jit(solution)/shard_map/ppermute | solution.py:12
  98.0 19.3 %collective-permute-start.9 = (bf16[224,1024]{1,0:T(8,128)(2,1)S(1)}, bf16[224,1024]{1,0:T(8,128)(2,1)S(1)}, u32[]{:S(2)}, u32[]{:S(2)}) collective-permute-start(bf16[224,1024]{1,0:T(8,128)(2,1)S(1)} %get-tuple-element.7), channel_id=1, source_target_pairs={{0,3},{1,0},{2,1},{3,2},{4,7},{5,4},{6,5},{7,6},{8,11},{9,8},{10,9... | collective-permute-start | bytes 1376264 | tf_op jit(solution)/shard_map/ppermute | solution.py:12
  103.6 23.3 %collective-permute-start.17 = (bf16[224,1024]{1,0:T(8,128)(2,1)S(1)}, bf16[224,1024]{1,0:T(8,128)(2,1)S(1)}, u32[]{:S(2)}, u32[]{:S(2)}) collective-permute-start(bf16[224,1024]{1,0:T(8,128)(2,1)S(1)} %get-tuple-element.8), channel_id=1, source_target_pairs={{0,1},{1,2},{2,3},{3,0},{4,5},{5,6},{6,7},{7,4},{8,9},{9,10},{10,1... | collective-permute-start | bytes 1376264 | tf_op jit(solution)/shard_map/ppermute | solution.py:12
  105.6 21.6 %collective-permute-start.18 = (bf16[224,1024]{1,0:T(8,128)(2,1)S(1)}, bf16[224,1024]{1,0:T(8,128)(2,1)S(1)}, u32[]{:S(2)}, u32[]{:S(2)}) collective-permute-start(bf16[224,1024]{1,0:T(8,128)(2,1)S(1)} %get-tuple-element.10), channel_id=1, source_target_pairs={{0,3},{1,0},{2,1},{3,2},{4,7},{5,4},{6,5},{7,6},{8,11},{9,8},{10,9... | collective-permute-start | bytes 1376264 | tf_op jit(solution)/shard_map/ppermute | solution.py:12
  110.7 25.3 %collective-permute-start.19 = (bf16[224,1024]{1,0:T(8,128)(2,1)S(1)}, bf16[224,1024]{1,0:T(8,128)(2,1)S(1)}, u32[]{:S(2)}, u32[]{:S(2)}) collective-permute-start(bf16[224,1024]{1,0:T(8,128)(2,1)S(1)} %get-tuple-element.9), channel_id=1, source_target_pairs={{0,2},{1,3},{2,0},{3,1},{4,6},{5,7},{6,4},{7,5},{8,10},{9,11},{10,... | collective-permute-start | bytes 1376264 | tf_op jit(solution)/shard_map/ppermute | solution.py:12
  152.1 24.9 %collective-permute-start.12 = (bf16[4,56,768]{2,1,0:T(8,128)(2,1)}, bf16[4,56,768]{2,1,0:T(8,128)(2,1)}, u32[]{:S(2)}, u32[]{:S(2)}) collective-permute-start(bf16[4,56,768]{2,1,0:T(8,128)(2,1)} %get-tuple-element.11), channel_id=1, source_target_pairs={{0,16},{4,20},{8,24},{12,28},{16,0},{20,4},{24,8},{28,12},{32,48},... | collective-permute-start | bytes 1032200 | tf_op jit(solution)/shard_map/ppermute | solution.py:12
  154.1 30.1 %collective-permute-start.13 = (bf16[4,56,768]{2,1,0:T(8,128)(2,1)S(1)}, bf16[4,56,768]{2,1,0:T(8,128)(2,1)}, u32[]{:S(2)}, u32[]{:S(2)}) collective-permute-start(bf16[4,56,768]{2,1,0:T(8,128)(2,1)S(1)} %get-tuple-element.12), channel_id=1, source_target_pairs={{0,24},{4,28},{8,16},{12,20},{16,8},{20,12},{24,0},{28,4},{32,56},... | collective-permute-start | bytes 1032200 | tf_op jit(solution)/shard_map/ppermute | solution.py:12
  156.9 27.3 %collective-permute-start.21 = (bf16[4,56,768]{2,1,0:T(8,128)(2,1)}, bf16[4,56,768]{2,1,0:T(8,128)(2,1)}, u32[]{:S(2)}, u32[]{:S(2)}) collective-permute-start(bf16[4,56,768]{2,1,0:T(8,128)(2,1)} %fusion.131), channel_id=1, source_target_pairs={{0,8},{4,12},{8,0},{12,4},{16,24},{20,28},{24,16},{28,20},{32,40},... | collective-permute-start | bytes 1032200 | tf_op jit(solution)/shard_map/ppermute | solution.py:12
  185.7 24.4 %collective-permute-start.22 = (bf16[56,768]{1,0:T(8,128)(2,1)S(1)}, bf16[56,768]{1,0:T(8,128)(2,1)S(1)}, u32[]{:S(2)}, u32[]{:S(2)}) collective-permute-start(bf16[56,768]{1,0:T(8,128)(2,1)S(1)} %get-tuple-element.18), channel_id=1, source_target_pairs={{0,0},{1,97},{2,82},{3,35},{4,4},{5,101},{6,86},{7,39},{8,8},{9,10... | collective-permute-start | bytes 258056 | tf_op jit(solution)/shard_map/ppermute | solution.py:12
  186.4 23.7 %collective-permute-start.23 = (bf16[56,768]{1,0:T(8,128)(2,1)S(1)}, bf16[56,768]{1,0:T(8,128)(2,1)S(1)}, u32[]{:S(2)}, u32[]{:S(2)}) collective-permute-start(bf16[56,768]{1,0:T(8,128)(2,1)S(1)} %get-tuple-element.17), channel_id=1, source_target_pairs={{0,1},{1,98},{2,83},{3,32},{4,5},{5,102},{6,87},{7,36},{8,9},{9,10... | collective-permute-start | bytes 258056 | tf_op jit(solution)/shard_map/ppermute | solution.py:12
  194.8 32.1 %collective-permute-start.24 = (bf16[56,768]{1,0:T(8,128)(2,1)S(1)}, bf16[56,768]{1,0:T(8,128)(2,1)S(1)}, u32[]{:S(2)}, u32[]{:S(2)}) collective-permute-start(bf16[56,768]{1,0:T(8,128)(2,1)S(1)} %get-tuple-element.16), channel_id=1, source_target_pairs={{0,2},{1,99},{2,80},{3,33},{4,6},{5,103},{6,84},{7,37},{8,10},{9,1... | collective-permute-start | bytes 258056 | tf_op jit(solution)/shard_map/ppermute | solution.py:12
  203.0 24.0 %collective-permute-start.25 = (bf16[56,768]{1,0:T(8,128)(2,1)S(1)}, bf16[56,768]{1,0:T(8,128)(2,1)S(1)}, u32[]{:S(2)}, u32[]{:S(2)}) collective-permute-start(bf16[56,768]{1,0:T(8,128)(2,1)S(1)} %get-tuple-element.15), channel_id=1, source_target_pairs={{0,3},{1,96},{2,81},{3,34},{4,7},{5,100},{6,85},{7,38},{8,11},{9,1... | collective-permute-start | bytes 258056 | tf_op jit(solution)/shard_map/ppermute | solution.py:12
  (12 other events, 154.2 us)
Sparse Core Ops, SparseCore 0:
  9.5 77.4 all-gather.2

commit v3 on v2

--- a/solution.py
+++ b/solution.py
@@ -5,7 +5,7 @@
 
 EXP_FLIGHT = 2
 ROW_LIMIT = 56
-CHUNK_GROUPS = ((2, 3), (0, 1))
+CHUNK_GROUPS = ((0, 1), (2, 3))
 
 
 def moved(value, axis, targets):
@@ -37,6 +37,14 @@
     return sum(part.astype(jnp.float32) for part in (blocks[0], from_left, from_right, from_far))
 
 
+def cut_slices(own):
+    from_right = along_cuts(own, 3)
+    from_left = along_cuts(own, 1)
+    part = own.shape[0] // 2
+    far = [along_cuts(from_right[:part], 3), along_cuts(from_left[part:], 1)]
+    return [[own], [from_right], far, [from_left]]
+
+
 def back_home(value, step):
     targets = []
     for j in range(lax.axis_size("expert")):
@@ -49,8 +57,9 @@
 def shards(activations, pred_routes, true_routes, gate_scores, mis_rows, mis_count, w_up, w_down):
     arrived = lax.ppermute(activations, "segment", [(i, (i + 1) % 4) for i in range(4)])[0]
     tok_rows, width = arrived.shape
-    up = w_up[0, 0]
-    downs = lax.all_gather(w_down[0, 0], "cuts")
+    up = jnp.concatenate([w_up[0, 0], other_core(w_up[0, 0])], axis=1)
+    ff = w_down.shape[2]
+    downs = [pieces + [other_core(piece) for piece in pieces] for pieces in cut_slices(w_down[0, 0])]
     chip = lax.axis_index("expert") // 2
     cut = lax.axis_index("cuts")
     half = chip // 8
@@ -95,34 +104,37 @@
 
     def hidden_part(m):
         rows = chunk if m == 0 else swapped_chips(chunk, m)
-        both = jnp.concatenate([rows, other_core(rows)], axis=1)
-        flat = both.reshape(8 * ROW_LIMIT, width)
+        flat = rows.reshape(4 * ROW_LIMIT, width)
         part = jnp.dot(flat, up, preferred_element_type=jnp.float32).astype(jnp.bfloat16)
-        return part.reshape(4, 2 * ROW_LIMIT, up.shape[1])
+        return part.reshape(4, ROW_LIMIT, 2 * ff)
+
+    def times_down(active, pieces):
+        low_unit, summed = 0, None
+        for piece in pieces:
+            high_unit = low_unit + piece.shape[0]
+            term = jnp.dot(active[:, low_unit:high_unit], piece, preferred_element_type=jnp.float32)
+            summed = term if summed is None else summed + term
+            low_unit = high_unit
+        return summed
 
     total = jnp.zeros((4, ROW_LIMIT, width), jnp.float32)
     for group in CHUNK_GROUPS:
         parts = jnp.concatenate([hidden_part(m) for m in group], axis=1)
         hidden = cut_sum([parts[b] for b in range(4)])
         active = jax.nn.gelu(hidden).astype(jnp.bfloat16)
-        out = jnp.stack(
-            [jnp.dot(active, downs[f], preferred_element_type=jnp.float32) for f in range(4)]
-        ).astype(jnp.bfloat16)
-        out = out.reshape(4, len(group), 2, ROW_LIMIT, width)
-        both = out[:, :, 0].astype(jnp.float32) + other_core(out[:, :, 1]).astype(jnp.float32)
+        out = jnp.stack([times_down(active, pieces) for pieces in downs])
+        out = out.reshape(4, len(group), ROW_LIMIT, width)
         for at, m in enumerate(group):
             if m == 0:
-                total = total + both[:, at]
+                total = total + out[:, at]
             else:
-                total = total + swapped_chips(both[:, at].astype(jnp.bfloat16), m).astype(jnp.float32)
+                total = total + swapped_chips(out[:, at].astype(jnp.bfloat16), m).astype(jnp.float32)
 
     rounded = total.astype(jnp.bfloat16)
-    ring = jnp.concatenate([rounded, rounded[:3]])
-    slices = lax.dynamic_slice_in_dim(ring, cut, 4, axis=0)
     same_sum = jnp.zeros((ROW_LIMIT, width), jnp.float32)
     other_sum = same_sum
     for step in range(4):
-        part = back_home(slices[step], step).astype(jnp.float32)
+        part = back_home(rounded[step], step).astype(jnp.float32)
         source = (cut - step) % 4
         is_same = (source == 0) | ((source == 1) & low) | ((source == 3) & ~low)
         same_sum = same_sum + jnp.where(is_same, part, 0.0)

time: 236 us -> 252 us (1.068)
  the two profiles are of different devices: /device:TPU:32 before, /device:TPU:6 now
where the time goes in v3:
time: 252 us; the launch traced here: 250 us
  starting transfers between devices  129 us (51%)
  waiting for transfers between devices  96.7 us (38%)
  matrix products  18.2 us (7%)
  other arithmetic  4.55 us (2%)
    ppermute x29, starting transfers between devices, moved(): return lax.ppermute(value, axis, list(enumerate(targets)))  126 us
    ppermute x29, waiting for transfers between devices, moved(): return lax.ppermute(value, axis, list(enumerate(targets)))  96.7 us
    dot_general x4, matrix products, hidden_part(): jnp.dot(flat, up, preferred_element_type=jnp.float32).astype(jnp.bfloat16)  9.86 us
    dot_general x20, matrix products, times_down(): jnp.dot(active[:, low_unit:high_unit], piece, preferred_element_type=jnp....  6.79 us
  transfers between devices with their start and end apart: 30, of which 10 were waited for; matrix products, arithmetic and copies ran while one was open for 7% of the time, Pallas kernels for 0%

profile of v3, /device:TPU:6, one launch (start us, length us, event | category | flops | bytes accessed | tf_op | source)
XLA Modules:
  0.0 250.5 jit_solution(11901065087421490520)
XLA Ops:
  0.0 3.6 %collective-permute-start = (bf16[1,128,768]{2,1,0:T(8,128)(2,1)}, bf16[1,128,768]{2,1,0:T(8,128)(2,1)S(1)}, u32[]{:S(2)}, u32[]{:S(2)}) collective-permute-start(bf16[1,128,768]{2,1,0:T(8,128)(2,1)} %param.8), channel_id=1, source_target_pairs={{0,128},{128,256},{256,384},{384,0},{1,129},{129,257},{257,385},{3... | collective-permute-start | bytes 589832 | tf_op jit(solution)/shard_map/ppermute | solution.py:58
  11.0 9.1 %collective-permute-start.1 = (bf16[56,768]{1,0:T(8,128)(2,1)S(1)}, bf16[56,768]{1,0:T(8,128)(2,1)S(1)}, u32[]{:S(2)}, u32[]{:S(2)}) collective-permute-start(bf16[56,768]{1,0:T(8,128)(2,1)S(1)} %get-tuple-element.21), channel_id=1, source_target_pairs={{0,32},{4,36},{8,40},{12,44},{16,48},{20,52},{24,56},{28,60},{32,6... | collective-permute-start | bytes 258056 | tf_op jit(solution)/shard_map/ppermute | solution.py:12
  20.1 5.6 %collective-permute-start.3 = (bf16[56,768]{1,0:T(8,128)(2,1)S(1)}, bf16[56,768]{1,0:T(8,128)(2,1)S(1)}, u32[]{:S(2)}, u32[]{:S(2)}) collective-permute-start(bf16[56,768]{1,0:T(8,128)(2,1)S(1)} %get-tuple-element.19), channel_id=1, source_target_pairs={{0,96},{4,100},{8,104},{12,108},{16,112},{20,116},{24,120},{28,124... | collective-permute-start | bytes 258056 | tf_op jit(solution)/shard_map/ppermute | solution.py:12
  25.7 9.9 %collective-permute-start.2 = (bf16[56,768]{1,0:T(8,128)(2,1)S(1)}, bf16[56,768]{1,0:T(8,128)(2,1)S(1)}, u32[]{:S(2)}, u32[]{:S(2)}) collective-permute-start(bf16[56,768]{1,0:T(8,128)(2,1)S(1)} %get-tuple-element.20), channel_id=1, source_target_pairs={{0,80},{4,84},{8,88},{12,92},{16,64},{20,68},{24,72},{28,76},{32,1... | collective-permute-start | bytes 258056 | tf_op jit(solution)/shard_map/ppermute | solution.py:12
  35.6 7.3 %collective-permute-done.2 = bf16[56,768]{1,0:T(8,128)(2,1)S(1)} collective-permute-done((bf16[56,768]{1,0:T(8,128)(2,1)S(1)}, bf16[56,768]{1,0:T(8,128)(2,1)S(1)}, u32[]{:S(2)}, u32[]{:S(2)}) %collective-permute-start.2) | collective-permute-done | bytes 86048 | tf_op jit(solution)/shard_map/ppermute | solution.py:12
  43.0 8.1 %collective-permute-start.19 = (bf16[4,56,768]{2,1,0:T(8,128)(2,1)S(1)}, bf16[4,56,768]{2,1,0:T(8,128)(2,1)S(1)}, u32[]{:S(2)}, u32[]{:S(2)}) collective-permute-start(bf16[4,56,768]{2,1,0:T(8,128)(2,1)S(1)} %constant_dynamic-slice_fusion), channel_id=1, source_target_pairs={{0,16},{4,20},{8,24},{12,28},{16,0},{20,4},{24,8},{28,12},{32,48},... | collective-permute-start | bytes 1032200 | tf_op jit(solution)/shard_map/ppermute | solution.py:12
  55.0 15.5 %collective-permute-done.19 = bf16[4,56,768]{2,1,0:T(8,128)(2,1)S(1)} collective-permute-done((bf16[4,56,768]{2,1,0:T(8,128)(2,1)S(1)}, bf16[4,56,768]{2,1,0:T(8,128)(2,1)S(1)}, u32[]{:S(2)}, u32[]{:S(2)}) %collective-permute-start.19) | collective-permute-done | bytes 344096 | tf_op jit(solution)/shard_map/ppermute | solution.py:12
  70.5 4.3 %collective-permute-start.13 = (bf16[1024,768]{1,0:T(8,128)(2,1)S(1)}, bf16[1024,768]{1,0:T(8,128)(2,1)S(1)}, u32[]{:S(2)}, u32[]{:S(2)}) collective-permute-start(bf16[1024,768]{1,0:T(8,128)(2,1)S(1)} %bitcast.142), channel_id=1, source_target_pairs={{0,1},{1,2},{2,3},{3,0},{4,5},{5,6},{6,7},{7,4},{8,9},{9,10},{10,1... | collective-permute-start | bytes 4718600 | tf_op jit(solution)/shard_map/ppermute | solution.py:12
  74.8 4.3 %collective-permute-start.5 = (bf16[4,56,768]{2,1,0:T(8,128)(2,1)S(1)}, bf16[4,56,768]{2,1,0:T(8,128)(2,1)S(1)}, u32[]{:S(2)}, u32[]{:S(2)}) collective-permute-start(bf16[4,56,768]{2,1,0:T(8,128)(2,1)S(1)} %constant_dynamic-slice_fusion), channel_id=1, source_target_pairs={{0,8},{4,12},{8,0},{12,4},{16,24},{20,28},{24,16},{28,20},{32,40},... | collective-permute-start | bytes 1032200 | tf_op jit(solution)/shard_map/ppermute | solution.py:12
  86.5 3.6 %collective-permute-start.23 = (bf16[112,2048]{1,0:T(8,128)(2,1)S(1)}, bf16[112,2048]{1,0:T(8,128)(2,1)S(1)}, u32[]{:S(2)}, u32[]{:S(2)}) collective-permute-start(bf16[112,2048]{1,0:T(8,128)(2,1)S(1)} %get-tuple-element.6), channel_id=1, source_target_pairs={{0,2},{1,3},{2,0},{3,1},{4,6},{5,7},{6,4},{7,5},{8,10},{9,11},{10,... | collective-permute-start | bytes 1376264 | tf_op jit(solution)/shard_map/ppermute | solution.py:12
  97.1 12.5 %collective-permute-done.13 = bf16[1024,768]{1,0:T(8,128)(2,1)S(1)} collective-permute-done((bf16[1024,768]{1,0:T(8,128)(2,1)S(1)}, bf16[1024,768]{1,0:T(8,128)(2,1)S(1)}, u32[]{:S(2)}, u32[]{:S(2)}) %collective-permute-start.13) | collective-permute-done | bytes 1572896 | tf_op jit(solution)/shard_map/ppermute | solution.py:12
  109.6 5.5 %collective-permute-start.6 = (bf16[112,2048]{1,0:T(8,128)(2,1)S(1)}, bf16[112,2048]{1,0:T(8,128)(2,1)S(1)}, u32[]{:S(2)}, u32[]{:S(2)}) collective-permute-start(bf16[112,2048]{1,0:T(8,128)(2,1)S(1)} %get-tuple-element.8), channel_id=1, source_target_pairs={{0,1},{1,2},{2,3},{3,0},{4,5},{5,6},{6,7},{7,4},{8,9},{9,10},{10,1... | collective-permute-start | bytes 1376264 | tf_op jit(solution)/shard_map/ppermute | solution.py:12
  115.2 13.9 %collective-permute-done.21 = bf16[112,2048]{1,0:T(8,128)(2,1)S(1)} collective-permute-done((bf16[112,2048]{1,0:T(8,128)(2,1)S(1)}, bf16[112,2048]{1,0:T(8,128)(2,1)S(1)}, u32[]{:S(2)}, u32[]{:S(2)}) %collective-permute-start.21) | collective-permute-done | bytes 458784 | tf_op jit(solution)/shard_map/ppermute | solution.py:12
  131.0 6.6 %collective-permute-start.7 = (bf16[112,2048]{1,0:T(8,128)(2,1)S(1)}, bf16[112,2048]{1,0:T(8,128)(2,1)S(1)}, u32[]{:S(2)}, u32[]{:S(2)}) collective-permute-start(bf16[112,2048]{1,0:T(8,128)(2,1)S(1)} %get-tuple-element.10), channel_id=1, source_target_pairs={{0,3},{1,0},{2,1},{3,2},{4,7},{5,4},{6,5},{7,6},{8,11},{9,8},{10,9... | collective-permute-start | bytes 1376264 | tf_op jit(solution)/shard_map/ppermute | solution.py:12
  140.4 8.0 %collective-permute-done.6 = bf16[112,2048]{1,0:T(8,128)(2,1)S(1)} collective-permute-done((bf16[112,2048]{1,0:T(8,128)(2,1)S(1)}, bf16[112,2048]{1,0:T(8,128)(2,1)S(1)}, u32[]{:S(2)}, u32[]{:S(2)}) %collective-permute-start.6) | collective-permute-done | bytes 458784 | tf_op jit(solution)/shard_map/ppermute | solution.py:12
  148.4 5.7 %collective-permute-start.14 = (bf16[512,768]{1,0:T(8,128)(2,1)S(1)}, bf16[512,768]{1,0:T(8,128)(2,1)S(1)}, u32[]{:S(2)}, u32[]{:S(2)}) collective-permute-start(bf16[512,768]{1,0:T(8,128)(2,1)S(1)} %slice.152), channel_id=1, source_target_pairs={{0,1},{1,2},{2,3},{3,0},{4,5},{5,6},{6,7},{7,4},{8,9},{9,10},{10,1... | collective-permute-start | bytes 2359304 | tf_op jit(solution)/shard_map/ppermute | solution.py:12
  177.4 6.3 %collective-permute-start.25 = (bf16[4,56,768]{2,1,0:T(8,128)(2,1)S(1)}, bf16[4,56,768]{2,1,0:T(8,128)(2,1)}, u32[]{:S(2)}, u32[]{:S(2)}) collective-permute-start(bf16[4,56,768]{2,1,0:T(8,128)(2,1)S(1)} %get-tuple-element.12), channel_id=1, source_target_pairs={{0,24},{4,28},{8,16},{12,20},{16,8},{20,12},{24,0},{28,4},{32,56},... | collective-permute-start | bytes 1032200 | tf_op jit(solution)/shard_map/ppermute | solution.py:12
  183.9 5.2 %collective-permute-done.18 = bf16[4,56,768]{2,1,0:T(8,128)(2,1)S(1)} collective-permute-done((bf16[4,56,768]{2,1,0:T(8,128)(2,1)S(1)}, bf16[4,56,768]{2,1,0:T(8,128)(2,1)S(1)}, u32[]{:S(2)}, u32[]{:S(2)}) %collective-permute-start.18) | collective-permute-done | bytes 344096 | tf_op jit(solution)/shard_map/ppermute | solution.py:12
  189.1 14.8 %collective-permute-done.24 = bf16[4,56,768]{2,1,0:T(8,128)(2,1)S(1)} collective-permute-done((bf16[4,56,768]{2,1,0:T(8,128)(2,1)S(1)}, bf16[4,56,768]{2,1,0:T(8,128)(2,1)S(1)}, u32[]{:S(2)}, u32[]{:S(2)}) %collective-permute-start.24) | collective-permute-done | bytes 344096 | tf_op jit(solution)/shard_map/ppermute | solution.py:12
  205.1 7.9 %collective-permute-start.29 = (bf16[56,768]{1,0:T(8,128)(2,1)S(1)}, bf16[56,768]{1,0:T(8,128)(2,1)S(1)}, u32[]{:S(2)}, u32[]{:S(2)}) collective-permute-start(bf16[56,768]{1,0:T(8,128)(2,1)S(1)} %get-tuple-element.15), channel_id=1, source_target_pairs={{0,3},{1,96},{2,81},{3,34},{4,7},{5,100},{6,85},{7,38},{8,11},{9,1... | collective-permute-start | bytes 258056 | tf_op jit(solution)/shard_map/ppermute | solution.py:12
  213.0 5.7 %collective-permute-start.28 = (bf16[56,768]{1,0:T(8,128)(2,1)S(1)}, bf16[56,768]{1,0:T(8,128)(2,1)S(1)}, u32[]{:S(2)}, u32[]{:S(2)}) collective-permute-start(bf16[56,768]{1,0:T(8,128)(2,1)S(1)} %get-tuple-element.16), channel_id=1, source_target_pairs={{0,2},{1,99},{2,80},{3,33},{4,6},{5,103},{6,84},{7,37},{8,10},{9,1... | collective-permute-start | bytes 258056 | tf_op jit(solution)/shard_map/ppermute | solution.py:12
  218.8 7.1 %collective-permute-start.27 = (bf16[56,768]{1,0:T(8,128)(2,1)S(1)}, bf16[56,768]{1,0:T(8,128)(2,1)S(1)}, u32[]{:S(2)}, u32[]{:S(2)}) collective-permute-start(bf16[56,768]{1,0:T(8,128)(2,1)S(1)} %get-tuple-element.17), channel_id=1, source_target_pairs={{0,1},{1,98},{2,83},{3,32},{4,5},{5,102},{6,87},{7,36},{8,9},{9,10... | collective-permute-start | bytes 258056 | tf_op jit(solution)/shard_map/ppermute | solution.py:12
  225.9 6.7 %collective-permute-start.26 = (bf16[56,768]{1,0:T(8,128)(2,1)S(1)}, bf16[56,768]{1,0:T(8,128)(2,1)S(1)}, u32[]{:S(2)}, u32[]{:S(2)}) collective-permute-start(bf16[56,768]{1,0:T(8,128)(2,1)S(1)} %get-tuple-element.18), channel_id=1, source_target_pairs={{0,0},{1,97},{2,82},{3,35},{4,4},{5,101},{6,86},{7,39},{8,8},{9,10... | collective-permute-start | bytes 258056 | tf_op jit(solution)/shard_map/ppermute | solution.py:12
  235.8 13.4 %collective-permute-done.26 = bf16[56,768]{1,0:T(8,128)(2,1)S(1)} collective-permute-done((bf16[56,768]{1,0:T(8,128)(2,1)S(1)}, bf16[56,768]{1,0:T(8,128)(2,1)S(1)}, u32[]{:S(2)}, u32[]{:S(2)}) %collective-permute-start.26) | collective-permute-done | bytes 86048 | tf_op jit(solution)/shard_map/ppermute | solution.py:12
  (103 shorter events, 58.4 us)
Async XLA Ops:
  3.6 71.2 %collective-permute-start.4 = (bf16[768,1024]{1,0:T(8,128)(2,1)}, bf16[768,1024]{1,0:T(8,128)(2,1)}, u32[]{:S(2)}, u32[]{:S(2)}) collective-permute-start(bf16[768,1024]{1,0:T(8,128)(2,1)} %bitcast.161), channel_id=1, source_target_pairs={{0,4},{4,0},{8,12},{12,8},{16,20},{20,16},{24,28},{28,24},{32,36},... | collective-permute-start | bytes 4718600 | tf_op jit(solution)/shard_map/ppermute | solution.py:12
  5.5 80.9 %collective-permute-start.10 = (bf16[1024,768]{1,0:T(8,128)(2,1)}, bf16[1024,768]{1,0:T(8,128)(2,1)S(1)}, u32[]{:S(2)}, u32[]{:S(2)}) collective-permute-start(bf16[1024,768]{1,0:T(8,128)(2,1)} %bitcast.140), channel_id=1, source_target_pairs={{0,3},{1,0},{2,1},{3,2},{4,7},{5,4},{6,5},{7,6},{8,11},{9,8},{10,9... | collective-permute-start | bytes 4718600 | tf_op jit(solution)/shard_map/ppermute | solution.py:12
  11.0 24.6 %collective-permute-start.1 = (bf16[56,768]{1,0:T(8,128)(2,1)S(1)}, bf16[56,768]{1,0:T(8,128)(2,1)S(1)}, u32[]{:S(2)}, u32[]{:S(2)}) collective-permute-start(bf16[56,768]{1,0:T(8,128)(2,1)S(1)} %get-tuple-element.21), channel_id=1, source_target_pairs={{0,32},{4,36},{8,40},{12,44},{16,48},{20,52},{24,56},{28,60},{32,6... | collective-permute-start | bytes 258056 | tf_op jit(solution)/shard_map/ppermute | solution.py:12
  20.1 22.8 %collective-permute-start.3 = (bf16[56,768]{1,0:T(8,128)(2,1)S(1)}, bf16[56,768]{1,0:T(8,128)(2,1)S(1)}, u32[]{:S(2)}, u32[]{:S(2)}) collective-permute-start(bf16[56,768]{1,0:T(8,128)(2,1)S(1)} %get-tuple-element.19), channel_id=1, source_target_pairs={{0,96},{4,100},{8,104},{12,108},{16,112},{20,116},{24,120},{28,124... | collective-permute-start | bytes 258056 | tf_op jit(solution)/shard_map/ppermute | solution.py:12
  25.7 17.2 %collective-permute-start.2 = (bf16[56,768]{1,0:T(8,128)(2,1)S(1)}, bf16[56,768]{1,0:T(8,128)(2,1)S(1)}, u32[]{:S(2)}, u32[]{:S(2)}) collective-permute-start(bf16[56,768]{1,0:T(8,128)(2,1)S(1)} %get-tuple-element.20), channel_id=1, source_target_pairs={{0,80},{4,84},{8,88},{12,92},{16,64},{20,68},{24,72},{28,76},{32,1... | collective-permute-start | bytes 258056 | tf_op jit(solution)/shard_map/ppermute | solution.py:12
  43.0 27.5 %collective-permute-start.19 = (bf16[4,56,768]{2,1,0:T(8,128)(2,1)S(1)}, bf16[4,56,768]{2,1,0:T(8,128)(2,1)S(1)}, u32[]{:S(2)}, u32[]{:S(2)}) collective-permute-start(bf16[4,56,768]{2,1,0:T(8,128)(2,1)S(1)} %constant_dynamic-slice_fusion), channel_id=1, source_target_pairs={{0,16},{4,20},{8,24},{12,28},{16,0},{20,4},{24,8},{28,12},{32,48},... | collective-permute-start | bytes 1032200 | tf_op jit(solution)/shard_map/ppermute | solution.py:12
  51.1 30.9 %collective-permute-start.20 = (bf16[4,56,768]{2,1,0:T(8,128)(2,1)S(1)}, bf16[4,56,768]{2,1,0:T(8,128)(2,1)S(1)}, u32[]{:S(2)}, u32[]{:S(2)}) collective-permute-start(bf16[4,56,768]{2,1,0:T(8,128)(2,1)S(1)} %constant_dynamic-slice_fusion), channel_id=1, source_target_pairs={{0,24},{4,28},{8,16},{12,20},{16,8},{20,12},{24,0},{28,4},{32,56},... | collective-permute-start | bytes 1032200 | tf_op jit(solution)/shard_map/ppermute | solution.py:12
  53.1 106.8 %collective-permute-start.9 = (bf16[1024,768]{1,0:T(8,128)(2,1)S(1)}, bf16[1024,768]{1,0:T(8,128)(2,1)S(1)}, u32[]{:S(2)}, u32[]{:S(2)}) collective-permute-start(bf16[1024,768]{1,0:T(8,128)(2,1)S(1)} %bitcast.141), channel_id=1, source_target_pairs={{0,4},{4,0},{8,12},{12,8},{16,20},{20,16},{24,28},{28,24},{32,36},... | collective-permute-start | bytes 4718600 | tf_op jit(solution)/shard_map/ppermute | solution.py:12
  70.5 39.2 %collective-permute-start.13 = (bf16[1024,768]{1,0:T(8,128)(2,1)S(1)}, bf16[1024,768]{1,0:T(8,128)(2,1)S(1)}, u32[]{:S(2)}, u32[]{:S(2)}) collective-permute-start(bf16[1024,768]{1,0:T(8,128)(2,1)S(1)} %bitcast.142), channel_id=1, source_target_pairs={{0,1},{1,2},{2,3},{3,0},{4,5},{5,6},{6,7},{7,4},{8,9},{9,10},{10,1... | collective-permute-start | bytes 4718600 | tf_op jit(solution)/shard_map/ppermute | solution.py:12
  84.5 44.6 %collective-permute-start.21 = (bf16[112,2048]{1,0:T(8,128)(2,1)S(1)}, bf16[112,2048]{1,0:T(8,128)(2,1)S(1)}, u32[]{:S(2)}, u32[]{:S(2)}) collective-permute-start(bf16[112,2048]{1,0:T(8,128)(2,1)S(1)} %get-tuple-element.5), channel_id=1, source_target_pairs={{0,1},{1,2},{2,3},{3,0},{4,5},{5,6},{6,7},{7,4},{8,9},{9,10},{10,1... | collective-permute-start | bytes 1376264 | tf_op jit(solution)/shard_map/ppermute | solution.py:12
  86.5 44.5 %collective-permute-start.23 = (bf16[112,2048]{1,0:T(8,128)(2,1)S(1)}, bf16[112,2048]{1,0:T(8,128)(2,1)S(1)}, u32[]{:S(2)}, u32[]{:S(2)}) collective-permute-start(bf16[112,2048]{1,0:T(8,128)(2,1)S(1)} %get-tuple-element.6), channel_id=1, source_target_pairs={{0,2},{1,3},{2,0},{3,1},{4,6},{5,7},{6,4},{7,5},{8,10},{9,11},{10,... | collective-permute-start | bytes 1376264 | tf_op jit(solution)/shard_map/ppermute | solution.py:12
  90.1 47.5 %collective-permute-start.22 = (bf16[112,2048]{1,0:T(8,128)(2,1)S(1)}, bf16[112,2048]{1,0:T(8,128)(2,1)S(1)}, u32[]{:S(2)}, u32[]{:S(2)}) collective-permute-start(bf16[112,2048]{1,0:T(8,128)(2,1)S(1)} %get-tuple-element.7), channel_id=1, source_target_pairs={{0,3},{1,0},{2,1},{3,2},{4,7},{5,4},{6,5},{7,6},{8,11},{9,8},{10,9... | collective-permute-start | bytes 1376264 | tf_op jit(solution)/shard_map/ppermute | solution.py:12
  109.6 38.8 %collective-permute-start.6 = (bf16[112,2048]{1,0:T(8,128)(2,1)S(1)}, bf16[112,2048]{1,0:T(8,128)(2,1)S(1)}, u32[]{:S(2)}, u32[]{:S(2)}) collective-permute-start(bf16[112,2048]{1,0:T(8,128)(2,1)S(1)} %get-tuple-element.8), channel_id=1, source_target_pairs={{0,1},{1,2},{2,3},{3,0},{4,5},{5,6},{6,7},{7,4},{8,9},{9,10},{10,1... | collective-permute-start | bytes 1376264 | tf_op jit(solution)/shard_map/ppermute | solution.py:12
  129.1 25.1 %collective-permute-start.8 = (bf16[112,2048]{1,0:T(8,128)(2,1)S(1)}, bf16[112,2048]{1,0:T(8,128)(2,1)S(1)}, u32[]{:S(2)}, u32[]{:S(2)}) collective-permute-start(bf16[112,2048]{1,0:T(8,128)(2,1)S(1)} %get-tuple-element.9), channel_id=1, source_target_pairs={{0,2},{1,3},{2,0},{3,1},{4,6},{5,7},{6,4},{7,5},{8,10},{9,11},{10,... | collective-permute-start | bytes 1376264 | tf_op jit(solution)/shard_map/ppermute | solution.py:12
  131.0 25.1 %collective-permute-start.7 = (bf16[112,2048]{1,0:T(8,128)(2,1)S(1)}, bf16[112,2048]{1,0:T(8,128)(2,1)S(1)}, u32[]{:S(2)}, u32[]{:S(2)}) collective-permute-start(bf16[112,2048]{1,0:T(8,128)(2,1)S(1)} %get-tuple-element.10), channel_id=1, source_target_pairs={{0,3},{1,0},{2,1},{3,2},{4,7},{5,4},{6,5},{7,6},{8,11},{9,8},{10,9... | collective-permute-start | bytes 1376264 | tf_op jit(solution)/shard_map/ppermute | solution.py:12
  137.6 29.4 %collective-permute-start.12 = (bf16[512,768]{1,0:T(8,128)(2,1)S(1)}, bf16[512,768]{1,0:T(8,128)(2,1)S(1)}, u32[]{:S(2)}, u32[]{:S(2)}) collective-permute-start(bf16[512,768]{1,0:T(8,128)(2,1)S(1)} %slice.150), channel_id=1, source_target_pairs={{0,3},{1,0},{2,1},{3,2},{4,7},{5,4},{6,5},{7,6},{8,11},{9,8},{10,9... | collective-permute-start | bytes 2359304 | tf_op jit(solution)/shard_map/ppermute | solution.py:12
  148.4 16.4 %collective-permute-start.14 = (bf16[512,768]{1,0:T(8,128)(2,1)S(1)}, bf16[512,768]{1,0:T(8,128)(2,1)S(1)}, u32[]{:S(2)}, u32[]{:S(2)}) collective-permute-start(bf16[512,768]{1,0:T(8,128)(2,1)S(1)} %slice.152), channel_id=1, source_target_pairs={{0,1},{1,2},{2,3},{3,0},{4,5},{5,6},{6,7},{7,4},{8,9},{9,10},{10,1... | collective-permute-start | bytes 2359304 | tf_op jit(solution)/shard_map/ppermute | solution.py:12
  154.2 16.6 %collective-permute-start.11 = (bf16[1024,768]{1,0:T(8,128)(2,1)S(1)}, bf16[1024,768]{1,0:T(8,128)(2,1)S(1)}, u32[]{:S(2)}, u32[]{:S(2)}) collective-permute-start(bf16[1024,768]{1,0:T(8,128)(2,1)S(1)} %collective-permute-done.10), channel_id=1, source_target_pairs={{0,4},{4,0},{8,12},{12,8},{16,20},{20,16},{24,28},{28,24},{32,36},... | collective-permute-start | bytes 4718600 | tf_op jit(solution)/shard_map/ppermute | solution.py:12
  175.5 28.5 %collective-permute-start.24 = (bf16[4,56,768]{2,1,0:T(8,128)(2,1)S(1)}, bf16[4,56,768]{2,1,0:T(8,128)(2,1)S(1)}, u32[]{:S(2)}, u32[]{:S(2)}) collective-permute-start(bf16[4,56,768]{2,1,0:T(8,128)(2,1)S(1)} %get-tuple-element.11), channel_id=1, source_target_pairs={{0,16},{4,20},{8,24},{12,28},{16,0},{20,4},{24,8},{28,12},{32,48},... | collective-permute-start | bytes 1032200 | tf_op jit(solution)/shard_map/ppermute | solution.py:12
  177.4 26.6 %collective-permute-start.25 = (bf16[4,56,768]{2,1,0:T(8,128)(2,1)S(1)}, bf16[4,56,768]{2,1,0:T(8,128)(2,1)}, u32[]{:S(2)}, u32[]{:S(2)}) collective-permute-start(bf16[4,56,768]{2,1,0:T(8,128)(2,1)S(1)} %get-tuple-element.12), channel_id=1, source_target_pairs={{0,24},{4,28},{8,16},{12,20},{16,8},{20,12},{24,0},{28,4},{32,56},... | collective-permute-start | bytes 1032200 | tf_op jit(solution)/shard_map/ppermute | solution.py:12
  205.1 27.7 %collective-permute-start.29 = (bf16[56,768]{1,0:T(8,128)(2,1)S(1)}, bf16[56,768]{1,0:T(8,128)(2,1)S(1)}, u32[]{:S(2)}, u32[]{:S(2)}) collective-permute-start(bf16[56,768]{1,0:T(8,128)(2,1)S(1)} %get-tuple-element.15), channel_id=1, source_target_pairs={{0,3},{1,96},{2,81},{3,34},{4,7},{5,100},{6,85},{7,38},{8,11},{9,1... | collective-permute-start | bytes 258056 | tf_op jit(solution)/shard_map/ppermute | solution.py:12
  213.0 19.8 %collective-permute-start.28 = (bf16[56,768]{1,0:T(8,128)(2,1)S(1)}, bf16[56,768]{1,0:T(8,128)(2,1)S(1)}, u32[]{:S(2)}, u32[]{:S(2)}) collective-permute-start(bf16[56,768]{1,0:T(8,128)(2,1)S(1)} %get-tuple-element.16), channel_id=1, source_target_pairs={{0,2},{1,99},{2,80},{3,33},{4,6},{5,103},{6,84},{7,37},{8,10},{9,1... | collective-permute-start | bytes 258056 | tf_op jit(solution)/shard_map/ppermute | solution.py:12
  218.8 17.0 %collective-permute-start.27 = (bf16[56,768]{1,0:T(8,128)(2,1)S(1)}, bf16[56,768]{1,0:T(8,128)(2,1)S(1)}, u32[]{:S(2)}, u32[]{:S(2)}) collective-permute-start(bf16[56,768]{1,0:T(8,128)(2,1)S(1)} %get-tuple-element.17), channel_id=1, source_target_pairs={{0,1},{1,98},{2,83},{3,32},{4,5},{5,102},{6,87},{7,36},{8,9},{9,10... | collective-permute-start | bytes 258056 | tf_op jit(solution)/shard_map/ppermute | solution.py:12
  225.9 23.2 %collective-permute-start.26 = (bf16[56,768]{1,0:T(8,128)(2,1)S(1)}, bf16[56,768]{1,0:T(8,128)(2,1)S(1)}, u32[]{:S(2)}, u32[]{:S(2)}) collective-permute-start(bf16[56,768]{1,0:T(8,128)(2,1)S(1)} %get-tuple-element.18), channel_id=1, source_target_pairs={{0,0},{1,97},{2,82},{3,35},{4,4},{5,101},{6,86},{7,39},{8,8},{9,10... | collective-permute-start | bytes 258056 | tf_op jit(solution)/shard_map/ppermute | solution.py:12
  (9 other events, 133.4 us)

commit v4 on v2

--- a/solution.py
+++ b/solution.py
@@ -23,6 +23,11 @@
 
 def other_core(value):
     return moved(value, "expert", [j ^ 1 for j in range(lax.axis_size("expert"))])
+
+
+def after(value, *others):
+    corners = [other[(0,) * other.ndim] * 0 for other in others]
+    return value + sum(corners).astype(value.dtype)
 
 
 def along_cuts(value, by):
@@ -37,20 +42,50 @@
     return sum(part.astype(jnp.float32) for part in (blocks[0], from_left, from_right, from_far))
 
 
-def back_home(value, step):
-    targets = []
-    for j in range(lax.axis_size("expert")):
+def between_devices(value, target):
+    count = lax.axis_size("expert")
+    pairs = []
+    for j in range(count):
         for c in range(4):
-            home = [j, (j - 8) % 32, j ^ 20, (j + 8) % 32][c]
-            targets.append(home * 4 + (c + step) % 4)
-    return moved(value, ("expert", "cuts"), targets)
+            to = target(j, c)
+            if to is not None:
+                pairs.append((j * 4 + c, to[0] * 4 + to[1] % 4))
+    return lax.ppermute(value, ("expert", "cuts"), pairs)
+
+
+def near_pieces(own):
+    first = between_devices(own, lambda j, c: (j, c - 1) if j % 2 == 0 else (j, c + 1))
+    second = between_devices(own, lambda j, c: (j ^ 1, c + 1) if j % 2 == 0 else (j ^ 1, c - 1))
+    return first, second
+
+
+def last_pieces(own, near, core):
+    relayed = between_devices(near[1], lambda j, c: (j, c + 1) if j % 2 == 1 else None)
+    sent = jnp.where(core == 0, near[1], own)
+    last = between_devices(sent, lambda j, c: (j ^ 1, c - 1) if j % 2 == 0 else (j ^ 1, c))
+    return jnp.where(core == 0, own, relayed), last
+
+
+def slice_step(part, core):
+    return (1, 3)[core] if part == 0 else (0, 2)[core]
+
+
+def back_home(value, part, other):
+    def target(j, c):
+        k = (c + 2 * (j // 2 % 2)) % 4
+        home = [j, (j - 8) % 32, j ^ 20, (j + 8) % 32][k]
+        return home ^ other, c + slice_step(part, j % 2)
+
+    return between_devices(value, target)
 
 
 def shards(activations, pred_routes, true_routes, gate_scores, mis_rows, mis_count, w_up, w_down):
     arrived = lax.ppermute(activations, "segment", [(i, (i + 1) % 4) for i in range(4)])[0]
     tok_rows, width = arrived.shape
-    up = w_up[0, 0]
-    downs = lax.all_gather(w_down[0, 0], "cuts")
+    core = lax.axis_index("expert") % 2
+    up_other = other_core(w_up[0, 0])
+    up = lax.optimization_barrier(jnp.concatenate([w_up[0, 0], up_other], axis=1))
+    ff = w_down.shape[2]
     chip = lax.axis_index("expert") // 2
     cut = lax.axis_index("cuts")
     half = chip // 8
@@ -79,7 +114,10 @@
     picker = picked.astype(jnp.bfloat16).reshape(2 * ROW_LIMIT, tok_rows)
     weights = jnp.where(picked, factor[:, None, :], 0.0).reshape(2 * ROW_LIMIT, tok_rows)
 
+    near = near_pieces(w_down[0, 0])
+    last = last_pieces(w_down[0, 0], near, core)
     packed = jnp.dot(picker, arrived, preferred_element_type=jnp.float32).astype(jnp.bfloat16)
+    packed = after(packed, up_other)
     same, other = packed[:ROW_LIMIT], packed[ROW_LIMIT:]
     ahead = jnp.where(low, same, other)
     behind = jnp.where(low, other, same)
@@ -90,43 +128,55 @@
         swapped_chips(other, 10),
         along_chips(behind, -4),
     ]
-    ring = jnp.stack(sources + sources[:3])
-    chunk = lax.dynamic_slice_in_dim(ring, cut, 4, axis=0)
+    first = (cut + 2 * (chip % 2)) % 4
+    numbers = ((first + jnp.arange(4)) % 4)[:, None, None]
+    chunk = sum(jnp.where(numbers == k, rows[None], 0) for k, rows in enumerate(sources))
+    chunk = after(chunk, near[0], near[1])
 
     def hidden_part(m):
         rows = chunk if m == 0 else swapped_chips(chunk, m)
-        both = jnp.concatenate([rows, other_core(rows)], axis=1)
-        flat = both.reshape(8 * ROW_LIMIT, width)
+        flat = rows.reshape(4 * ROW_LIMIT, width)
         part = jnp.dot(flat, up, preferred_element_type=jnp.float32).astype(jnp.bfloat16)
-        return part.reshape(4, 2 * ROW_LIMIT, up.shape[1])
-
-    total = jnp.zeros((4, ROW_LIMIT, width), jnp.float32)
+        return part.reshape(4, ROW_LIMIT, 2 * ff)
+
+    def times_down(own_units, other_units):
+        core_units = jnp.where(core == 0, own_units, other_units), jnp.where(core == 0, other_units, own_units)
+        terms = [(own_units, near[0]), (other_units, near[1])], list(zip(core_units, last))
+        dots = [[jnp.dot(u, w, preferred_element_type=jnp.float32) for u, w in t] for t in terms]
+        return jnp.stack([a + b for a, b in dots])
+
+    hiddens = []
     for group in CHUNK_GROUPS:
         parts = jnp.concatenate([hidden_part(m) for m in group], axis=1)
-        hidden = cut_sum([parts[b] for b in range(4)])
+        hiddens.append(cut_sum([parts[b] for b in range(4)]))
+
+    total = jnp.zeros((2, 2, ROW_LIMIT, width), jnp.float32)
+    for group, hidden in zip(CHUNK_GROUPS, hiddens):
         active = jax.nn.gelu(hidden).astype(jnp.bfloat16)
-        out = jnp.stack(
-            [jnp.dot(active, downs[f], preferred_element_type=jnp.float32) for f in range(4)]
-        ).astype(jnp.bfloat16)
-        out = out.reshape(4, len(group), 2, ROW_LIMIT, width)
-        both = out[:, :, 0].astype(jnp.float32) + other_core(out[:, :, 1]).astype(jnp.float32)
+        swapped = other_core(active)
+        own_units = jnp.concatenate([active[:, :ff], swapped[:, ff:]])
+        other_units = jnp.concatenate([active[:, ff:], swapped[:, :ff]])
+        if 2 in group and 0 not in group:
+            own_units = after(own_units, hiddens[1])
+        out = times_down(own_units, other_units).reshape(2, 2, len(group), ROW_LIMIT, width)
         for at, m in enumerate(group):
             if m == 0:
-                total = total + both[:, at]
+                total = total + out[:, :, at]
             else:
-                total = total + swapped_chips(both[:, at].astype(jnp.bfloat16), m).astype(jnp.float32)
+                sent = out[:, :, at].astype(jnp.bfloat16)
+                total = total + swapped_chips(sent, m).astype(jnp.float32)
 
     rounded = total.astype(jnp.bfloat16)
-    ring = jnp.concatenate([rounded, rounded[:3]])
-    slices = lax.dynamic_slice_in_dim(ring, cut, 4, axis=0)
     same_sum = jnp.zeros((ROW_LIMIT, width), jnp.float32)
     other_sum = same_sum
-    for step in range(4):
-        part = back_home(slices[step], step).astype(jnp.float32)
-        source = (cut - step) % 4
-        is_same = (source == 0) | ((source == 1) & low) | ((source == 3) & ~low)
-        same_sum = same_sum + jnp.where(is_same, part, 0.0)
-        other_sum = other_sum + jnp.where(is_same, 0.0, part)
+    for part in range(2):
+        for other in range(2):
+            rows = back_home(rounded[part, other], part, other).astype(jnp.float32)
+            step = jnp.where(core ^ other == 0, slice_step(part, 0), slice_step(part, 1))
+            source = (first - step) % 4
+            is_same = (source == 0) | ((source == 1) & low) | ((source == 3) & ~low)
+            same_sum = same_sum + jnp.where(is_same, rows, 0.0)
+            other_sum = other_sum + jnp.where(is_same, 0.0, rows)
     spread = jnp.dot(
         weights.T,
         jnp.concatenate([same_sum, other_sum]),

time: 236 us -> 214 us (0.907)
  the two profiles are of different devices: /device:TPU:32 before, /device:TPU:6 now
where the time goes in v4:
time: 214 us; the launch traced here: 213 us
  starting transfers between devices  101 us (47%)
  waiting for transfers between devices  85.8 us (40%)
  matrix products  9.41 us (4%)
  other arithmetic  8.31 us (4%)
  local copies, waits for them, and re-layouts  4.56 us (2%)
  between operations  4.06 us (2%)
    ppermute x18, waiting for transfers between devices, moved(): return lax.ppermute(value, axis, list(enumerate(targets)))  72.8 us
    ppermute x18, starting transfers between devices, moved(): return lax.ppermute(value, axis, list(enumerate(targets)))  67.9 us
    ppermute x8, starting transfers between devices, between_devices(): return lax.ppermute(value, ('expert', 'cuts'), pairs)  31.1 us
    ppermute x8, waiting for transfers between devices, between_devices(): return lax.ppermute(value, ('expert', 'cuts'), pairs)  9.69 us
    dot_general x8, matrix products, times_down(): jnp.dot(u, w, preferred_element_type=jnp.float32)  4.35 us
  transfers between devices with their start and end apart: 27, of which 13 were waited for; matrix products, arithmetic and copies ran while one was open for 8% of the time, Pallas kernels for 0%

profile of v4, /device:TPU:6, one launch (start us, length us, event | category | flops | bytes accessed | tf_op | source)
XLA Modules:
  0.0 213.1 jit_solution(16069500197490506075)
XLA Ops:
  1.9 7.9 %collective-permute-start.6 = (bf16[1024,768]{1,0:T(8,128)(2,1)}, bf16[1024,768]{1,0:T(8,128)(2,1)S(1)}, u32[]{:S(2)}, u32[]{:S(2)}) collective-permute-start(bf16[1024,768]{1,0:T(8,128)(2,1)} %bitcast.146), channel_id=1, source_target_pairs={{0,5},{1,6},{2,7},{3,4},{4,3},{5,0},{6,1},{7,2},{8,13},{9,14},{10,... | collective-permute-start | bytes 4718600 | tf_op jit(solution)/shard_map/ppermute | solution.py:53
  18.7 3.3 %collective-permute-done = bf16[1,128,768]{2,1,0:T(8,128)(2,1)S(1)} collective-permute-done((bf16[1,128,768]{2,1,0:T(8,128)(2,1)}, bf16[1,128,768]{2,1,0:T(8,128)(2,1)S(1)}, u32[]{:S(2)}, u32[]{:S(2)}) %collective-permute-start) | collective-permute-done | bytes 196640 | tf_op jit(solution)/shard_map/ppermute | solution.py:83
  22.2 6.1 %collective-permute-start.2 = (bf16[56,768]{1,0:T(8,128)(2,1)S(1)}, bf16[56,768]{1,0:T(8,128)(2,1)S(1)}, u32[]{:S(2)}, u32[]{:S(2)}) collective-permute-start(bf16[56,768]{1,0:T(8,128)(2,1)S(1)} %get-tuple-element.30), channel_id=1, source_target_pairs={{0,32},{4,36},{8,40},{12,44},{16,48},{20,52},{24,56},{28,60},{32,6... | collective-permute-start | bytes 258056 | tf_op jit(solution)/shard_map/ppermute | solution.py:12
  28.3 10.0 %collective-permute-start.3 = (bf16[56,768]{1,0:T(8,128)(2,1)S(1)}, bf16[56,768]{1,0:T(8,128)(2,1)S(1)}, u32[]{:S(2)}, u32[]{:S(2)}) collective-permute-start(bf16[56,768]{1,0:T(8,128)(2,1)S(1)} %get-tuple-element.32), channel_id=1, source_target_pairs={{0,80},{4,84},{8,88},{12,92},{16,64},{20,68},{24,72},{28,76},{32,1... | collective-permute-start | bytes 258056 | tf_op jit(solution)/shard_map/ppermute | solution.py:12
  38.3 5.6 %collective-permute-start.4 = (bf16[56,768]{1,0:T(8,128)(2,1)S(1)}, bf16[56,768]{1,0:T(8,128)(2,1)S(1)}, u32[]{:S(2)}, u32[]{:S(2)}) collective-permute-start(bf16[56,768]{1,0:T(8,128)(2,1)S(1)} %get-tuple-element.31), channel_id=1, source_target_pairs={{0,96},{4,100},{8,104},{12,108},{16,112},{20,116},{24,120},{28,124... | collective-permute-start | bytes 258056 | tf_op jit(solution)/shard_map/ppermute | solution.py:12
  47.8 3.1 %collective-permute-done.3 = bf16[56,768]{1,0:T(8,128)(2,1)S(1)} collective-permute-done((bf16[56,768]{1,0:T(8,128)(2,1)S(1)}, bf16[56,768]{1,0:T(8,128)(2,1)S(1)}, u32[]{:S(2)}, u32[]{:S(2)}) %collective-permute-start.3) | collective-permute-done | bytes 86048 | tf_op jit(solution)/shard_map/ppermute | solution.py:12
  50.9 2.9 %collective-permute-done.4 = bf16[56,768]{1,0:T(8,128)(2,1)S(1)} collective-permute-done((bf16[56,768]{1,0:T(8,128)(2,1)S(1)}, bf16[56,768]{1,0:T(8,128)(2,1)S(1)}, u32[]{:S(2)}, u32[]{:S(2)}) %collective-permute-start.4) | collective-permute-done | bytes 86048 | tf_op jit(solution)/shard_map/ppermute | solution.py:12
  58.5 3.4 %collective-permute-start.8 = (bf16[4,56,768]{2,1,0:T(8,128)(2,1)S(1)}, bf16[4,56,768]{2,1,0:T(8,128)(2,1)S(1)}, u32[]{:S(2)}, u32[]{:S(2)}) collective-permute-start(bf16[4,56,768]{2,1,0:T(8,128)(2,1)S(1)} %add_add_fusion), channel_id=1, source_target_pairs={{0,24},{4,28},{8,16},{12,20},{16,8},{20,12},{24,0},{28,4},{32,56},... | collective-permute-start | bytes 1032200 | tf_op jit(solution)/shard_map/ppermute | solution.py:12
  62.0 3.9 %collective-permute-start.13 = (bf16[4,56,768]{2,1,0:T(8,128)(2,1)S(1)}, bf16[4,56,768]{2,1,0:T(8,128)(2,1)S(1)}, u32[]{:S(2)}, u32[]{:S(2)}) collective-permute-start(bf16[4,56,768]{2,1,0:T(8,128)(2,1)S(1)} %add_add_fusion), channel_id=1, source_target_pairs={{0,8},{4,12},{8,0},{12,4},{16,24},{20,28},{24,16},{28,20},{32,40},... | collective-permute-start | bytes 1032200 | tf_op jit(solution)/shard_map/ppermute | solution.py:12
  66.9 12.9 %collective-permute-done.7 = bf16[4,56,768]{2,1,0:T(8,128)(2,1)S(1)} collective-permute-done((bf16[4,56,768]{2,1,0:T(8,128)(2,1)S(1)}, bf16[4,56,768]{2,1,0:T(8,128)(2,1)S(1)}, u32[]{:S(2)}, u32[]{:S(2)}) %collective-permute-start.7) | collective-permute-done | bytes 344096 | tf_op jit(solution)/shard_map/ppermute | solution.py:12
  87.0 3.8 %collective-permute-start.9 = (bf16[112,2048]{1,0:T(8,128)(2,1)S(1)}, bf16[112,2048]{1,0:T(8,128)(2,1)S(1)}, u32[]{:S(2)}, u32[]{:S(2)}) collective-permute-start(bf16[112,2048]{1,0:T(8,128)(2,1)S(1)} %get-tuple-element.7), channel_id=1, source_target_pairs={{0,1},{1,2},{2,3},{3,0},{4,5},{5,6},{6,7},{7,4},{8,9},{9,10},{10,1... | collective-permute-start | bytes 1376264 | tf_op jit(solution)/shard_map/ppermute | solution.py:12
  91.8 15.2 %collective-permute-done.10 = bf16[112,2048]{1,0:T(8,128)(2,1)S(1)} collective-permute-done((bf16[112,2048]{1,0:T(8,128)(2,1)S(1)}, bf16[112,2048]{1,0:T(8,128)(2,1)S(1)}, u32[]{:S(2)}, u32[]{:S(2)}) %collective-permute-start.10) | collective-permute-done | bytes 458784 | tf_op jit(solution)/shard_map/ppermute | solution.py:12
  109.0 3.9 %collective-permute-start.15 = (bf16[112,2048]{1,0:T(8,128)(2,1)S(1)}, bf16[112,2048]{1,0:T(8,128)(2,1)S(1)}, u32[]{:S(2)}, u32[]{:S(2)}) collective-permute-start(bf16[112,2048]{1,0:T(8,128)(2,1)S(1)} %get-tuple-element.12), channel_id=1, source_target_pairs={{0,3},{1,0},{2,1},{3,2},{4,7},{5,4},{6,5},{7,6},{8,11},{9,8},{10,9... | collective-permute-start | bytes 1376264 | tf_op jit(solution)/shard_map/ppermute | solution.py:12
  115.4 7.0 %collective-permute-done.14 = bf16[112,2048]{1,0:T(8,128)(2,1)S(1)} collective-permute-done((bf16[112,2048]{1,0:T(8,128)(2,1)S(1)}, bf16[112,2048]{1,0:T(8,128)(2,1)S(1)}, u32[]{:S(2)}, u32[]{:S(2)}) %collective-permute-start.14) | collective-permute-done | bytes 458784 | tf_op jit(solution)/shard_map/ppermute | solution.py:12
  124.3 9.1 %collective-permute-done.15 = bf16[112,2048]{1,0:T(8,128)(2,1)S(1)} collective-permute-done((bf16[112,2048]{1,0:T(8,128)(2,1)S(1)}, bf16[112,2048]{1,0:T(8,128)(2,1)S(1)}, u32[]{:S(2)}, u32[]{:S(2)}) %collective-permute-start.15) | collective-permute-done | bytes 458784 | tf_op jit(solution)/shard_map/ppermute | solution.py:12
  142.4 8.0 %collective-permute-start.19 = (bf16[2,2,56,768]{3,2,1,0:T(8,128)(2,1)S(1)}, bf16[2,2,56,768]{3,2,1,0:T(8,128)(2,1)S(1)}, u32[]{:S(2)}, u32[]{:S(2)}) collective-permute-start(bf16[2,2,56,768]{3,2,1,0:T(8,128)(2,1)S(1)} %get-tuple-element.13), channel_id=1, source_target_pairs={{0,16},{4,20},{8,24},{12,28},{16,0},{20,4},{24,8},{28,12},{32,48},... | collective-permute-start | bytes 1032200 | tf_op jit(solution)/shard_map/ppermute | solution.py:12
  150.5 5.3 %collective-permute-start.20 = (bf16[2,2,56,768]{3,2,1,0:T(8,128)(2,1)S(1)}, bf16[2,2,56,768]{3,2,1,0:T(8,128)(2,1)S(1)}, u32[]{:S(2)}, u32[]{:S(2)}) collective-permute-start(bf16[2,2,56,768]{3,2,1,0:T(8,128)(2,1)S(1)} %get-tuple-element.14), channel_id=1, source_target_pairs={{0,24},{4,28},{8,16},{12,20},{16,8},{20,12},{24,0},{28,4},{32,56},... | collective-permute-start | bytes 1032200 | tf_op jit(solution)/shard_map/ppermute | solution.py:12
  159.2 14.9 %collective-permute-done.19 = bf16[2,2,56,768]{3,2,1,0:T(8,128)(2,1)S(1)} collective-permute-done((bf16[2,2,56,768]{3,2,1,0:T(8,128)(2,1)S(1)}, bf16[2,2,56,768]{3,2,1,0:T(8,128)(2,1)S(1)}, u32[]{:S(2)}, u32[]{:S(2)}) %collective-permute-start.19) | collective-permute-done | bytes 344096 | tf_op jit(solution)/shard_map/ppermute | solution.py:12
  174.1 6.1 %collective-permute-done.22 = bf16[2,2,56,768]{3,2,1,0:T(8,128)(2,1)} collective-permute-done((bf16[2,2,56,768]{3,2,1,0:T(8,128)(2,1)S(1)}, bf16[2,2,56,768]{3,2,1,0:T(8,128)(2,1)}, u32[]{:S(2)}, u32[]{:S(2)}) %collective-permute-start.22) | collective-permute-done | bytes 344096 | tf_op jit(solution)/shard_map/ppermute | solution.py:12
  181.3 4.0 %collective-permute-start.23 = (bf16[56,768]{1,0:T(8,128)(2,1)S(1)}, bf16[56,768]{1,0:T(8,128)(2,1)S(1)}, u32[]{:S(2)}, u32[]{:S(2)}) collective-permute-start(bf16[56,768]{1,0:T(8,128)(2,1)S(1)} %get-tuple-element.28), channel_id=1, source_target_pairs={{0,1},{1,98},{2,83},{3,32},{4,7},{5,100},{6,85},{7,38},{8,89},{9,4... | collective-permute-start | bytes 258056 | tf_op jit(solution)/shard_map/ppermute | solution.py:53
  185.4 4.2 %collective-permute-start.24 = (bf16[56,768]{1,0:T(8,128)(2,1)S(1)}, bf16[56,768]{1,0:T(8,128)(2,1)S(1)}, u32[]{:S(2)}, u32[]{:S(2)}) collective-permute-start(bf16[56,768]{1,0:T(8,128)(2,1)S(1)} %get-tuple-element.27), channel_id=1, source_target_pairs={{0,5},{1,102},{2,87},{3,36},{4,3},{5,96},{6,81},{7,34},{8,93},{9,4... | collective-permute-start | bytes 258056 | tf_op jit(solution)/shard_map/ppermute | solution.py:53
  189.6 3.4 %collective-permute-start.25 = (bf16[56,768]{1,0:T(8,128)(2,1)S(1)}, bf16[56,768]{1,0:T(8,128)(2,1)S(1)}, u32[]{:S(2)}, u32[]{:S(2)}) collective-permute-start(bf16[56,768]{1,0:T(8,128)(2,1)S(1)} %get-tuple-element.26), channel_id=1, source_target_pairs={{0,0},{1,97},{2,82},{3,35},{4,6},{5,103},{6,84},{7,37},{8,88},{9,4... | collective-permute-start | bytes 258056 | tf_op jit(solution)/shard_map/ppermute | solution.py:53
  193.0 8.9 %collective-permute-start.26 = (bf16[56,768]{1,0:T(8,128)(2,1)S(1)}, bf16[56,768]{1,0:T(8,128)(2,1)S(1)}, u32[]{:S(2)}, u32[]{:S(2)}) collective-permute-start(bf16[56,768]{1,0:T(8,128)(2,1)S(1)} %get-tuple-element.25), channel_id=1, source_target_pairs={{0,4},{1,101},{2,86},{3,39},{4,2},{5,99},{6,80},{7,33},{8,92},{9,4... | collective-permute-start | bytes 258056 | tf_op jit(solution)/shard_map/ppermute | solution.py:53
  202.5 9.3 %collective-permute-done.26 = bf16[56,768]{1,0:T(8,128)(2,1)S(1)} collective-permute-done((bf16[56,768]{1,0:T(8,128)(2,1)S(1)}, bf16[56,768]{1,0:T(8,128)(2,1)S(1)}, u32[]{:S(2)}, u32[]{:S(2)}) %collective-permute-start.26) | collective-permute-done | bytes 86048 | tf_op jit(solution)/shard_map/ppermute | solution.py:53
  (97 shorter events, 46.9 us)
Async XLA Ops:
  0.0 16.8 %collective-permute-start.1 = (bf16[768,1024]{1,0:T(8,128)(2,1)}, bf16[768,1024]{1,0:T(8,128)(2,1)}, u32[]{:S(2)}, u32[]{:S(2)}) collective-permute-start(bf16[768,1024]{1,0:T(8,128)(2,1)} %bitcast.148), channel_id=1, source_target_pairs={{0,4},{4,0},{8,12},{12,8},{16,20},{20,16},{24,28},{28,24},{32,36},... | collective-permute-start | bytes 4718600 | tf_op jit(solution)/shard_map/ppermute | solution.py:12
  1.9 42.0 %collective-permute-start.6 = (bf16[1024,768]{1,0:T(8,128)(2,1)}, bf16[1024,768]{1,0:T(8,128)(2,1)S(1)}, u32[]{:S(2)}, u32[]{:S(2)}) collective-permute-start(bf16[1024,768]{1,0:T(8,128)(2,1)} %bitcast.146), channel_id=1, source_target_pairs={{0,5},{1,6},{2,7},{3,4},{4,3},{5,0},{6,1},{7,2},{8,13},{9,14},{10,... | collective-permute-start | bytes 4718600 | tf_op jit(solution)/shard_map/ppermute | solution.py:53
  9.8 36.2 %collective-permute-start.5 = (bf16[1024,768]{1,0:T(8,128)(2,1)}, bf16[1024,768]{1,0:T(8,128)(2,1)S(1)}, u32[]{:S(2)}, u32[]{:S(2)}) collective-permute-start(bf16[1024,768]{1,0:T(8,128)(2,1)} %bitcast.147), channel_id=1, source_target_pairs={{0,3},{1,0},{2,1},{3,2},{4,5},{5,6},{6,7},{7,4},{8,11},{9,8},{10,9... | collective-permute-start | bytes 4718600 | tf_op jit(solution)/shard_map/ppermute | solution.py:53
  22.2 25.6 %collective-permute-start.2 = (bf16[56,768]{1,0:T(8,128)(2,1)S(1)}, bf16[56,768]{1,0:T(8,128)(2,1)S(1)}, u32[]{:S(2)}, u32[]{:S(2)}) collective-permute-start(bf16[56,768]{1,0:T(8,128)(2,1)S(1)} %get-tuple-element.30), channel_id=1, source_target_pairs={{0,32},{4,36},{8,40},{12,44},{16,48},{20,52},{24,56},{28,60},{32,6... | collective-permute-start | bytes 258056 | tf_op jit(solution)/shard_map/ppermute | solution.py:12
  28.3 22.7 %collective-permute-start.3 = (bf16[56,768]{1,0:T(8,128)(2,1)S(1)}, bf16[56,768]{1,0:T(8,128)(2,1)S(1)}, u32[]{:S(2)}, u32[]{:S(2)}) collective-permute-start(bf16[56,768]{1,0:T(8,128)(2,1)S(1)} %get-tuple-element.32), channel_id=1, source_target_pairs={{0,80},{4,84},{8,88},{12,92},{16,64},{20,68},{24,72},{28,76},{32,1... | collective-permute-start | bytes 258056 | tf_op jit(solution)/shard_map/ppermute | solution.py:12
  38.3 15.5 %collective-permute-start.4 = (bf16[56,768]{1,0:T(8,128)(2,1)S(1)}, bf16[56,768]{1,0:T(8,128)(2,1)S(1)}, u32[]{:S(2)}, u32[]{:S(2)}) collective-permute-start(bf16[56,768]{1,0:T(8,128)(2,1)S(1)} %get-tuple-element.31), channel_id=1, source_target_pairs={{0,96},{4,100},{8,104},{12,108},{16,112},{20,116},{24,120},{28,124... | collective-permute-start | bytes 258056 | tf_op jit(solution)/shard_map/ppermute | solution.py:12
  54.0 25.8 %collective-permute-start.7 = (bf16[4,56,768]{2,1,0:T(8,128)(2,1)S(1)}, bf16[4,56,768]{2,1,0:T(8,128)(2,1)S(1)}, u32[]{:S(2)}, u32[]{:S(2)}) collective-permute-start(bf16[4,56,768]{2,1,0:T(8,128)(2,1)S(1)} %add_add_fusion), channel_id=1, source_target_pairs={{0,16},{4,20},{8,24},{12,28},{16,0},{20,4},{24,8},{28,12},{32,48},... | collective-permute-start | bytes 1032200 | tf_op jit(solution)/shard_map/ppermute | solution.py:12
  57.7 82.6 %collective-permute-start.18 = (bf16[1024,768]{1,0:T(8,128)(2,1)S(1)}, bf16[1024,768]{1,0:T(8,128)(2,1)S(1)}, u32[]{:S(2)}, u32[]{:S(2)}) collective-permute-start(bf16[1024,768]{1,0:T(8,128)(2,1)S(1)} %broadcast_select_fusion), channel_id=1, source_target_pairs={{0,7},{1,4},{2,5},{3,6},{4,0},{5,1},{6,2},{7,3},{8,15},{9,12},{10,... | collective-permute-start | bytes 4718600 | tf_op jit(solution)/shard_map/ppermute | solution.py:53
  57.8 83.1 %collective-permute-start.17 = (bf16[1024,768]{1,0:T(8,128)(2,1)S(1)}, bf16[1024,768]{1,0:T(8,128)(2,1)S(1)}, u32[]{:S(2)}, u32[]{:S(2)}) collective-permute-start(bf16[1024,768]{1,0:T(8,128)(2,1)S(1)} %collective-permute-done.6), channel_id=1, source_target_pairs={{4,5},{5,6},{6,7},{7,4},{12,13},{13,14},{14,15},{15,12},{20,21},{2... | collective-permute-start | bytes 4718600 | tf_op jit(solution)/shard_map/ppermute | solution.py:53
  58.5 22.2 %collective-permute-start.8 = (bf16[4,56,768]{2,1,0:T(8,128)(2,1)S(1)}, bf16[4,56,768]{2,1,0:T(8,128)(2,1)S(1)}, u32[]{:S(2)}, u32[]{:S(2)}) collective-permute-start(bf16[4,56,768]{2,1,0:T(8,128)(2,1)S(1)} %add_add_fusion), channel_id=1, source_target_pairs={{0,24},{4,28},{8,16},{12,20},{16,8},{20,12},{24,0},{28,4},{32,56},... | collective-permute-start | bytes 1032200 | tf_op jit(solution)/shard_map/ppermute | solution.py:12
  62.0 25.0 %collective-permute-start.13 = (bf16[4,56,768]{2,1,0:T(8,128)(2,1)S(1)}, bf16[4,56,768]{2,1,0:T(8,128)(2,1)S(1)}, u32[]{:S(2)}, u32[]{:S(2)}) collective-permute-start(bf16[4,56,768]{2,1,0:T(8,128)(2,1)S(1)} %add_add_fusion), channel_id=1, source_target_pairs={{0,8},{4,12},{8,0},{12,4},{16,24},{20,28},{24,16},{28,20},{32,40},... | collective-permute-start | bytes 1032200 | tf_op jit(solution)/shard_map/ppermute | solution.py:12
  81.8 25.3 %collective-permute-start.10 = (bf16[112,2048]{1,0:T(8,128)(2,1)S(1)}, bf16[112,2048]{1,0:T(8,128)(2,1)S(1)}, u32[]{:S(2)}, u32[]{:S(2)}) collective-permute-start(bf16[112,2048]{1,0:T(8,128)(2,1)S(1)} %get-tuple-element.9), channel_id=1, source_target_pairs={{0,3},{1,0},{2,1},{3,2},{4,7},{5,4},{6,5},{7,6},{8,11},{9,8},{10,9... | collective-permute-start | bytes 1376264 | tf_op jit(solution)/shard_map/ppermute | solution.py:12
  83.7 25.3 %collective-permute-start.11 = (bf16[112,2048]{1,0:T(8,128)(2,1)S(1)}, bf16[112,2048]{1,0:T(8,128)(2,1)S(1)}, u32[]{:S(2)}, u32[]{:S(2)}) collective-permute-start(bf16[112,2048]{1,0:T(8,128)(2,1)S(1)} %get-tuple-element.8), channel_id=1, source_target_pairs={{0,2},{1,3},{2,0},{3,1},{4,6},{5,7},{6,4},{7,5},{8,10},{9,11},{10,... | collective-permute-start | bytes 1376264 | tf_op jit(solution)/shard_map/ppermute | solution.py:12
  87.0 25.9 %collective-permute-start.9 = (bf16[112,2048]{1,0:T(8,128)(2,1)S(1)}, bf16[112,2048]{1,0:T(8,128)(2,1)S(1)}, u32[]{:S(2)}, u32[]{:S(2)}) collective-permute-start(bf16[112,2048]{1,0:T(8,128)(2,1)S(1)} %get-tuple-element.7), channel_id=1, source_target_pairs={{0,1},{1,2},{2,3},{3,0},{4,5},{5,6},{6,7},{7,4},{8,9},{9,10},{10,1... | collective-permute-start | bytes 1376264 | tf_op jit(solution)/shard_map/ppermute | solution.py:12
  107.0 15.3 %collective-permute-start.14 = (bf16[112,2048]{1,0:T(8,128)(2,1)S(1)}, bf16[112,2048]{1,0:T(8,128)(2,1)S(1)}, u32[]{:S(2)}, u32[]{:S(2)}) collective-permute-start(bf16[112,2048]{1,0:T(8,128)(2,1)S(1)} %get-tuple-element.10), channel_id=1, source_target_pairs={{0,1},{1,2},{2,3},{3,0},{4,5},{5,6},{6,7},{7,4},{8,9},{9,10},{10,1... | collective-permute-start | bytes 1376264 | tf_op jit(solution)/shard_map/ppermute | solution.py:12
  109.0 24.4 %collective-permute-start.15 = (bf16[112,2048]{1,0:T(8,128)(2,1)S(1)}, bf16[112,2048]{1,0:T(8,128)(2,1)S(1)}, u32[]{:S(2)}, u32[]{:S(2)}) collective-permute-start(bf16[112,2048]{1,0:T(8,128)(2,1)S(1)} %get-tuple-element.12), channel_id=1, source_target_pairs={{0,3},{1,0},{2,1},{3,2},{4,7},{5,4},{6,5},{7,6},{8,11},{9,8},{10,9... | collective-permute-start | bytes 1376264 | tf_op jit(solution)/shard_map/ppermute | solution.py:12
  112.9 20.5 %collective-permute-start.16 = (bf16[112,2048]{1,0:T(8,128)(2,1)S(1)}, bf16[112,2048]{1,0:T(8,128)(2,1)S(1)}, u32[]{:S(2)}, u32[]{:S(2)}) collective-permute-start(bf16[112,2048]{1,0:T(8,128)(2,1)S(1)} %get-tuple-element.11), channel_id=1, source_target_pairs={{0,2},{1,3},{2,0},{3,1},{4,6},{5,7},{6,4},{7,5},{8,10},{9,11},{10,... | collective-permute-start | bytes 1376264 | tf_op jit(solution)/shard_map/ppermute | solution.py:12
  122.4 14.7 %collective-permute-start.12 = (bf16[112,2048]{1,0:T(8,128)(2,1)S(1)}, bf16[112,2048]{1,0:T(8,128)(2,1)S(1)}, u32[]{:S(2)}, u32[]{:S(2)}) collective-permute-start(bf16[112,2048]{1,0:T(8,128)(2,1)S(1)} %fusion.8), channel_id=1, source_target_pairs={{0,4},{4,0},{8,12},{12,8},{16,20},{20,16},{24,28},{28,24},{32,36},... | collective-permute-start | bytes 1376264 | tf_op jit(solution)/shard_map/ppermute | solution.py:12
  142.4 31.7 %collective-permute-start.19 = (bf16[2,2,56,768]{3,2,1,0:T(8,128)(2,1)S(1)}, bf16[2,2,56,768]{3,2,1,0:T(8,128)(2,1)S(1)}, u32[]{:S(2)}, u32[]{:S(2)}) collective-permute-start(bf16[2,2,56,768]{3,2,1,0:T(8,128)(2,1)S(1)} %get-tuple-element.13), channel_id=1, source_target_pairs={{0,16},{4,20},{8,24},{12,28},{16,0},{20,4},{24,8},{28,12},{32,48},... | collective-permute-start | bytes 1032200 | tf_op jit(solution)/shard_map/ppermute | solution.py:12
  150.5 23.6 %collective-permute-start.20 = (bf16[2,2,56,768]{3,2,1,0:T(8,128)(2,1)S(1)}, bf16[2,2,56,768]{3,2,1,0:T(8,128)(2,1)S(1)}, u32[]{:S(2)}, u32[]{:S(2)}) collective-permute-start(bf16[2,2,56,768]{3,2,1,0:T(8,128)(2,1)S(1)} %get-tuple-element.14), channel_id=1, source_target_pairs={{0,24},{4,28},{8,16},{12,20},{16,8},{20,12},{24,0},{28,4},{32,56},... | collective-permute-start | bytes 1032200 | tf_op jit(solution)/shard_map/ppermute | solution.py:12
  157.0 23.1 %collective-permute-start.22 = (bf16[2,2,56,768]{3,2,1,0:T(8,128)(2,1)S(1)}, bf16[2,2,56,768]{3,2,1,0:T(8,128)(2,1)}, u32[]{:S(2)}, u32[]{:S(2)}) collective-permute-start(bf16[2,2,56,768]{3,2,1,0:T(8,128)(2,1)S(1)} %fusion.48), channel_id=1, source_target_pairs={{0,8},{4,12},{8,0},{12,4},{16,24},{20,28},{24,16},{28,20},{32,40},... | collective-permute-start | bytes 1032200 | tf_op jit(solution)/shard_map/ppermute | solution.py:12
  181.3 20.7 %collective-permute-start.23 = (bf16[56,768]{1,0:T(8,128)(2,1)S(1)}, bf16[56,768]{1,0:T(8,128)(2,1)S(1)}, u32[]{:S(2)}, u32[]{:S(2)}) collective-permute-start(bf16[56,768]{1,0:T(8,128)(2,1)S(1)} %get-tuple-element.28), channel_id=1, source_target_pairs={{0,1},{1,98},{2,83},{3,32},{4,7},{5,100},{6,85},{7,38},{8,89},{9,4... | collective-permute-start | bytes 258056 | tf_op jit(solution)/shard_map/ppermute | solution.py:53
  185.4 16.7 %collective-permute-start.24 = (bf16[56,768]{1,0:T(8,128)(2,1)S(1)}, bf16[56,768]{1,0:T(8,128)(2,1)S(1)}, u32[]{:S(2)}, u32[]{:S(2)}) collective-permute-start(bf16[56,768]{1,0:T(8,128)(2,1)S(1)} %get-tuple-element.27), channel_id=1, source_target_pairs={{0,5},{1,102},{2,87},{3,36},{4,3},{5,96},{6,81},{7,34},{8,93},{9,4... | collective-permute-start | bytes 258056 | tf_op jit(solution)/shard_map/ppermute | solution.py:53
  193.0 18.8 %collective-permute-start.26 = (bf16[56,768]{1,0:T(8,128)(2,1)S(1)}, bf16[56,768]{1,0:T(8,128)(2,1)S(1)}, u32[]{:S(2)}, u32[]{:S(2)}) collective-permute-start(bf16[56,768]{1,0:T(8,128)(2,1)S(1)} %get-tuple-element.25), channel_id=1, source_target_pairs={{0,4},{1,101},{2,86},{3,39},{4,2},{5,99},{6,80},{7,33},{8,92},{9,4... | collective-permute-start | bytes 258056 | tf_op jit(solution)/shard_map/ppermute | solution.py:53
  (6 other events, 48.2 us)

commit v5 on v4

--- a/solution.py
+++ b/solution.py
@@ -36,10 +36,15 @@
 
 
 def cut_sum(blocks):
-    from_left = along_cuts(blocks[1], 1)
-    from_right = along_cuts(blocks[3], 3)
-    from_far = along_cuts(blocks[2], 2)
-    return sum(part.astype(jnp.float32) for part in (blocks[0], from_left, from_right, from_far))
+    part = blocks[2].shape[0] // 2
+    from_left = along_cuts(blocks[2][:part], 1).astype(jnp.float32)
+    from_right = along_cuts(blocks[2][part:], 3).astype(jnp.float32)
+    added = (blocks[1][:part] + from_left).astype(jnp.bfloat16)
+    to_right = jnp.concatenate([added, blocks[1][part:]])
+    added = (blocks[3][part:] + from_right).astype(jnp.bfloat16)
+    to_left = jnp.concatenate([blocks[3][:part], added])
+    arrivals = [along_cuts(to_right, 1), along_cuts(to_left, 3)]
+    return blocks[0] + sum(part.astype(jnp.float32) for part in arrivals)
 
 
 def between_devices(value, target):
@@ -132,9 +137,13 @@
     numbers = ((first + jnp.arange(4)) % 4)[:, None, None]
     chunk = sum(jnp.where(numbers == k, rows[None], 0) for k, rows in enumerate(sources))
     chunk = after(chunk, near[0], near[1])
+    arrivals = []
 
     def hidden_part(m):
         rows = chunk if m == 0 else swapped_chips(chunk, m)
+        arrivals.append(rows)
+        if m == 0:
+            rows = after(rows, arrivals[0])
         flat = rows.reshape(4 * ROW_LIMIT, width)
         part = jnp.dot(flat, up, preferred_element_type=jnp.float32).astype(jnp.bfloat16)
         return part.reshape(4, ROW_LIMIT, 2 * ff)
@@ -156,8 +165,6 @@
         swapped = other_core(active)
         own_units = jnp.concatenate([active[:, :ff], swapped[:, ff:]])
         other_units = jnp.concatenate([active[:, ff:], swapped[:, :ff]])
-        if 2 in group and 0 not in group:
-            own_units = after(own_units, hiddens[1])
         out = times_down(own_units, other_units).reshape(2, 2, len(group), ROW_LIMIT, width)
         for at, m in enumerate(group):
             if m == 0:

time: 214 us -> 206 us (0.963); the launches traced: 213 us -> 202 us
  waiting for transfers between devices: 85.8 us -> 62.7 us
  starting transfers between devices: 101 us -> 107 us
  local copies, waits for them, and re-layouts: 4.56 us -> 9.23 us
    ppermute x18 -> x20, waiting for transfers between devices: 72.8 us -> 50.3 us  [moved(): return lax.ppermute(value, axis, list(enumerate(targets)))]
    ppermute x18 -> x20, starting transfers between devices: 67.9 us -> 74.3 us  [moved(): return lax.ppermute(value, axis, list(enumerate(targets)))]
    broadcast_in_dim x8, local copies, waits for them, and re-layouts: 0.65 us -> 5.1 us  [shards(): jnp.where(numbers == k, rows[None], 0)]
  transfers between devices with their start and end apart: 27 -> 29, of which waited for: 13 -> 13; matrix products, arithmetic and copies ran while one was open for 8% -> 12% of each run, Pallas kernels for 0% -> 0%
where the time goes in v5:
time: 206 us; the launch traced here: 202 us
  starting transfers between devices  107 us (52%)
  waiting for transfers between devices  62.7 us (30%)
  other arithmetic  10 us (5%)
  matrix products  9.53 us (5%)
  local copies, waits for them, and re-layouts  9.23 us (4%)
  between operations  4.16 us (2%)
    ppermute x20, starting transfers between devices, moved(): return lax.ppermute(value, axis, list(enumerate(targets)))  74.3 us
    ppermute x20, waiting for transfers between devices, moved(): return lax.ppermute(value, axis, list(enumerate(targets)))  50.3 us
    ppermute x8, starting transfers between devices, between_devices(): return lax.ppermute(value, ('expert', 'cuts'), pairs)  30.5 us
    ppermute x8, waiting for transfers between devices, between_devices(): return lax.ppermute(value, ('expert', 'cuts'), pairs)  8.69 us
    broadcast_in_dim x8, local copies, waits for them, and re-layouts, shards(): jnp.where(numbers == k, rows[None], 0)  5.1 us
    dot_general x8, matrix products, times_down(): jnp.dot(u, w, preferred_element_type=jnp.float32)  4.45 us
  transfers between devices with their start and end apart: 29, of which 13 were waited for; matrix products, arithmetic and copies ran while one was open for 12% of the time, Pallas kernels for 0%

profile of v5, /device:TPU:6, one launch (start us, length us, event | category | flops | bytes accessed | tf_op | source)
XLA Modules:
  0.0 202.4 jit_solution(10658586709447673150)
XLA Ops:
  1.9 7.9 %collective-permute-start.6 = (bf16[1024,768]{1,0:T(8,128)(2,1)}, bf16[1024,768]{1,0:T(8,128)(2,1)S(1)}, u32[]{:S(2)}, u32[]{:S(2)}) collective-permute-start(bf16[1024,768]{1,0:T(8,128)(2,1)} %bitcast.131), channel_id=1, source_target_pairs={{0,5},{1,6},{2,7},{3,4},{4,3},{5,0},{6,1},{7,2},{8,13},{9,14},{10,... | collective-permute-start | bytes 4718600 | tf_op jit(solution)/shard_map/ppermute | solution.py:58
  18.2 3.8 %collective-permute-done = bf16[1,128,768]{2,1,0:T(8,128)(2,1)S(1)} collective-permute-done((bf16[1,128,768]{2,1,0:T(8,128)(2,1)}, bf16[1,128,768]{2,1,0:T(8,128)(2,1)S(1)}, u32[]{:S(2)}, u32[]{:S(2)}) %collective-permute-start) | collective-permute-done | bytes 196640 | tf_op jit(solution)/shard_map/ppermute | solution.py:88
  22.9 6.1 %collective-permute-start.2 = (bf16[56,768]{1,0:T(8,128)(2,1)}, bf16[56,768]{1,0:T(8,128)(2,1)S(1)}, u32[]{:S(2)}, u32[]{:S(2)}) collective-permute-start(bf16[56,768]{1,0:T(8,128)(2,1)} %get-tuple-element.30), channel_id=1, source_target_pairs={{0,32},{4,36},{8,40},{12,44},{16,48},{20,52},{24,56},{28,60},{32,6... | collective-permute-start | bytes 258056 | tf_op jit(solution)/shard_map/ppermute | solution.py:12
  28.9 10.0 %collective-permute-start.3 = (bf16[56,768]{1,0:T(8,128)(2,1)}, bf16[56,768]{1,0:T(8,128)(2,1)}, u32[]{:S(2)}, u32[]{:S(2)}) collective-permute-start(bf16[56,768]{1,0:T(8,128)(2,1)} %get-tuple-element.32), channel_id=1, source_target_pairs={{0,80},{4,84},{8,88},{12,92},{16,64},{20,68},{24,72},{28,76},{32,1... | collective-permute-start | bytes 258056 | tf_op jit(solution)/shard_map/ppermute | solution.py:12
  39.0 5.5 %collective-permute-start.4 = (bf16[56,768]{1,0:T(8,128)(2,1)}, bf16[56,768]{1,0:T(8,128)(2,1)}, u32[]{:S(2)}, u32[]{:S(2)}) collective-permute-start(bf16[56,768]{1,0:T(8,128)(2,1)} %get-tuple-element.31), channel_id=1, source_target_pairs={{0,96},{4,100},{8,104},{12,108},{16,112},{20,116},{24,120},{28,124... | collective-permute-start | bytes 258056 | tf_op jit(solution)/shard_map/ppermute | solution.py:12
  61.2 3.3 %collective-permute-start.8 = (bf16[4,56,768]{2,1,0:T(8,128)(2,1)S(1)}, bf16[4,56,768]{2,1,0:T(8,128)(2,1)S(1)}, u32[]{:S(2)}, u32[]{:S(2)}) collective-permute-start(bf16[4,56,768]{2,1,0:T(8,128)(2,1)S(1)} %add_add_fusion), channel_id=1, source_target_pairs={{0,24},{4,28},{8,16},{12,20},{16,8},{20,12},{24,0},{28,4},{32,56},... | collective-permute-start | bytes 1032200 | tf_op jit(solution)/shard_map/ppermute | solution.py:12
  64.6 4.0 %collective-permute-start.18 = (bf16[4,56,768]{2,1,0:T(8,128)(2,1)S(1)}, bf16[4,56,768]{2,1,0:T(8,128)(2,1)S(1)}, u32[]{:S(2)}, u32[]{:S(2)}) collective-permute-start(bf16[4,56,768]{2,1,0:T(8,128)(2,1)S(1)} %add_add_fusion), channel_id=1, source_target_pairs={{0,8},{4,12},{8,0},{12,4},{16,24},{20,28},{24,16},{28,20},{32,40},... | collective-permute-start | bytes 1032200 | tf_op jit(solution)/shard_map/ppermute | solution.py:12
  68.5 13.2 %collective-permute-done.7 = bf16[4,56,768]{2,1,0:T(8,128)(2,1)S(1)} collective-permute-done((bf16[4,56,768]{2,1,0:T(8,128)(2,1)S(1)}, bf16[4,56,768]{2,1,0:T(8,128)(2,1)S(1)}, u32[]{:S(2)}, u32[]{:S(2)}) %collective-permute-start.7) | collective-permute-done | bytes 344096 | tf_op jit(solution)/shard_map/ppermute | solution.py:12
  85.6 3.9 %collective-permute-start.11 = (bf16[56,2048]{1,0:T(8,128)(2,1)S(1)}, bf16[56,2048]{1,0:T(8,128)(2,1)S(1)}, u32[]{:S(2)}, u32[]{:S(2)}) collective-permute-start(bf16[56,2048]{1,0:T(8,128)(2,1)S(1)} %get-tuple-element.8), channel_id=1, source_target_pairs={{0,3},{1,0},{2,1},{3,2},{4,7},{5,4},{6,5},{7,6},{8,11},{9,8},{10,9... | collective-permute-start | bytes 688136 | tf_op jit(solution)/shard_map/ppermute | solution.py:12
  92.8 3.1 %collective-permute-start.19 = (bf16[56,2048]{1,0:T(8,128)(2,1)S(1)}, bf16[56,2048]{1,0:T(8,128)(2,1)S(1)}, u32[]{:S(2)}, u32[]{:S(2)}) collective-permute-start(bf16[56,2048]{1,0:T(8,128)(2,1)S(1)} %get-tuple-element.9), channel_id=1, source_target_pairs={{0,1},{1,2},{2,3},{3,0},{4,5},{5,6},{6,7},{7,4},{8,9},{9,10},{10,1... | collective-permute-start | bytes 688136 | tf_op jit(solution)/shard_map/ppermute | solution.py:12
  99.7 4.3 %collective-permute-start.10 = (bf16[112,2048]{1,0:T(8,128)(2,1)S(1)}, bf16[112,2048]{1,0:T(8,128)(2,1)S(1)}, u32[]{:S(2)}, u32[]{:S(2)}) collective-permute-start(bf16[112,2048]{1,0:T(8,128)(2,1)S(1)} %pad_maximum_fusion.4), channel_id=1, source_target_pairs={{0,1},{1,2},{2,3},{3,0},{4,5},{5,6},{6,7},{7,4},{8,9},{9,10},{10,1... | collective-permute-start | bytes 1376264 | tf_op jit(solution)/shard_map/ppermute | solution.py:12
  106.9 4.5 %collective-permute-start.20 = (bf16[112,2048]{1,0:T(8,128)(2,1)S(1)}, bf16[112,2048]{1,0:T(8,128)(2,1)S(1)}, u32[]{:S(2)}, u32[]{:S(2)}) collective-permute-start(bf16[112,2048]{1,0:T(8,128)(2,1)S(1)} %pad_maximum_fusion.8), channel_id=1, source_target_pairs={{0,1},{1,2},{2,3},{3,0},{4,5},{5,6},{6,7},{7,4},{8,9},{9,10},{10,1... | collective-permute-start | bytes 1376264 | tf_op jit(solution)/shard_map/ppermute | solution.py:12
  111.5 3.6 %collective-permute-done.10 = bf16[112,2048]{1,0:T(8,128)(2,1)S(1)} collective-permute-done((bf16[112,2048]{1,0:T(8,128)(2,1)S(1)}, bf16[112,2048]{1,0:T(8,128)(2,1)S(1)}, u32[]{:S(2)}, u32[]{:S(2)}) %collective-permute-start.10) | collective-permute-done | bytes 458784 | tf_op jit(solution)/shard_map/ppermute | solution.py:12
  122.9 5.4 %collective-permute-done.22 = bf16[112,2048]{1,0:T(8,128)(2,1)S(1)} collective-permute-done((bf16[112,2048]{1,0:T(8,128)(2,1)S(1)}, bf16[112,2048]{1,0:T(8,128)(2,1)S(1)}, u32[]{:S(2)}, u32[]{:S(2)}) %collective-permute-start.22) | collective-permute-done | bytes 458784 | tf_op jit(solution)/shard_map/ppermute | solution.py:12
  134.1 5.9 %collective-permute-start.16 = (bf16[2,2,56,768]{3,2,1,0:T(8,128)(2,1)}, bf16[2,2,56,768]{3,2,1,0:T(8,128)(2,1)}, u32[]{:S(2)}, u32[]{:S(2)}) collective-permute-start(bf16[2,2,56,768]{3,2,1,0:T(8,128)(2,1)} %get-tuple-element.13), channel_id=1, source_target_pairs={{0,16},{4,20},{8,24},{12,28},{16,0},{20,4},{24,8},{28,12},{32,48},... | collective-permute-start | bytes 1032200 | tf_op jit(solution)/shard_map/ppermute | solution.py:12
  140.1 5.5 %collective-permute-start.17 = (bf16[2,2,56,768]{3,2,1,0:T(8,128)(2,1)}, bf16[2,2,56,768]{3,2,1,0:T(8,128)(2,1)}, u32[]{:S(2)}, u32[]{:S(2)}) collective-permute-start(bf16[2,2,56,768]{3,2,1,0:T(8,128)(2,1)} %get-tuple-element.14), channel_id=1, source_target_pairs={{0,24},{4,28},{8,16},{12,20},{16,8},{20,12},{24,0},{28,4},{32,56},... | collective-permute-start | bytes 1032200 | tf_op jit(solution)/shard_map/ppermute | solution.py:12
  150.2 13.9 %collective-permute-done.16 = bf16[2,2,56,768]{3,2,1,0:T(8,128)(2,1)} collective-permute-done((bf16[2,2,56,768]{3,2,1,0:T(8,128)(2,1)}, bf16[2,2,56,768]{3,2,1,0:T(8,128)(2,1)}, u32[]{:S(2)}, u32[]{:S(2)}) %collective-permute-start.16) | collective-permute-done | bytes 344096 | tf_op jit(solution)/shard_map/ppermute | solution.py:12
  164.1 7.0 %collective-permute-done.24 = bf16[2,2,56,768]{3,2,1,0:T(8,128)(2,1)S(1)} collective-permute-done((bf16[2,2,56,768]{3,2,1,0:T(8,128)(2,1)S(1)}, bf16[2,2,56,768]{3,2,1,0:T(8,128)(2,1)S(1)}, u32[]{:S(2)}, u32[]{:S(2)}) %collective-permute-start.24) | collective-permute-done | bytes 344096 | tf_op jit(solution)/shard_map/ppermute | solution.py:12
  172.3 5.3 %collective-permute-start.25 = (bf16[56,768]{1,0:T(8,128)(2,1)S(1)}, bf16[56,768]{1,0:T(8,128)(2,1)S(1)}, u32[]{:S(2)}, u32[]{:S(2)}) collective-permute-start(bf16[56,768]{1,0:T(8,128)(2,1)S(1)} %get-tuple-element.28), channel_id=1, source_target_pairs={{0,1},{1,98},{2,83},{3,32},{4,7},{5,100},{6,85},{7,38},{8,89},{9,4... | collective-permute-start | bytes 258056 | tf_op jit(solution)/shard_map/ppermute | solution.py:58
  177.6 3.5 %collective-permute-start.26 = (bf16[56,768]{1,0:T(8,128)(2,1)S(1)}, bf16[56,768]{1,0:T(8,128)(2,1)S(1)}, u32[]{:S(2)}, u32[]{:S(2)}) collective-permute-start(bf16[56,768]{1,0:T(8,128)(2,1)S(1)} %get-tuple-element.27), channel_id=1, source_target_pairs={{0,5},{1,102},{2,87},{3,36},{4,3},{5,96},{6,81},{7,34},{8,93},{9,4... | collective-permute-start | bytes 258056 | tf_op jit(solution)/shard_map/ppermute | solution.py:58
  181.1 5.5 %collective-permute-start.27 = (bf16[56,768]{1,0:T(8,128)(2,1)S(1)}, bf16[56,768]{1,0:T(8,128)(2,1)S(1)}, u32[]{:S(2)}, u32[]{:S(2)}) collective-permute-start(bf16[56,768]{1,0:T(8,128)(2,1)S(1)} %get-tuple-element.26), channel_id=1, source_target_pairs={{0,0},{1,97},{2,82},{3,35},{4,6},{5,103},{6,84},{7,37},{8,88},{9,4... | collective-permute-start | bytes 258056 | tf_op jit(solution)/shard_map/ppermute | solution.py:58
  186.6 5.6 %collective-permute-start.28 = (bf16[56,768]{1,0:T(8,128)(2,1)S(1)}, bf16[56,768]{1,0:T(8,128)(2,1)S(1)}, u32[]{:S(2)}, u32[]{:S(2)}) collective-permute-start(bf16[56,768]{1,0:T(8,128)(2,1)S(1)} %get-tuple-element.25), channel_id=1, source_target_pairs={{0,4},{1,101},{2,86},{3,39},{4,2},{5,99},{6,80},{7,33},{8,92},{9,4... | collective-permute-start | bytes 258056 | tf_op jit(solution)/shard_map/ppermute | solution.py:58
  192.4 3.1 %collective-permute-done.27 = bf16[56,768]{1,0:T(8,128)(2,1)S(1)} collective-permute-done((bf16[56,768]{1,0:T(8,128)(2,1)S(1)}, bf16[56,768]{1,0:T(8,128)(2,1)S(1)}, u32[]{:S(2)}, u32[]{:S(2)}) %collective-permute-start.27) | collective-permute-done | bytes 86048 | tf_op jit(solution)/shard_map/ppermute | solution.py:58
  195.5 5.6 %collective-permute-done.28 = bf16[56,768]{1,0:T(8,128)(2,1)S(1)} collective-permute-done((bf16[56,768]{1,0:T(8,128)(2,1)S(1)}, bf16[56,768]{1,0:T(8,128)(2,1)S(1)}, u32[]{:S(2)}, u32[]{:S(2)}) %collective-permute-start.28) | collective-permute-done | bytes 86048 | tf_op jit(solution)/shard_map/ppermute | solution.py:58
  (113 shorter events, 58.8 us)
Async XLA Ops:
  0.0 16.3 %collective-permute-start.1 = (bf16[768,1024]{1,0:T(8,128)(2,1)}, bf16[768,1024]{1,0:T(8,128)(2,1)}, u32[]{:S(2)}, u32[]{:S(2)}) collective-permute-start(bf16[768,1024]{1,0:T(8,128)(2,1)} %bitcast.133), channel_id=1, source_target_pairs={{0,4},{4,0},{8,12},{12,8},{16,20},{20,16},{24,28},{28,24},{32,36},... | collective-permute-start | bytes 4718600 | tf_op jit(solution)/shard_map/ppermute | solution.py:12
  1.9 47.5 %collective-permute-start.6 = (bf16[1024,768]{1,0:T(8,128)(2,1)}, bf16[1024,768]{1,0:T(8,128)(2,1)S(1)}, u32[]{:S(2)}, u32[]{:S(2)}) collective-permute-start(bf16[1024,768]{1,0:T(8,128)(2,1)} %bitcast.131), channel_id=1, source_target_pairs={{0,5},{1,6},{2,7},{3,4},{4,3},{5,0},{6,1},{7,2},{8,13},{9,14},{10,... | collective-permute-start | bytes 4718600 | tf_op jit(solution)/shard_map/ppermute | solution.py:58
  9.8 40.2 %collective-permute-start.5 = (bf16[1024,768]{1,0:T(8,128)(2,1)}, bf16[1024,768]{1,0:T(8,128)(2,1)S(1)}, u32[]{:S(2)}, u32[]{:S(2)}) collective-permute-start(bf16[1024,768]{1,0:T(8,128)(2,1)} %bitcast.132), channel_id=1, source_target_pairs={{0,3},{1,0},{2,1},{3,2},{4,5},{5,6},{6,7},{7,4},{8,11},{9,8},{10,9... | collective-permute-start | bytes 4718600 | tf_op jit(solution)/shard_map/ppermute | solution.py:58
  22.9 28.9 %collective-permute-start.2 = (bf16[56,768]{1,0:T(8,128)(2,1)}, bf16[56,768]{1,0:T(8,128)(2,1)S(1)}, u32[]{:S(2)}, u32[]{:S(2)}) collective-permute-start(bf16[56,768]{1,0:T(8,128)(2,1)} %get-tuple-element.30), channel_id=1, source_target_pairs={{0,32},{4,36},{8,40},{12,44},{16,48},{20,52},{24,56},{28,60},{32,6... | collective-permute-start | bytes 258056 | tf_op jit(solution)/shard_map/ppermute | solution.py:12
  28.9 23.0 %collective-permute-start.3 = (bf16[56,768]{1,0:T(8,128)(2,1)}, bf16[56,768]{1,0:T(8,128)(2,1)}, u32[]{:S(2)}, u32[]{:S(2)}) collective-permute-start(bf16[56,768]{1,0:T(8,128)(2,1)} %get-tuple-element.32), channel_id=1, source_target_pairs={{0,80},{4,84},{8,88},{12,92},{16,64},{20,68},{24,72},{28,76},{32,1... | collective-permute-start | bytes 258056 | tf_op jit(solution)/shard_map/ppermute | solution.py:12
  39.0 15.8 %collective-permute-start.4 = (bf16[56,768]{1,0:T(8,128)(2,1)}, bf16[56,768]{1,0:T(8,128)(2,1)}, u32[]{:S(2)}, u32[]{:S(2)}) collective-permute-start(bf16[56,768]{1,0:T(8,128)(2,1)} %get-tuple-element.31), channel_id=1, source_target_pairs={{0,96},{4,100},{8,104},{12,108},{16,112},{20,116},{24,120},{28,124... | collective-permute-start | bytes 258056 | tf_op jit(solution)/shard_map/ppermute | solution.py:12
  55.9 25.8 %collective-permute-start.7 = (bf16[4,56,768]{2,1,0:T(8,128)(2,1)S(1)}, bf16[4,56,768]{2,1,0:T(8,128)(2,1)S(1)}, u32[]{:S(2)}, u32[]{:S(2)}) collective-permute-start(bf16[4,56,768]{2,1,0:T(8,128)(2,1)S(1)} %add_add_fusion), channel_id=1, source_target_pairs={{0,16},{4,20},{8,24},{12,28},{16,0},{20,4},{24,8},{28,12},{32,48},... | collective-permute-start | bytes 1032200 | tf_op jit(solution)/shard_map/ppermute | solution.py:12
  60.4 71.0 %collective-permute-start.15 = (bf16[1024,768]{1,0:T(8,128)(2,1)S(1)}, bf16[1024,768]{1,0:T(8,128)(2,1)S(1)}, u32[]{:S(2)}, u32[]{:S(2)}) collective-permute-start(bf16[1024,768]{1,0:T(8,128)(2,1)S(1)} %broadcast_select_fusion), channel_id=1, source_target_pairs={{0,7},{1,4},{2,5},{3,6},{4,0},{5,1},{6,2},{7,3},{8,15},{9,12},{10,... | collective-permute-start | bytes 4718600 | tf_op jit(solution)/shard_map/ppermute | solution.py:58
  60.5 71.5 %collective-permute-start.14 = (bf16[1024,768]{1,0:T(8,128)(2,1)S(1)}, bf16[1024,768]{1,0:T(8,128)(2,1)S(1)}, u32[]{:S(2)}, u32[]{:S(2)}) collective-permute-start(bf16[1024,768]{1,0:T(8,128)(2,1)S(1)} %collective-permute-done.6), channel_id=1, source_target_pairs={{4,5},{5,6},{6,7},{7,4},{12,13},{13,14},{14,15},{15,12},{20,21},{2... | collective-permute-start | bytes 4718600 | tf_op jit(solution)/shard_map/ppermute | solution.py:58
  61.2 23.4 %collective-permute-start.8 = (bf16[4,56,768]{2,1,0:T(8,128)(2,1)S(1)}, bf16[4,56,768]{2,1,0:T(8,128)(2,1)S(1)}, u32[]{:S(2)}, u32[]{:S(2)}) collective-permute-start(bf16[4,56,768]{2,1,0:T(8,128)(2,1)S(1)} %add_add_fusion), channel_id=1, source_target_pairs={{0,24},{4,28},{8,16},{12,20},{16,8},{20,12},{24,0},{28,4},{32,56},... | collective-permute-start | bytes 1032200 | tf_op jit(solution)/shard_map/ppermute | solution.py:12
  64.6 28.2 %collective-permute-start.18 = (bf16[4,56,768]{2,1,0:T(8,128)(2,1)S(1)}, bf16[4,56,768]{2,1,0:T(8,128)(2,1)S(1)}, u32[]{:S(2)}, u32[]{:S(2)}) collective-permute-start(bf16[4,56,768]{2,1,0:T(8,128)(2,1)S(1)} %add_add_fusion), channel_id=1, source_target_pairs={{0,8},{4,12},{8,0},{12,4},{16,24},{20,28},{24,16},{28,20},{32,40},... | collective-permute-start | bytes 1032200 | tf_op jit(solution)/shard_map/ppermute | solution.py:12
  82.7 14.2 %collective-permute-start.9 = (bf16[56,2048]{1,0:T(8,128)(2,1)S(1)}, bf16[56,2048]{1,0:T(8,128)(2,1)S(1)}, u32[]{:S(2)}, u32[]{:S(2)}) collective-permute-start(bf16[56,2048]{1,0:T(8,128)(2,1)S(1)} %get-tuple-element.5), channel_id=1, source_target_pairs={{0,1},{1,2},{2,3},{3,0},{4,5},{5,6},{6,7},{7,4},{8,9},{9,10},{10,1... | collective-permute-start | bytes 688136 | tf_op jit(solution)/shard_map/ppermute | solution.py:12
  85.6 14.2 %collective-permute-start.11 = (bf16[56,2048]{1,0:T(8,128)(2,1)S(1)}, bf16[56,2048]{1,0:T(8,128)(2,1)S(1)}, u32[]{:S(2)}, u32[]{:S(2)}) collective-permute-start(bf16[56,2048]{1,0:T(8,128)(2,1)S(1)} %get-tuple-element.8), channel_id=1, source_target_pairs={{0,3},{1,0},{2,1},{3,2},{4,7},{5,4},{6,5},{7,6},{8,11},{9,8},{10,9... | collective-permute-start | bytes 688136 | tf_op jit(solution)/shard_map/ppermute | solution.py:12
  99.7 15.4 %collective-permute-start.10 = (bf16[112,2048]{1,0:T(8,128)(2,1)S(1)}, bf16[112,2048]{1,0:T(8,128)(2,1)S(1)}, u32[]{:S(2)}, u32[]{:S(2)}) collective-permute-start(bf16[112,2048]{1,0:T(8,128)(2,1)S(1)} %pad_maximum_fusion.4), channel_id=1, source_target_pairs={{0,1},{1,2},{2,3},{3,0},{4,5},{5,6},{6,7},{7,4},{8,9},{9,10},{10,1... | collective-permute-start | bytes 1376264 | tf_op jit(solution)/shard_map/ppermute | solution.py:12
  104.2 15.1 %collective-permute-start.12 = (bf16[112,2048]{1,0:T(8,128)(2,1)S(1)}, bf16[112,2048]{1,0:T(8,128)(2,1)S(1)}, u32[]{:S(2)}, u32[]{:S(2)}) collective-permute-start(bf16[112,2048]{1,0:T(8,128)(2,1)S(1)} %pad_maximum_fusion.5), channel_id=1, source_target_pairs={{0,3},{1,0},{2,1},{3,2},{4,7},{5,4},{6,5},{7,6},{8,11},{9,8},{10,9... | collective-permute-start | bytes 1376264 | tf_op jit(solution)/shard_map/ppermute | solution.py:12
  106.9 16.0 %collective-permute-start.20 = (bf16[112,2048]{1,0:T(8,128)(2,1)S(1)}, bf16[112,2048]{1,0:T(8,128)(2,1)S(1)}, u32[]{:S(2)}, u32[]{:S(2)}) collective-permute-start(bf16[112,2048]{1,0:T(8,128)(2,1)S(1)} %pad_maximum_fusion.8), channel_id=1, source_target_pairs={{0,1},{1,2},{2,3},{3,0},{4,5},{5,6},{6,7},{7,4},{8,9},{9,10},{10,1... | collective-permute-start | bytes 1376264 | tf_op jit(solution)/shard_map/ppermute | solution.py:12
  128.8 16.7 %collective-permute-start.23 = (bf16[112,2048]{1,0:T(8,128)(2,1)S(1)}, bf16[112,2048]{1,0:T(8,128)(2,1)S(1)}, u32[]{:S(2)}, u32[]{:S(2)}) collective-permute-start(bf16[112,2048]{1,0:T(8,128)(2,1)S(1)} %fusion.16), channel_id=1, source_target_pairs={{0,4},{4,0},{8,12},{12,8},{16,20},{20,16},{24,28},{28,24},{32,36},... | collective-permute-start | bytes 1376264 | tf_op jit(solution)/shard_map/ppermute | solution.py:12
  134.1 29.9 %collective-permute-start.16 = (bf16[2,2,56,768]{3,2,1,0:T(8,128)(2,1)}, bf16[2,2,56,768]{3,2,1,0:T(8,128)(2,1)}, u32[]{:S(2)}, u32[]{:S(2)}) collective-permute-start(bf16[2,2,56,768]{3,2,1,0:T(8,128)(2,1)} %get-tuple-element.13), channel_id=1, source_target_pairs={{0,16},{4,20},{8,24},{12,28},{16,0},{20,4},{24,8},{28,12},{32,48},... | collective-permute-start | bytes 1032200 | tf_op jit(solution)/shard_map/ppermute | solution.py:12
  140.1 24.0 %collective-permute-start.17 = (bf16[2,2,56,768]{3,2,1,0:T(8,128)(2,1)}, bf16[2,2,56,768]{3,2,1,0:T(8,128)(2,1)}, u32[]{:S(2)}, u32[]{:S(2)}) collective-permute-start(bf16[2,2,56,768]{3,2,1,0:T(8,128)(2,1)} %get-tuple-element.14), channel_id=1, source_target_pairs={{0,24},{4,28},{8,16},{12,20},{16,8},{20,12},{24,0},{28,4},{32,56},... | collective-permute-start | bytes 1032200 | tf_op jit(solution)/shard_map/ppermute | solution.py:12
  148.0 23.0 %collective-permute-start.24 = (bf16[2,2,56,768]{3,2,1,0:T(8,128)(2,1)S(1)}, bf16[2,2,56,768]{3,2,1,0:T(8,128)(2,1)S(1)}, u32[]{:S(2)}, u32[]{:S(2)}) collective-permute-start(bf16[2,2,56,768]{3,2,1,0:T(8,128)(2,1)S(1)} %fusion.32), channel_id=1, source_target_pairs={{0,8},{4,12},{8,0},{12,4},{16,24},{20,28},{24,16},{28,20},{32,40},... | collective-permute-start | bytes 1032200 | tf_op jit(solution)/shard_map/ppermute | solution.py:12
  172.3 20.1 %collective-permute-start.25 = (bf16[56,768]{1,0:T(8,128)(2,1)S(1)}, bf16[56,768]{1,0:T(8,128)(2,1)S(1)}, u32[]{:S(2)}, u32[]{:S(2)}) collective-permute-start(bf16[56,768]{1,0:T(8,128)(2,1)S(1)} %get-tuple-element.28), channel_id=1, source_target_pairs={{0,1},{1,98},{2,83},{3,32},{4,7},{5,100},{6,85},{7,38},{8,89},{9,4... | collective-permute-start | bytes 258056 | tf_op jit(solution)/shard_map/ppermute | solution.py:58
  177.6 14.8 %collective-permute-start.26 = (bf16[56,768]{1,0:T(8,128)(2,1)S(1)}, bf16[56,768]{1,0:T(8,128)(2,1)S(1)}, u32[]{:S(2)}, u32[]{:S(2)}) collective-permute-start(bf16[56,768]{1,0:T(8,128)(2,1)S(1)} %get-tuple-element.27), channel_id=1, source_target_pairs={{0,5},{1,102},{2,87},{3,36},{4,3},{5,96},{6,81},{7,34},{8,93},{9,4... | collective-permute-start | bytes 258056 | tf_op jit(solution)/shard_map/ppermute | solution.py:58
  181.1 14.4 %collective-permute-start.27 = (bf16[56,768]{1,0:T(8,128)(2,1)S(1)}, bf16[56,768]{1,0:T(8,128)(2,1)S(1)}, u32[]{:S(2)}, u32[]{:S(2)}) collective-permute-start(bf16[56,768]{1,0:T(8,128)(2,1)S(1)} %get-tuple-element.26), channel_id=1, source_target_pairs={{0,0},{1,97},{2,82},{3,35},{4,6},{5,103},{6,84},{7,37},{8,88},{9,4... | collective-permute-start | bytes 258056 | tf_op jit(solution)/shard_map/ppermute | solution.py:58
  186.6 14.5 %collective-permute-start.28 = (bf16[56,768]{1,0:T(8,128)(2,1)S(1)}, bf16[56,768]{1,0:T(8,128)(2,1)S(1)}, u32[]{:S(2)}, u32[]{:S(2)}) collective-permute-start(bf16[56,768]{1,0:T(8,128)(2,1)S(1)} %get-tuple-element.25), channel_id=1, source_target_pairs={{0,4},{1,101},{2,86},{3,39},{4,2},{5,99},{6,80},{7,33},{8,92},{9,4... | collective-permute-start | bytes 258056 | tf_op jit(solution)/shard_map/ppermute | solution.py:58
  (9 other events, 74.6 us)

commit v6 on v5

--- a/solution.py
+++ b/solution.py
@@ -75,11 +75,11 @@
     return (1, 3)[core] if part == 0 else (0, 2)[core]
 
 
-def back_home(value, part, other):
+def back_home(value, part):
     def target(j, c):
         k = (c + 2 * (j // 2 % 2)) % 4
         home = [j, (j - 8) % 32, j ^ 20, (j + 8) % 32][k]
-        return home ^ other, c + slice_step(part, j % 2)
+        return home, c + slice_step(part, j % 2)
 
     return between_devices(value, target)
 
@@ -121,8 +121,8 @@
 
     near = near_pieces(w_down[0, 0])
     last = last_pieces(w_down[0, 0], near, core)
+    picker = after(picker, up_other)
     packed = jnp.dot(picker, arrived, preferred_element_type=jnp.float32).astype(jnp.bfloat16)
-    packed = after(packed, up_other)
     same, other = packed[:ROW_LIMIT], packed[ROW_LIMIT:]
     ahead = jnp.where(low, same, other)
     behind = jnp.where(low, other, same)
@@ -134,13 +134,13 @@
         along_chips(behind, -4),
     ]
     first = (cut + 2 * (chip % 2)) % 4
-    numbers = ((first + jnp.arange(4)) % 4)[:, None, None]
-    chunk = sum(jnp.where(numbers == k, rows[None], 0) for k, rows in enumerate(sources))
-    chunk = after(chunk, near[0], near[1])
+    ring = jnp.stack(sources + sources[:3])
+    chunk = lax.dynamic_slice_in_dim(ring, first, 4, axis=0)
+    near_chunk = after(chunk, near[0], near[1])
     arrivals = []
 
     def hidden_part(m):
-        rows = chunk if m == 0 else swapped_chips(chunk, m)
+        rows = chunk if m == 0 else swapped_chips(near_chunk if m == 1 else chunk, m)
         arrivals.append(rows)
         if m == 0:
             rows = after(rows, arrivals[0])
@@ -174,11 +174,13 @@
                 total = total + swapped_chips(sent, m).astype(jnp.float32)
 
     rounded = total.astype(jnp.bfloat16)
+    came = jnp.stack([back_home(rounded[part], part) for part in range(2)])
+    came = [came[:, 0], other_core(came[:, 1])]
     same_sum = jnp.zeros((ROW_LIMIT, width), jnp.float32)
     other_sum = same_sum
     for part in range(2):
         for other in range(2):
-            rows = back_home(rounded[part, other], part, other).astype(jnp.float32)
+            rows = came[other][part].astype(jnp.float32)
             step = jnp.where(core ^ other == 0, slice_step(part, 0), slice_step(part, 1))
             source = (first - step) % 4
             is_same = (source == 0) | ((source == 1) & low) | ((source == 3) & ~low)

time: 206 us -> 199 us (0.966)
  waiting for transfers between devices: 62.7 us -> 73.5 us
  starting transfers between devices: 107 us -> 99.9 us
  local copies, waits for them, and re-layouts: 9.23 us -> 3.28 us
  other arithmetic: 10 us -> 5.69 us
    ppermute x8 -> x6, starting transfers between devices: 30.5 us -> 21.9 us  [between_devices(): return lax.ppermute(value, ('expert', 'cuts'), pairs)]
    ppermute x20 -> x21, waiting for transfers between devices: 50.3 us -> 56 us  [moved(): return lax.ppermute(value, axis, list(enumerate(targets)))]
    broadcast_in_dim x8 -> x0, local copies, waits for them, and re-layouts: 5.1 us -> none  [shards(): jnp.where(numbers == k, rows[None], 0)]
    ppermute x8 -> x6, waiting for transfers between devices: 8.69 us -> 13.7 us  [between_devices(): return lax.ppermute(value, ('expert', 'cuts'), pairs)]
    add x2 -> x3, other arithmetic: 2.32 us -> 0.1 us  [after(): return value + sum(corners).astype(value.dtype)]
    ppermute x20 -> x21, starting transfers between devices: 74.3 us -> 76.1 us  [moved(): return lax.ppermute(value, axis, list(enumerate(targets)))]
  transfers between devices with their start and end apart: 29 -> 28, of which waited for: 13 -> 15; matrix products, arithmetic and copies ran while one was open for 12% -> 9% of each run, Pallas kernels for 0% -> 0%
where the time goes in v6:
time: 199 us; the launch traced here: 196 us
  starting transfers between devices  99.9 us (50%)
  waiting for transfers between devices  73.5 us (37%)
  matrix products  9.51 us (5%)
  other arithmetic  5.69 us (3%)
  between operations  4.19 us (2%)
  local copies, waits for them, and re-layouts  3.28 us (2%)
    ppermute x21, starting transfers between devices, moved(): return lax.ppermute(value, axis, list(enumerate(targets)))  76.1 us
    ppermute x21, waiting for transfers between devices, moved(): return lax.ppermute(value, axis, list(enumerate(targets)))  56 us
    ppermute x6, starting transfers between devices, between_devices(): return lax.ppermute(value, ('expert', 'cuts'), pairs)  21.9 us
    ppermute x6, waiting for transfers between devices, between_devices(): return lax.ppermute(value, ('expert', 'cuts'), pairs)  13.7 us
    dot_general x8, matrix products, times_down(): jnp.dot(u, w, preferred_element_type=jnp.float32)  4.45 us
  transfers between devices with their start and end apart: 28, of which 15 were waited for; matrix products, arithmetic and copies ran while one was open for 9% of the time, Pallas kernels for 0%

profile of v6, /device:TPU:6, one launch (start us, length us, event | category | flops | bytes accessed | tf_op | source)
XLA Modules:
  0.0 196.1 jit_solution(17366075390586472159)
XLA Ops:
  1.9 7.9 %collective-permute-start.13 = (bf16[1024,768]{1,0:T(8,128)(2,1)}, bf16[1024,768]{1,0:T(8,128)(2,1)S(1)}, u32[]{:S(2)}, u32[]{:S(2)}) collective-permute-start(bf16[1024,768]{1,0:T(8,128)(2,1)} %bitcast.159), channel_id=1, source_target_pairs={{0,5},{1,6},{2,7},{3,4},{4,3},{5,0},{6,1},{7,2},{8,13},{9,14},{10,... | collective-permute-start | bytes 4718600 | tf_op jit(solution)/shard_map/ppermute | solution.py:58
  18.1 3.8 %collective-permute-done = bf16[1,128,768]{2,1,0:T(8,128)(2,1)S(1)} collective-permute-done((bf16[1,128,768]{2,1,0:T(8,128)(2,1)}, bf16[1,128,768]{2,1,0:T(8,128)(2,1)S(1)}, u32[]{:S(2)}, u32[]{:S(2)}) %collective-permute-start) | collective-permute-done | bytes 196640 | tf_op jit(solution)/shard_map/ppermute | solution.py:88
  22.2 6.1 %collective-permute-start.2 = (bf16[56,768]{1,0:T(8,128)(2,1)S(1)}, bf16[56,768]{1,0:T(8,128)(2,1)S(1)}, u32[]{:S(2)}, u32[]{:S(2)}) collective-permute-start(bf16[56,768]{1,0:T(8,128)(2,1)S(1)} %get-tuple-element.31), channel_id=1, source_target_pairs={{0,32},{4,36},{8,40},{12,44},{16,48},{20,52},{24,56},{28,60},{32,6... | collective-permute-start | bytes 258056 | tf_op jit(solution)/shard_map/ppermute | solution.py:12
  28.3 10.0 %collective-permute-start.3 = (bf16[56,768]{1,0:T(8,128)(2,1)S(1)}, bf16[56,768]{1,0:T(8,128)(2,1)S(1)}, u32[]{:S(2)}, u32[]{:S(2)}) collective-permute-start(bf16[56,768]{1,0:T(8,128)(2,1)S(1)} %get-tuple-element.30), channel_id=1, source_target_pairs={{0,80},{4,84},{8,88},{12,92},{16,64},{20,68},{24,72},{28,76},{32,1... | collective-permute-start | bytes 258056 | tf_op jit(solution)/shard_map/ppermute | solution.py:12
  38.3 5.5 %collective-permute-start.4 = (bf16[56,768]{1,0:T(8,128)(2,1)S(1)}, bf16[56,768]{1,0:T(8,128)(2,1)S(1)}, u32[]{:S(2)}, u32[]{:S(2)}) collective-permute-start(bf16[56,768]{1,0:T(8,128)(2,1)S(1)} %get-tuple-element.29), channel_id=1, source_target_pairs={{0,96},{4,100},{8,104},{12,108},{16,112},{20,116},{24,120},{28,124... | collective-permute-start | bytes 258056 | tf_op jit(solution)/shard_map/ppermute | solution.py:12
  46.8 4.2 %collective-permute-done.3 = bf16[56,768]{1,0:T(8,128)(2,1)S(1)} collective-permute-done((bf16[56,768]{1,0:T(8,128)(2,1)S(1)}, bf16[56,768]{1,0:T(8,128)(2,1)S(1)}, u32[]{:S(2)}, u32[]{:S(2)}) %collective-permute-start.3) | collective-permute-done | bytes 86048 | tf_op jit(solution)/shard_map/ppermute | solution.py:12
  50.9 2.9 %collective-permute-done.4 = bf16[56,768]{1,0:T(8,128)(2,1)S(1)} collective-permute-done((bf16[56,768]{1,0:T(8,128)(2,1)S(1)}, bf16[56,768]{1,0:T(8,128)(2,1)S(1)}, u32[]{:S(2)}, u32[]{:S(2)}) %collective-permute-start.4) | collective-permute-done | bytes 86048 | tf_op jit(solution)/shard_map/ppermute | solution.py:12
  58.8 3.3 %collective-permute-start.6 = (bf16[4,56,768]{2,1,0:T(8,128)(2,1)S(1)}, bf16[4,56,768]{2,1,0:T(8,128)(2,1)S(1)}, u32[]{:S(2)}, u32[]{:S(2)}) collective-permute-start(bf16[4,56,768]{2,1,0:T(8,128)(2,1)S(1)} %get-tuple-element.6), channel_id=1, source_target_pairs={{0,24},{4,28},{8,16},{12,20},{16,8},{20,12},{24,0},{28,4},{32,56},... | collective-permute-start | bytes 1032200 | tf_op jit(solution)/shard_map/ppermute | solution.py:12
  62.1 4.0 %collective-permute-start.18 = (bf16[4,56,768]{2,1,0:T(8,128)(2,1)S(1)}, bf16[4,56,768]{2,1,0:T(8,128)(2,1)S(1)}, u32[]{:S(2)}, u32[]{:S(2)}) collective-permute-start(bf16[4,56,768]{2,1,0:T(8,128)(2,1)S(1)} %get-tuple-element.5), channel_id=1, source_target_pairs={{0,8},{4,12},{8,0},{12,4},{16,24},{20,28},{24,16},{28,20},{32,40},... | collective-permute-start | bytes 1032200 | tf_op jit(solution)/shard_map/ppermute | solution.py:12
  66.1 13.6 %collective-permute-done.5 = bf16[4,56,768]{2,1,0:T(8,128)(2,1)S(1)} collective-permute-done((bf16[4,56,768]{2,1,0:T(8,128)(2,1)S(1)}, bf16[4,56,768]{2,1,0:T(8,128)(2,1)S(1)}, u32[]{:S(2)}, u32[]{:S(2)}) %collective-permute-start.5) | collective-permute-done | bytes 344096 | tf_op jit(solution)/shard_map/ppermute | solution.py:12
  83.5 3.9 %collective-permute-start.9 = (bf16[56,2048]{1,0:T(8,128)(2,1)S(1)}, bf16[56,2048]{1,0:T(8,128)(2,1)S(1)}, u32[]{:S(2)}, u32[]{:S(2)}) collective-permute-start(bf16[56,2048]{1,0:T(8,128)(2,1)S(1)} %get-tuple-element.10), channel_id=1, source_target_pairs={{0,3},{1,0},{2,1},{3,2},{4,7},{5,4},{6,5},{7,6},{8,11},{9,8},{10,9... | collective-permute-start | bytes 688136 | tf_op jit(solution)/shard_map/ppermute | solution.py:12
  89.6 3.1 %collective-permute-start.19 = (bf16[56,2048]{1,0:T(8,128)(2,1)S(1)}, bf16[56,2048]{1,0:T(8,128)(2,1)S(1)}, u32[]{:S(2)}, u32[]{:S(2)}) collective-permute-start(bf16[56,2048]{1,0:T(8,128)(2,1)S(1)} %get-tuple-element.11), channel_id=1, source_target_pairs={{0,1},{1,2},{2,3},{3,0},{4,5},{5,6},{6,7},{7,4},{8,9},{9,10},{10,1... | collective-permute-start | bytes 688136 | tf_op jit(solution)/shard_map/ppermute | solution.py:12
  96.5 4.3 %collective-permute-start.8 = (bf16[112,2048]{1,0:T(8,128)(2,1)S(1)}, bf16[112,2048]{1,0:T(8,128)(2,1)S(1)}, u32[]{:S(2)}, u32[]{:S(2)}) collective-permute-start(bf16[112,2048]{1,0:T(8,128)(2,1)S(1)} %pad_maximum_fusion.4), channel_id=1, source_target_pairs={{0,1},{1,2},{2,3},{3,0},{4,5},{5,6},{6,7},{7,4},{8,9},{9,10},{10,1... | collective-permute-start | bytes 1376264 | tf_op jit(solution)/shard_map/ppermute | solution.py:12
  103.7 4.5 %collective-permute-start.20 = (bf16[112,2048]{1,0:T(8,128)(2,1)S(1)}, bf16[112,2048]{1,0:T(8,128)(2,1)S(1)}, u32[]{:S(2)}, u32[]{:S(2)}) collective-permute-start(bf16[112,2048]{1,0:T(8,128)(2,1)S(1)} %pad_maximum_fusion.8), channel_id=1, source_target_pairs={{0,1},{1,2},{2,3},{3,0},{4,5},{5,6},{6,7},{7,4},{8,9},{9,10},{10,1... | collective-permute-start | bytes 1376264 | tf_op jit(solution)/shard_map/ppermute | solution.py:12
  108.3 3.6 %collective-permute-done.8 = bf16[112,2048]{1,0:T(8,128)(2,1)S(1)} collective-permute-done((bf16[112,2048]{1,0:T(8,128)(2,1)S(1)}, bf16[112,2048]{1,0:T(8,128)(2,1)S(1)}, u32[]{:S(2)}, u32[]{:S(2)}) %collective-permute-start.8) | collective-permute-done | bytes 458784 | tf_op jit(solution)/shard_map/ppermute | solution.py:12
  119.7 5.4 %collective-permute-done.22 = bf16[112,2048]{1,0:T(8,128)(2,1)S(1)} collective-permute-done((bf16[112,2048]{1,0:T(8,128)(2,1)S(1)}, bf16[112,2048]{1,0:T(8,128)(2,1)S(1)}, u32[]{:S(2)}, u32[]{:S(2)}) %collective-permute-start.22) | collective-permute-done | bytes 458784 | tf_op jit(solution)/shard_map/ppermute | solution.py:12
  130.1 6.0 %collective-permute-start.16 = (bf16[2,2,56,768]{3,2,1,0:T(8,128)(2,1)S(1)}, bf16[2,2,56,768]{3,2,1,0:T(8,128)(2,1)S(1)}, u32[]{:S(2)}, u32[]{:S(2)}) collective-permute-start(bf16[2,2,56,768]{3,2,1,0:T(8,128)(2,1)S(1)} %get-tuple-element.15), channel_id=1, source_target_pairs={{0,16},{4,20},{8,24},{12,28},{16,0},{20,4},{24,8},{28,12},{32,48},... | collective-permute-start | bytes 1032200 | tf_op jit(solution)/shard_map/ppermute | solution.py:12
  136.0 5.3 %collective-permute-start.17 = (bf16[2,2,56,768]{3,2,1,0:T(8,128)(2,1)S(1)}, bf16[2,2,56,768]{3,2,1,0:T(8,128)(2,1)S(1)}, u32[]{:S(2)}, u32[]{:S(2)}) collective-permute-start(bf16[2,2,56,768]{3,2,1,0:T(8,128)(2,1)S(1)} %get-tuple-element.16), channel_id=1, source_target_pairs={{0,24},{4,28},{8,16},{12,20},{16,8},{20,12},{24,0},{28,4},{32,56},... | collective-permute-start | bytes 1032200 | tf_op jit(solution)/shard_map/ppermute | solution.py:12
  145.7 14.0 %collective-permute-done.16 = bf16[2,2,56,768]{3,2,1,0:T(8,128)(2,1)S(1)} collective-permute-done((bf16[2,2,56,768]{3,2,1,0:T(8,128)(2,1)S(1)}, bf16[2,2,56,768]{3,2,1,0:T(8,128)(2,1)S(1)}, u32[]{:S(2)}, u32[]{:S(2)}) %collective-permute-start.16) | collective-permute-done | bytes 344096 | tf_op jit(solution)/shard_map/ppermute | solution.py:12
  159.7 7.1 %collective-permute-done.24 = bf16[2,2,56,768]{3,2,1,0:T(8,128)(2,1)S(1)} collective-permute-done((bf16[2,2,56,768]{3,2,1,0:T(8,128)(2,1)S(1)}, bf16[2,2,56,768]{3,2,1,0:T(8,128)(2,1)S(1)}, u32[]{:S(2)}, u32[]{:S(2)}) %collective-permute-start.24) | collective-permute-done | bytes 344096 | tf_op jit(solution)/shard_map/ppermute | solution.py:12
  167.0 5.3 %collective-permute-start.25 = (bf16[2,56,768]{2,1,0:T(8,128)(2,1)S(1)}, bf16[2,56,768]{2,1,0:T(8,128)(2,1)S(1)}, u32[]{:S(2)}, u32[]{:S(2)}) collective-permute-start(bf16[2,56,768]{2,1,0:T(8,128)(2,1)S(1)} %get-tuple-element.27), channel_id=1, source_target_pairs={{0,1},{1,98},{2,83},{3,32},{4,7},{5,100},{6,85},{7,38},{8,89},{9,4... | collective-permute-start | bytes 516104 | tf_op jit(solution)/shard_map/ppermute | solution.py:58
  172.4 6.0 %collective-permute-start.26 = (bf16[2,56,768]{2,1,0:T(8,128)(2,1)S(1)}, bf16[2,56,768]{2,1,0:T(8,128)(2,1)S(1)}, u32[]{:S(2)}, u32[]{:S(2)}) collective-permute-start(bf16[2,56,768]{2,1,0:T(8,128)(2,1)S(1)} %get-tuple-element.28), channel_id=1, source_target_pairs={{0,0},{1,97},{2,82},{3,35},{4,6},{5,103},{6,84},{7,37},{8,88},{9,4... | collective-permute-start | bytes 516104 | tf_op jit(solution)/shard_map/ppermute | solution.py:58
  178.4 8.4 %collective-permute-done.25 = bf16[2,56,768]{2,1,0:T(8,128)(2,1)S(1)} collective-permute-done((bf16[2,56,768]{2,1,0:T(8,128)(2,1)S(1)}, bf16[2,56,768]{2,1,0:T(8,128)(2,1)S(1)}, u32[]{:S(2)}, u32[]{:S(2)}) %collective-permute-start.25) | collective-permute-done | bytes 172064 | tf_op jit(solution)/shard_map/ppermute | solution.py:58
  186.8 4.7 %collective-permute-done.26 = bf16[2,56,768]{2,1,0:T(8,128)(2,1)S(1)} collective-permute-done((bf16[2,56,768]{2,1,0:T(8,128)(2,1)S(1)}, bf16[2,56,768]{2,1,0:T(8,128)(2,1)S(1)}, u32[]{:S(2)}, u32[]{:S(2)}) %collective-permute-start.26) | collective-permute-done | bytes 172064 | tf_op jit(solution)/shard_map/ppermute | solution.py:58
  (107 shorter events, 49.0 us)
Async XLA Ops:
  0.0 16.2 %collective-permute-start.1 = (bf16[768,1024]{1,0:T(8,128)(2,1)}, bf16[768,1024]{1,0:T(8,128)(2,1)}, u32[]{:S(2)}, u32[]{:S(2)}) collective-permute-start(bf16[768,1024]{1,0:T(8,128)(2,1)} %bitcast.161), channel_id=1, source_target_pairs={{0,4},{4,0},{8,12},{12,8},{16,20},{20,16},{24,28},{28,24},{32,36},... | collective-permute-start | bytes 4718600 | tf_op jit(solution)/shard_map/ppermute | solution.py:12
  1.9 41.9 %collective-permute-start.13 = (bf16[1024,768]{1,0:T(8,128)(2,1)}, bf16[1024,768]{1,0:T(8,128)(2,1)S(1)}, u32[]{:S(2)}, u32[]{:S(2)}) collective-permute-start(bf16[1024,768]{1,0:T(8,128)(2,1)} %bitcast.159), channel_id=1, source_target_pairs={{0,5},{1,6},{2,7},{3,4},{4,3},{5,0},{6,1},{7,2},{8,13},{9,14},{10,... | collective-permute-start | bytes 4718600 | tf_op jit(solution)/shard_map/ppermute | solution.py:58
  9.8 35.1 %collective-permute-start.12 = (bf16[1024,768]{1,0:T(8,128)(2,1)}, bf16[1024,768]{1,0:T(8,128)(2,1)S(1)}, u32[]{:S(2)}, u32[]{:S(2)}) collective-permute-start(bf16[1024,768]{1,0:T(8,128)(2,1)} %bitcast.160), channel_id=1, source_target_pairs={{0,3},{1,0},{2,1},{3,2},{4,5},{5,6},{6,7},{7,4},{8,11},{9,8},{10,9... | collective-permute-start | bytes 4718600 | tf_op jit(solution)/shard_map/ppermute | solution.py:58
  22.2 24.6 %collective-permute-start.2 = (bf16[56,768]{1,0:T(8,128)(2,1)S(1)}, bf16[56,768]{1,0:T(8,128)(2,1)S(1)}, u32[]{:S(2)}, u32[]{:S(2)}) collective-permute-start(bf16[56,768]{1,0:T(8,128)(2,1)S(1)} %get-tuple-element.31), channel_id=1, source_target_pairs={{0,32},{4,36},{8,40},{12,44},{16,48},{20,52},{24,56},{28,60},{32,6... | collective-permute-start | bytes 258056 | tf_op jit(solution)/shard_map/ppermute | solution.py:12
  28.3 22.7 %collective-permute-start.3 = (bf16[56,768]{1,0:T(8,128)(2,1)S(1)}, bf16[56,768]{1,0:T(8,128)(2,1)S(1)}, u32[]{:S(2)}, u32[]{:S(2)}) collective-permute-start(bf16[56,768]{1,0:T(8,128)(2,1)S(1)} %get-tuple-element.30), channel_id=1, source_target_pairs={{0,80},{4,84},{8,88},{12,92},{16,64},{20,68},{24,72},{28,76},{32,1... | collective-permute-start | bytes 258056 | tf_op jit(solution)/shard_map/ppermute | solution.py:12
  38.3 15.5 %collective-permute-start.4 = (bf16[56,768]{1,0:T(8,128)(2,1)S(1)}, bf16[56,768]{1,0:T(8,128)(2,1)S(1)}, u32[]{:S(2)}, u32[]{:S(2)}) collective-permute-start(bf16[56,768]{1,0:T(8,128)(2,1)S(1)} %get-tuple-element.29), channel_id=1, source_target_pairs={{0,96},{4,100},{8,104},{12,108},{16,112},{20,116},{24,120},{28,124... | collective-permute-start | bytes 258056 | tf_op jit(solution)/shard_map/ppermute | solution.py:12
  53.9 25.8 %collective-permute-start.5 = (bf16[4,56,768]{2,1,0:T(8,128)(2,1)S(1)}, bf16[4,56,768]{2,1,0:T(8,128)(2,1)S(1)}, u32[]{:S(2)}, u32[]{:S(2)}) collective-permute-start(bf16[4,56,768]{2,1,0:T(8,128)(2,1)S(1)} %get-tuple-element.6), channel_id=1, source_target_pairs={{0,16},{4,20},{8,24},{12,28},{16,0},{20,4},{24,8},{28,12},{32,48},... | collective-permute-start | bytes 1032200 | tf_op jit(solution)/shard_map/ppermute | solution.py:12
  58.0 70.2 %collective-permute-start.15 = (bf16[1024,768]{1,0:T(8,128)(2,1)S(1)}, bf16[1024,768]{1,0:T(8,128)(2,1)S(1)}, u32[]{:S(2)}, u32[]{:S(2)}) collective-permute-start(bf16[1024,768]{1,0:T(8,128)(2,1)S(1)} %broadcast_select_fusion), channel_id=1, source_target_pairs={{0,7},{1,4},{2,5},{3,6},{4,0},{5,1},{6,2},{7,3},{8,15},{9,12},{10,... | collective-permute-start | bytes 4718600 | tf_op jit(solution)/shard_map/ppermute | solution.py:58
  58.0 70.7 %collective-permute-start.14 = (bf16[1024,768]{1,0:T(8,128)(2,1)S(1)}, bf16[1024,768]{1,0:T(8,128)(2,1)S(1)}, u32[]{:S(2)}, u32[]{:S(2)}) collective-permute-start(bf16[1024,768]{1,0:T(8,128)(2,1)S(1)} %collective-permute-done.13), channel_id=1, source_target_pairs={{4,5},{5,6},{6,7},{7,4},{12,13},{13,14},{14,15},{15,12},{20,21},{2... | collective-permute-start | bytes 4718600 | tf_op jit(solution)/shard_map/ppermute | solution.py:58
  58.8 23.8 %collective-permute-start.6 = (bf16[4,56,768]{2,1,0:T(8,128)(2,1)S(1)}, bf16[4,56,768]{2,1,0:T(8,128)(2,1)S(1)}, u32[]{:S(2)}, u32[]{:S(2)}) collective-permute-start(bf16[4,56,768]{2,1,0:T(8,128)(2,1)S(1)} %get-tuple-element.6), channel_id=1, source_target_pairs={{0,24},{4,28},{8,16},{12,20},{16,8},{20,12},{24,0},{28,4},{32,56},... | collective-permute-start | bytes 1032200 | tf_op jit(solution)/shard_map/ppermute | solution.py:12
  62.1 27.5 %collective-permute-start.18 = (bf16[4,56,768]{2,1,0:T(8,128)(2,1)S(1)}, bf16[4,56,768]{2,1,0:T(8,128)(2,1)S(1)}, u32[]{:S(2)}, u32[]{:S(2)}) collective-permute-start(bf16[4,56,768]{2,1,0:T(8,128)(2,1)S(1)} %get-tuple-element.5), channel_id=1, source_target_pairs={{0,8},{4,12},{8,0},{12,4},{16,24},{20,28},{24,16},{28,20},{32,40},... | collective-permute-start | bytes 1032200 | tf_op jit(solution)/shard_map/ppermute | solution.py:12
  80.6 13.0 %collective-permute-start.7 = (bf16[56,2048]{1,0:T(8,128)(2,1)S(1)}, bf16[56,2048]{1,0:T(8,128)(2,1)S(1)}, u32[]{:S(2)}, u32[]{:S(2)}) collective-permute-start(bf16[56,2048]{1,0:T(8,128)(2,1)S(1)} %get-tuple-element.7), channel_id=1, source_target_pairs={{0,1},{1,2},{2,3},{3,0},{4,5},{5,6},{6,7},{7,4},{8,9},{9,10},{10,1... | collective-permute-start | bytes 688136 | tf_op jit(solution)/shard_map/ppermute | solution.py:12
  83.5 13.0 %collective-permute-start.9 = (bf16[56,2048]{1,0:T(8,128)(2,1)S(1)}, bf16[56,2048]{1,0:T(8,128)(2,1)S(1)}, u32[]{:S(2)}, u32[]{:S(2)}) collective-permute-start(bf16[56,2048]{1,0:T(8,128)(2,1)S(1)} %get-tuple-element.10), channel_id=1, source_target_pairs={{0,3},{1,0},{2,1},{3,2},{4,7},{5,4},{6,5},{7,6},{8,11},{9,8},{10,9... | collective-permute-start | bytes 688136 | tf_op jit(solution)/shard_map/ppermute | solution.py:12
  89.6 11.4 %collective-permute-start.19 = (bf16[56,2048]{1,0:T(8,128)(2,1)S(1)}, bf16[56,2048]{1,0:T(8,128)(2,1)S(1)}, u32[]{:S(2)}, u32[]{:S(2)}) collective-permute-start(bf16[56,2048]{1,0:T(8,128)(2,1)S(1)} %get-tuple-element.11), channel_id=1, source_target_pairs={{0,1},{1,2},{2,3},{3,0},{4,5},{5,6},{6,7},{7,4},{8,9},{9,10},{10,1... | collective-permute-start | bytes 688136 | tf_op jit(solution)/shard_map/ppermute | solution.py:12
  96.5 15.4 %collective-permute-start.8 = (bf16[112,2048]{1,0:T(8,128)(2,1)S(1)}, bf16[112,2048]{1,0:T(8,128)(2,1)S(1)}, u32[]{:S(2)}, u32[]{:S(2)}) collective-permute-start(bf16[112,2048]{1,0:T(8,128)(2,1)S(1)} %pad_maximum_fusion.4), channel_id=1, source_target_pairs={{0,1},{1,2},{2,3},{3,0},{4,5},{5,6},{6,7},{7,4},{8,9},{9,10},{10,1... | collective-permute-start | bytes 1376264 | tf_op jit(solution)/shard_map/ppermute | solution.py:12
  101.0 15.1 %collective-permute-start.10 = (bf16[112,2048]{1,0:T(8,128)(2,1)S(1)}, bf16[112,2048]{1,0:T(8,128)(2,1)S(1)}, u32[]{:S(2)}, u32[]{:S(2)}) collective-permute-start(bf16[112,2048]{1,0:T(8,128)(2,1)S(1)} %pad_maximum_fusion.5), channel_id=1, source_target_pairs={{0,3},{1,0},{2,1},{3,2},{4,7},{5,4},{6,5},{7,6},{8,11},{9,8},{10,9... | collective-permute-start | bytes 1376264 | tf_op jit(solution)/shard_map/ppermute | solution.py:12
  103.7 16.0 %collective-permute-start.20 = (bf16[112,2048]{1,0:T(8,128)(2,1)S(1)}, bf16[112,2048]{1,0:T(8,128)(2,1)S(1)}, u32[]{:S(2)}, u32[]{:S(2)}) collective-permute-start(bf16[112,2048]{1,0:T(8,128)(2,1)S(1)} %pad_maximum_fusion.8), channel_id=1, source_target_pairs={{0,1},{1,2},{2,3},{3,0},{4,5},{5,6},{6,7},{7,4},{8,9},{9,10},{10,1... | collective-permute-start | bytes 1376264 | tf_op jit(solution)/shard_map/ppermute | solution.py:12
  111.9 13.3 %collective-permute-start.22 = (bf16[112,2048]{1,0:T(8,128)(2,1)S(1)}, bf16[112,2048]{1,0:T(8,128)(2,1)S(1)}, u32[]{:S(2)}, u32[]{:S(2)}) collective-permute-start(bf16[112,2048]{1,0:T(8,128)(2,1)S(1)} %pad_maximum_fusion.9), channel_id=1, source_target_pairs={{0,3},{1,0},{2,1},{3,2},{4,7},{5,4},{6,5},{7,6},{8,11},{9,8},{10,9... | collective-permute-start | bytes 1376264 | tf_op jit(solution)/shard_map/ppermute | solution.py:12
  125.6 15.7 %collective-permute-start.23 = (bf16[112,2048]{1,0:T(8,128)(2,1)S(1)}, bf16[112,2048]{1,0:T(8,128)(2,1)S(1)}, u32[]{:S(2)}, u32[]{:S(2)}) collective-permute-start(bf16[112,2048]{1,0:T(8,128)(2,1)S(1)} %fusion.15), channel_id=1, source_target_pairs={{0,4},{4,0},{8,12},{12,8},{16,20},{20,16},{24,28},{28,24},{32,36},... | collective-permute-start | bytes 1376264 | tf_op jit(solution)/shard_map/ppermute | solution.py:12
  130.1 29.7 %collective-permute-start.16 = (bf16[2,2,56,768]{3,2,1,0:T(8,128)(2,1)S(1)}, bf16[2,2,56,768]{3,2,1,0:T(8,128)(2,1)S(1)}, u32[]{:S(2)}, u32[]{:S(2)}) collective-permute-start(bf16[2,2,56,768]{3,2,1,0:T(8,128)(2,1)S(1)} %get-tuple-element.15), channel_id=1, source_target_pairs={{0,16},{4,20},{8,24},{12,28},{16,0},{20,4},{24,8},{28,12},{32,48},... | collective-permute-start | bytes 1032200 | tf_op jit(solution)/shard_map/ppermute | solution.py:12
  136.0 23.7 %collective-permute-start.17 = (bf16[2,2,56,768]{3,2,1,0:T(8,128)(2,1)S(1)}, bf16[2,2,56,768]{3,2,1,0:T(8,128)(2,1)S(1)}, u32[]{:S(2)}, u32[]{:S(2)}) collective-permute-start(bf16[2,2,56,768]{3,2,1,0:T(8,128)(2,1)S(1)} %get-tuple-element.16), channel_id=1, source_target_pairs={{0,24},{4,28},{8,16},{12,20},{16,8},{20,12},{24,0},{28,4},{32,56},... | collective-permute-start | bytes 1032200 | tf_op jit(solution)/shard_map/ppermute | solution.py:12
  143.8 23.0 %collective-permute-start.24 = (bf16[2,2,56,768]{3,2,1,0:T(8,128)(2,1)S(1)}, bf16[2,2,56,768]{3,2,1,0:T(8,128)(2,1)S(1)}, u32[]{:S(2)}, u32[]{:S(2)}) collective-permute-start(bf16[2,2,56,768]{3,2,1,0:T(8,128)(2,1)S(1)} %fusion.31), channel_id=1, source_target_pairs={{0,8},{4,12},{8,0},{12,4},{16,24},{20,28},{24,16},{28,20},{32,40},... | collective-permute-start | bytes 1032200 | tf_op jit(solution)/shard_map/ppermute | solution.py:12
  167.0 19.7 %collective-permute-start.25 = (bf16[2,56,768]{2,1,0:T(8,128)(2,1)S(1)}, bf16[2,56,768]{2,1,0:T(8,128)(2,1)S(1)}, u32[]{:S(2)}, u32[]{:S(2)}) collective-permute-start(bf16[2,56,768]{2,1,0:T(8,128)(2,1)S(1)} %get-tuple-element.27), channel_id=1, source_target_pairs={{0,1},{1,98},{2,83},{3,32},{4,7},{5,100},{6,85},{7,38},{8,89},{9,4... | collective-permute-start | bytes 516104 | tf_op jit(solution)/shard_map/ppermute | solution.py:58
  172.4 19.1 %collective-permute-start.26 = (bf16[2,56,768]{2,1,0:T(8,128)(2,1)S(1)}, bf16[2,56,768]{2,1,0:T(8,128)(2,1)S(1)}, u32[]{:S(2)}, u32[]{:S(2)}) collective-permute-start(bf16[2,56,768]{2,1,0:T(8,128)(2,1)S(1)} %get-tuple-element.28), channel_id=1, source_target_pairs={{0,0},{1,97},{2,82},{3,35},{4,6},{5,103},{6,84},{7,37},{8,88},{9,4... | collective-permute-start | bytes 516104 | tf_op jit(solution)/shard_map/ppermute | solution.py:58
  (7 other events, 113.9 us)

commit v7 on v6

--- a/solution.py
+++ b/solution.py
@@ -142,11 +142,10 @@
     def hidden_part(m):
         rows = chunk if m == 0 else swapped_chips(near_chunk if m == 1 else chunk, m)
         arrivals.append(rows)
-        if m == 0:
-            rows = after(rows, arrivals[0])
         flat = rows.reshape(4 * ROW_LIMIT, width)
         part = jnp.dot(flat, up, preferred_element_type=jnp.float32).astype(jnp.bfloat16)
-        return part.reshape(4, ROW_LIMIT, 2 * ff)
+        part = part.reshape(4, ROW_LIMIT, 2 * ff)
+        return after(part, arrivals[0]) if m == 0 else part
 
     def times_down(own_units, other_units):
         core_units = jnp.where(core == 0, own_units, other_units), jnp.where(core == 0, other_units, own_units)

time: 199 us -> 199 us (level)
  no operation moved by 1% of the time
where the time goes in v7:
time: 199 us; the launch traced here: 196 us
  starting transfers between devices  99.9 us (50%)
  waiting for transfers between devices  73.5 us (37%)
  matrix products  9.52 us (5%)
  other arithmetic  5.67 us (3%)
  between operations  4.18 us (2%)
  local copies, waits for them, and re-layouts  3.28 us (2%)
    ppermute x21, starting transfers between devices, moved(): return lax.ppermute(value, axis, list(enumerate(targets)))  76.1 us
    ppermute x21, waiting for transfers between devices, moved(): return lax.ppermute(value, axis, list(enumerate(targets)))  56 us
    ppermute x6, starting transfers between devices, between_devices(): return lax.ppermute(value, ('expert', 'cuts'), pairs)  21.9 us
    ppermute x6, waiting for transfers between devices, between_devices(): return lax.ppermute(value, ('expert', 'cuts'), pairs)  13.7 us
    dot_general x8, matrix products, times_down(): jnp.dot(u, w, preferred_element_type=jnp.float32)  4.45 us
  transfers between devices with their start and end apart: 28, of which 15 were waited for; matrix products, arithmetic and copies ran while one was open for 9% of the time, Pallas kernels for 0%

profile of v7, /device:TPU:6, one launch (start us, length us, event | category | flops | bytes accessed | tf_op | source)
XLA Modules:
  0.0 196.0 jit_solution(15581658316519422216)
XLA Ops:
  1.9 7.9 %collective-permute-start.13 = (bf16[1024,768]{1,0:T(8,128)(2,1)}, bf16[1024,768]{1,0:T(8,128)(2,1)S(1)}, u32[]{:S(2)}, u32[]{:S(2)}) collective-permute-start(bf16[1024,768]{1,0:T(8,128)(2,1)} %bitcast.159), channel_id=1, source_target_pairs={{0,5},{1,6},{2,7},{3,4},{4,3},{5,0},{6,1},{7,2},{8,13},{9,14},{10,... | collective-permute-start | bytes 4718600 | tf_op jit(solution)/shard_map/ppermute | solution.py:58
  18.1 3.8 %collective-permute-done = bf16[1,128,768]{2,1,0:T(8,128)(2,1)S(1)} collective-permute-done((bf16[1,128,768]{2,1,0:T(8,128)(2,1)}, bf16[1,128,768]{2,1,0:T(8,128)(2,1)S(1)}, u32[]{:S(2)}, u32[]{:S(2)}) %collective-permute-start) | collective-permute-done | bytes 196640 | tf_op jit(solution)/shard_map/ppermute | solution.py:88
  22.2 6.1 %collective-permute-start.2 = (bf16[56,768]{1,0:T(8,128)(2,1)S(1)}, bf16[56,768]{1,0:T(8,128)(2,1)S(1)}, u32[]{:S(2)}, u32[]{:S(2)}) collective-permute-start(bf16[56,768]{1,0:T(8,128)(2,1)S(1)} %get-tuple-element.31), channel_id=1, source_target_pairs={{0,32},{4,36},{8,40},{12,44},{16,48},{20,52},{24,56},{28,60},{32,6... | collective-permute-start | bytes 258056 | tf_op jit(solution)/shard_map/ppermute | solution.py:12
  28.3 10.0 %collective-permute-start.3 = (bf16[56,768]{1,0:T(8,128)(2,1)S(1)}, bf16[56,768]{1,0:T(8,128)(2,1)S(1)}, u32[]{:S(2)}, u32[]{:S(2)}) collective-permute-start(bf16[56,768]{1,0:T(8,128)(2,1)S(1)} %get-tuple-element.30), channel_id=1, source_target_pairs={{0,80},{4,84},{8,88},{12,92},{16,64},{20,68},{24,72},{28,76},{32,1... | collective-permute-start | bytes 258056 | tf_op jit(solution)/shard_map/ppermute | solution.py:12
  38.3 5.5 %collective-permute-start.4 = (bf16[56,768]{1,0:T(8,128)(2,1)S(1)}, bf16[56,768]{1,0:T(8,128)(2,1)S(1)}, u32[]{:S(2)}, u32[]{:S(2)}) collective-permute-start(bf16[56,768]{1,0:T(8,128)(2,1)S(1)} %get-tuple-element.29), channel_id=1, source_target_pairs={{0,96},{4,100},{8,104},{12,108},{16,112},{20,116},{24,120},{28,124... | collective-permute-start | bytes 258056 | tf_op jit(solution)/shard_map/ppermute | solution.py:12
  46.8 4.2 %collective-permute-done.3 = bf16[56,768]{1,0:T(8,128)(2,1)S(1)} collective-permute-done((bf16[56,768]{1,0:T(8,128)(2,1)S(1)}, bf16[56,768]{1,0:T(8,128)(2,1)S(1)}, u32[]{:S(2)}, u32[]{:S(2)}) %collective-permute-start.3) | collective-permute-done | bytes 86048 | tf_op jit(solution)/shard_map/ppermute | solution.py:12
  50.9 2.9 %collective-permute-done.4 = bf16[56,768]{1,0:T(8,128)(2,1)S(1)} collective-permute-done((bf16[56,768]{1,0:T(8,128)(2,1)S(1)}, bf16[56,768]{1,0:T(8,128)(2,1)S(1)}, u32[]{:S(2)}, u32[]{:S(2)}) %collective-permute-start.4) | collective-permute-done | bytes 86048 | tf_op jit(solution)/shard_map/ppermute | solution.py:12
  58.8 3.3 %collective-permute-start.6 = (bf16[4,56,768]{2,1,0:T(8,128)(2,1)S(1)}, bf16[4,56,768]{2,1,0:T(8,128)(2,1)S(1)}, u32[]{:S(2)}, u32[]{:S(2)}) collective-permute-start(bf16[4,56,768]{2,1,0:T(8,128)(2,1)S(1)} %get-tuple-element.6), channel_id=1, source_target_pairs={{0,24},{4,28},{8,16},{12,20},{16,8},{20,12},{24,0},{28,4},{32,56},... | collective-permute-start | bytes 1032200 | tf_op jit(solution)/shard_map/ppermute | solution.py:12
  62.1 4.0 %collective-permute-start.18 = (bf16[4,56,768]{2,1,0:T(8,128)(2,1)S(1)}, bf16[4,56,768]{2,1,0:T(8,128)(2,1)S(1)}, u32[]{:S(2)}, u32[]{:S(2)}) collective-permute-start(bf16[4,56,768]{2,1,0:T(8,128)(2,1)S(1)} %get-tuple-element.5), channel_id=1, source_target_pairs={{0,8},{4,12},{8,0},{12,4},{16,24},{20,28},{24,16},{28,20},{32,40},... | collective-permute-start | bytes 1032200 | tf_op jit(solution)/shard_map/ppermute | solution.py:12
  66.1 13.6 %collective-permute-done.5 = bf16[4,56,768]{2,1,0:T(8,128)(2,1)S(1)} collective-permute-done((bf16[4,56,768]{2,1,0:T(8,128)(2,1)S(1)}, bf16[4,56,768]{2,1,0:T(8,128)(2,1)S(1)}, u32[]{:S(2)}, u32[]{:S(2)}) %collective-permute-start.5) | collective-permute-done | bytes 344096 | tf_op jit(solution)/shard_map/ppermute | solution.py:12
  83.5 3.9 %collective-permute-start.9 = (bf16[56,2048]{1,0:T(8,128)(2,1)S(1)}, bf16[56,2048]{1,0:T(8,128)(2,1)S(1)}, u32[]{:S(2)}, u32[]{:S(2)}) collective-permute-start(bf16[56,2048]{1,0:T(8,128)(2,1)S(1)} %get-tuple-element.10), channel_id=1, source_target_pairs={{0,3},{1,0},{2,1},{3,2},{4,7},{5,4},{6,5},{7,6},{8,11},{9,8},{10,9... | collective-permute-start | bytes 688136 | tf_op jit(solution)/shard_map/ppermute | solution.py:12
  89.6 3.1 %collective-permute-start.19 = (bf16[56,2048]{1,0:T(8,128)(2,1)S(1)}, bf16[56,2048]{1,0:T(8,128)(2,1)S(1)}, u32[]{:S(2)}, u32[]{:S(2)}) collective-permute-start(bf16[56,2048]{1,0:T(8,128)(2,1)S(1)} %get-tuple-element.11), channel_id=1, source_target_pairs={{0,1},{1,2},{2,3},{3,0},{4,5},{5,6},{6,7},{7,4},{8,9},{9,10},{10,1... | collective-permute-start | bytes 688136 | tf_op jit(solution)/shard_map/ppermute | solution.py:12
  96.5 4.3 %collective-permute-start.8 = (bf16[112,2048]{1,0:T(8,128)(2,1)S(1)}, bf16[112,2048]{1,0:T(8,128)(2,1)S(1)}, u32[]{:S(2)}, u32[]{:S(2)}) collective-permute-start(bf16[112,2048]{1,0:T(8,128)(2,1)S(1)} %pad_maximum_fusion.4), channel_id=1, source_target_pairs={{0,1},{1,2},{2,3},{3,0},{4,5},{5,6},{6,7},{7,4},{8,9},{9,10},{10,1... | collective-permute-start | bytes 1376264 | tf_op jit(solution)/shard_map/ppermute | solution.py:12
  103.6 4.5 %collective-permute-start.20 = (bf16[112,2048]{1,0:T(8,128)(2,1)S(1)}, bf16[112,2048]{1,0:T(8,128)(2,1)S(1)}, u32[]{:S(2)}, u32[]{:S(2)}) collective-permute-start(bf16[112,2048]{1,0:T(8,128)(2,1)S(1)} %pad_maximum_fusion.8), channel_id=1, source_target_pairs={{0,1},{1,2},{2,3},{3,0},{4,5},{5,6},{6,7},{7,4},{8,9},{9,10},{10,1... | collective-permute-start | bytes 1376264 | tf_op jit(solution)/shard_map/ppermute | solution.py:12
  108.2 3.6 %collective-permute-done.8 = bf16[112,2048]{1,0:T(8,128)(2,1)S(1)} collective-permute-done((bf16[112,2048]{1,0:T(8,128)(2,1)S(1)}, bf16[112,2048]{1,0:T(8,128)(2,1)S(1)}, u32[]{:S(2)}, u32[]{:S(2)}) %collective-permute-start.8) | collective-permute-done | bytes 458784 | tf_op jit(solution)/shard_map/ppermute | solution.py:12
  119.7 5.4 %collective-permute-done.22 = bf16[112,2048]{1,0:T(8,128)(2,1)S(1)} collective-permute-done((bf16[112,2048]{1,0:T(8,128)(2,1)S(1)}, bf16[112,2048]{1,0:T(8,128)(2,1)S(1)}, u32[]{:S(2)}, u32[]{:S(2)}) %collective-permute-start.22) | collective-permute-done | bytes 458784 | tf_op jit(solution)/shard_map/ppermute | solution.py:12
  130.0 6.0 %collective-permute-start.16 = (bf16[2,2,56,768]{3,2,1,0:T(8,128)(2,1)S(1)}, bf16[2,2,56,768]{3,2,1,0:T(8,128)(2,1)S(1)}, u32[]{:S(2)}, u32[]{:S(2)}) collective-permute-start(bf16[2,2,56,768]{3,2,1,0:T(8,128)(2,1)S(1)} %get-tuple-element.15), channel_id=1, source_target_pairs={{0,16},{4,20},{8,24},{12,28},{16,0},{20,4},{24,8},{28,12},{32,48},... | collective-permute-start | bytes 1032200 | tf_op jit(solution)/shard_map/ppermute | solution.py:12
  136.0 5.3 %collective-permute-start.17 = (bf16[2,2,56,768]{3,2,1,0:T(8,128)(2,1)S(1)}, bf16[2,2,56,768]{3,2,1,0:T(8,128)(2,1)S(1)}, u32[]{:S(2)}, u32[]{:S(2)}) collective-permute-start(bf16[2,2,56,768]{3,2,1,0:T(8,128)(2,1)S(1)} %get-tuple-element.16), channel_id=1, source_target_pairs={{0,24},{4,28},{8,16},{12,20},{16,8},{20,12},{24,0},{28,4},{32,56},... | collective-permute-start | bytes 1032200 | tf_op jit(solution)/shard_map/ppermute | solution.py:12
  145.7 14.0 %collective-permute-done.16 = bf16[2,2,56,768]{3,2,1,0:T(8,128)(2,1)S(1)} collective-permute-done((bf16[2,2,56,768]{3,2,1,0:T(8,128)(2,1)S(1)}, bf16[2,2,56,768]{3,2,1,0:T(8,128)(2,1)S(1)}, u32[]{:S(2)}, u32[]{:S(2)}) %collective-permute-start.16) | collective-permute-done | bytes 344096 | tf_op jit(solution)/shard_map/ppermute | solution.py:12
  159.7 7.1 %collective-permute-done.24 = bf16[2,2,56,768]{3,2,1,0:T(8,128)(2,1)S(1)} collective-permute-done((bf16[2,2,56,768]{3,2,1,0:T(8,128)(2,1)S(1)}, bf16[2,2,56,768]{3,2,1,0:T(8,128)(2,1)S(1)}, u32[]{:S(2)}, u32[]{:S(2)}) %collective-permute-start.24) | collective-permute-done | bytes 344096 | tf_op jit(solution)/shard_map/ppermute | solution.py:12
  167.0 5.3 %collective-permute-start.25 = (bf16[2,56,768]{2,1,0:T(8,128)(2,1)S(1)}, bf16[2,56,768]{2,1,0:T(8,128)(2,1)S(1)}, u32[]{:S(2)}, u32[]{:S(2)}) collective-permute-start(bf16[2,56,768]{2,1,0:T(8,128)(2,1)S(1)} %get-tuple-element.27), channel_id=1, source_target_pairs={{0,1},{1,98},{2,83},{3,32},{4,7},{5,100},{6,85},{7,38},{8,89},{9,4... | collective-permute-start | bytes 516104 | tf_op jit(solution)/shard_map/ppermute | solution.py:58
  172.3 6.0 %collective-permute-start.26 = (bf16[2,56,768]{2,1,0:T(8,128)(2,1)S(1)}, bf16[2,56,768]{2,1,0:T(8,128)(2,1)S(1)}, u32[]{:S(2)}, u32[]{:S(2)}) collective-permute-start(bf16[2,56,768]{2,1,0:T(8,128)(2,1)S(1)} %get-tuple-element.28), channel_id=1, source_target_pairs={{0,0},{1,97},{2,82},{3,35},{4,6},{5,103},{6,84},{7,37},{8,88},{9,4... | collective-permute-start | bytes 516104 | tf_op jit(solution)/shard_map/ppermute | solution.py:58
  178.3 8.4 %collective-permute-done.25 = bf16[2,56,768]{2,1,0:T(8,128)(2,1)S(1)} collective-permute-done((bf16[2,56,768]{2,1,0:T(8,128)(2,1)S(1)}, bf16[2,56,768]{2,1,0:T(8,128)(2,1)S(1)}, u32[]{:S(2)}, u32[]{:S(2)}) %collective-permute-start.25) | collective-permute-done | bytes 172064 | tf_op jit(solution)/shard_map/ppermute | solution.py:58
  186.7 4.7 %collective-permute-done.26 = bf16[2,56,768]{2,1,0:T(8,128)(2,1)S(1)} collective-permute-done((bf16[2,56,768]{2,1,0:T(8,128)(2,1)S(1)}, bf16[2,56,768]{2,1,0:T(8,128)(2,1)S(1)}, u32[]{:S(2)}, u32[]{:S(2)}) %collective-permute-start.26) | collective-permute-done | bytes 172064 | tf_op jit(solution)/shard_map/ppermute | solution.py:58
  (106 shorter events, 49.0 us)
Async XLA Ops:
  0.0 16.2 %collective-permute-start.1 = (bf16[768,1024]{1,0:T(8,128)(2,1)}, bf16[768,1024]{1,0:T(8,128)(2,1)}, u32[]{:S(2)}, u32[]{:S(2)}) collective-permute-start(bf16[768,1024]{1,0:T(8,128)(2,1)} %bitcast.161), channel_id=1, source_target_pairs={{0,4},{4,0},{8,12},{12,8},{16,20},{20,16},{24,28},{28,24},{32,36},... | collective-permute-start | bytes 4718600 | tf_op jit(solution)/shard_map/ppermute | solution.py:12
  1.9 41.9 %collective-permute-start.13 = (bf16[1024,768]{1,0:T(8,128)(2,1)}, bf16[1024,768]{1,0:T(8,128)(2,1)S(1)}, u32[]{:S(2)}, u32[]{:S(2)}) collective-permute-start(bf16[1024,768]{1,0:T(8,128)(2,1)} %bitcast.159), channel_id=1, source_target_pairs={{0,5},{1,6},{2,7},{3,4},{4,3},{5,0},{6,1},{7,2},{8,13},{9,14},{10,... | collective-permute-start | bytes 4718600 | tf_op jit(solution)/shard_map/ppermute | solution.py:58
  9.8 35.1 %collective-permute-start.12 = (bf16[1024,768]{1,0:T(8,128)(2,1)}, bf16[1024,768]{1,0:T(8,128)(2,1)S(1)}, u32[]{:S(2)}, u32[]{:S(2)}) collective-permute-start(bf16[1024,768]{1,0:T(8,128)(2,1)} %bitcast.160), channel_id=1, source_target_pairs={{0,3},{1,0},{2,1},{3,2},{4,5},{5,6},{6,7},{7,4},{8,11},{9,8},{10,9... | collective-permute-start | bytes 4718600 | tf_op jit(solution)/shard_map/ppermute | solution.py:58
  22.2 24.6 %collective-permute-start.2 = (bf16[56,768]{1,0:T(8,128)(2,1)S(1)}, bf16[56,768]{1,0:T(8,128)(2,1)S(1)}, u32[]{:S(2)}, u32[]{:S(2)}) collective-permute-start(bf16[56,768]{1,0:T(8,128)(2,1)S(1)} %get-tuple-element.31), channel_id=1, source_target_pairs={{0,32},{4,36},{8,40},{12,44},{16,48},{20,52},{24,56},{28,60},{32,6... | collective-permute-start | bytes 258056 | tf_op jit(solution)/shard_map/ppermute | solution.py:12
  28.3 22.7 %collective-permute-start.3 = (bf16[56,768]{1,0:T(8,128)(2,1)S(1)}, bf16[56,768]{1,0:T(8,128)(2,1)S(1)}, u32[]{:S(2)}, u32[]{:S(2)}) collective-permute-start(bf16[56,768]{1,0:T(8,128)(2,1)S(1)} %get-tuple-element.30), channel_id=1, source_target_pairs={{0,80},{4,84},{8,88},{12,92},{16,64},{20,68},{24,72},{28,76},{32,1... | collective-permute-start | bytes 258056 | tf_op jit(solution)/shard_map/ppermute | solution.py:12
  38.3 15.5 %collective-permute-start.4 = (bf16[56,768]{1,0:T(8,128)(2,1)S(1)}, bf16[56,768]{1,0:T(8,128)(2,1)S(1)}, u32[]{:S(2)}, u32[]{:S(2)}) collective-permute-start(bf16[56,768]{1,0:T(8,128)(2,1)S(1)} %get-tuple-element.29), channel_id=1, source_target_pairs={{0,96},{4,100},{8,104},{12,108},{16,112},{20,116},{24,120},{28,124... | collective-permute-start | bytes 258056 | tf_op jit(solution)/shard_map/ppermute | solution.py:12
  53.9 25.8 %collective-permute-start.5 = (bf16[4,56,768]{2,1,0:T(8,128)(2,1)S(1)}, bf16[4,56,768]{2,1,0:T(8,128)(2,1)S(1)}, u32[]{:S(2)}, u32[]{:S(2)}) collective-permute-start(bf16[4,56,768]{2,1,0:T(8,128)(2,1)S(1)} %get-tuple-element.6), channel_id=1, source_target_pairs={{0,16},{4,20},{8,24},{12,28},{16,0},{20,4},{24,8},{28,12},{32,48},... | collective-permute-start | bytes 1032200 | tf_op jit(solution)/shard_map/ppermute | solution.py:12
  58.0 70.2 %collective-permute-start.15 = (bf16[1024,768]{1,0:T(8,128)(2,1)S(1)}, bf16[1024,768]{1,0:T(8,128)(2,1)S(1)}, u32[]{:S(2)}, u32[]{:S(2)}) collective-permute-start(bf16[1024,768]{1,0:T(8,128)(2,1)S(1)} %broadcast_select_fusion), channel_id=1, source_target_pairs={{0,7},{1,4},{2,5},{3,6},{4,0},{5,1},{6,2},{7,3},{8,15},{9,12},{10,... | collective-permute-start | bytes 4718600 | tf_op jit(solution)/shard_map/ppermute | solution.py:58
  58.0 70.7 %collective-permute-start.14 = (bf16[1024,768]{1,0:T(8,128)(2,1)S(1)}, bf16[1024,768]{1,0:T(8,128)(2,1)S(1)}, u32[]{:S(2)}, u32[]{:S(2)}) collective-permute-start(bf16[1024,768]{1,0:T(8,128)(2,1)S(1)} %collective-permute-done.13), channel_id=1, source_target_pairs={{4,5},{5,6},{6,7},{7,4},{12,13},{13,14},{14,15},{15,12},{20,21},{2... | collective-permute-start | bytes 4718600 | tf_op jit(solution)/shard_map/ppermute | solution.py:58
  58.8 23.8 %collective-permute-start.6 = (bf16[4,56,768]{2,1,0:T(8,128)(2,1)S(1)}, bf16[4,56,768]{2,1,0:T(8,128)(2,1)S(1)}, u32[]{:S(2)}, u32[]{:S(2)}) collective-permute-start(bf16[4,56,768]{2,1,0:T(8,128)(2,1)S(1)} %get-tuple-element.6), channel_id=1, source_target_pairs={{0,24},{4,28},{8,16},{12,20},{16,8},{20,12},{24,0},{28,4},{32,56},... | collective-permute-start | bytes 1032200 | tf_op jit(solution)/shard_map/ppermute | solution.py:12
  62.1 27.4 %collective-permute-start.18 = (bf16[4,56,768]{2,1,0:T(8,128)(2,1)S(1)}, bf16[4,56,768]{2,1,0:T(8,128)(2,1)S(1)}, u32[]{:S(2)}, u32[]{:S(2)}) collective-permute-start(bf16[4,56,768]{2,1,0:T(8,128)(2,1)S(1)} %get-tuple-element.5), channel_id=1, source_target_pairs={{0,8},{4,12},{8,0},{12,4},{16,24},{20,28},{24,16},{28,20},{32,40},... | collective-permute-start | bytes 1032200 | tf_op jit(solution)/shard_map/ppermute | solution.py:12
  80.6 13.0 %collective-permute-start.7 = (bf16[56,2048]{1,0:T(8,128)(2,1)S(1)}, bf16[56,2048]{1,0:T(8,128)(2,1)S(1)}, u32[]{:S(2)}, u32[]{:S(2)}) collective-permute-start(bf16[56,2048]{1,0:T(8,128)(2,1)S(1)} %get-tuple-element.7), channel_id=1, source_target_pairs={{0,1},{1,2},{2,3},{3,0},{4,5},{5,6},{6,7},{7,4},{8,9},{9,10},{10,1... | collective-permute-start | bytes 688136 | tf_op jit(solution)/shard_map/ppermute | solution.py:12
  83.5 13.0 %collective-permute-start.9 = (bf16[56,2048]{1,0:T(8,128)(2,1)S(1)}, bf16[56,2048]{1,0:T(8,128)(2,1)S(1)}, u32[]{:S(2)}, u32[]{:S(2)}) collective-permute-start(bf16[56,2048]{1,0:T(8,128)(2,1)S(1)} %get-tuple-element.10), channel_id=1, source_target_pairs={{0,3},{1,0},{2,1},{3,2},{4,7},{5,4},{6,5},{7,6},{8,11},{9,8},{10,9... | collective-permute-start | bytes 688136 | tf_op jit(solution)/shard_map/ppermute | solution.py:12
  89.6 11.4 %collective-permute-start.19 = (bf16[56,2048]{1,0:T(8,128)(2,1)S(1)}, bf16[56,2048]{1,0:T(8,128)(2,1)S(1)}, u32[]{:S(2)}, u32[]{:S(2)}) collective-permute-start(bf16[56,2048]{1,0:T(8,128)(2,1)S(1)} %get-tuple-element.11), channel_id=1, source_target_pairs={{0,1},{1,2},{2,3},{3,0},{4,5},{5,6},{6,7},{7,4},{8,9},{9,10},{10,1... | collective-permute-start | bytes 688136 | tf_op jit(solution)/shard_map/ppermute | solution.py:12
  96.5 15.3 %collective-permute-start.8 = (bf16[112,2048]{1,0:T(8,128)(2,1)S(1)}, bf16[112,2048]{1,0:T(8,128)(2,1)S(1)}, u32[]{:S(2)}, u32[]{:S(2)}) collective-permute-start(bf16[112,2048]{1,0:T(8,128)(2,1)S(1)} %pad_maximum_fusion.4), channel_id=1, source_target_pairs={{0,1},{1,2},{2,3},{3,0},{4,5},{5,6},{6,7},{7,4},{8,9},{9,10},{10,1... | collective-permute-start | bytes 1376264 | tf_op jit(solution)/shard_map/ppermute | solution.py:12
  100.9 15.1 %collective-permute-start.10 = (bf16[112,2048]{1,0:T(8,128)(2,1)S(1)}, bf16[112,2048]{1,0:T(8,128)(2,1)S(1)}, u32[]{:S(2)}, u32[]{:S(2)}) collective-permute-start(bf16[112,2048]{1,0:T(8,128)(2,1)S(1)} %pad_maximum_fusion.5), channel_id=1, source_target_pairs={{0,3},{1,0},{2,1},{3,2},{4,7},{5,4},{6,5},{7,6},{8,11},{9,8},{10,9... | collective-permute-start | bytes 1376264 | tf_op jit(solution)/shard_map/ppermute | solution.py:12
  103.6 16.0 %collective-permute-start.20 = (bf16[112,2048]{1,0:T(8,128)(2,1)S(1)}, bf16[112,2048]{1,0:T(8,128)(2,1)S(1)}, u32[]{:S(2)}, u32[]{:S(2)}) collective-permute-start(bf16[112,2048]{1,0:T(8,128)(2,1)S(1)} %pad_maximum_fusion.8), channel_id=1, source_target_pairs={{0,1},{1,2},{2,3},{3,0},{4,5},{5,6},{6,7},{7,4},{8,9},{9,10},{10,1... | collective-permute-start | bytes 1376264 | tf_op jit(solution)/shard_map/ppermute | solution.py:12
  111.8 13.3 %collective-permute-start.22 = (bf16[112,2048]{1,0:T(8,128)(2,1)S(1)}, bf16[112,2048]{1,0:T(8,128)(2,1)S(1)}, u32[]{:S(2)}, u32[]{:S(2)}) collective-permute-start(bf16[112,2048]{1,0:T(8,128)(2,1)S(1)} %pad_maximum_fusion.9), channel_id=1, source_target_pairs={{0,3},{1,0},{2,1},{3,2},{4,7},{5,4},{6,5},{7,6},{8,11},{9,8},{10,9... | collective-permute-start | bytes 1376264 | tf_op jit(solution)/shard_map/ppermute | solution.py:12
  125.5 15.7 %collective-permute-start.23 = (bf16[112,2048]{1,0:T(8,128)(2,1)S(1)}, bf16[112,2048]{1,0:T(8,128)(2,1)S(1)}, u32[]{:S(2)}, u32[]{:S(2)}) collective-permute-start(bf16[112,2048]{1,0:T(8,128)(2,1)S(1)} %fusion.16), channel_id=1, source_target_pairs={{0,4},{4,0},{8,12},{12,8},{16,20},{20,16},{24,28},{28,24},{32,36},... | collective-permute-start | bytes 1376264 | tf_op jit(solution)/shard_map/ppermute | solution.py:12
  130.0 29.7 %collective-permute-start.16 = (bf16[2,2,56,768]{3,2,1,0:T(8,128)(2,1)S(1)}, bf16[2,2,56,768]{3,2,1,0:T(8,128)(2,1)S(1)}, u32[]{:S(2)}, u32[]{:S(2)}) collective-permute-start(bf16[2,2,56,768]{3,2,1,0:T(8,128)(2,1)S(1)} %get-tuple-element.15), channel_id=1, source_target_pairs={{0,16},{4,20},{8,24},{12,28},{16,0},{20,4},{24,8},{28,12},{32,48},... | collective-permute-start | bytes 1032200 | tf_op jit(solution)/shard_map/ppermute | solution.py:12
  136.0 23.7 %collective-permute-start.17 = (bf16[2,2,56,768]{3,2,1,0:T(8,128)(2,1)S(1)}, bf16[2,2,56,768]{3,2,1,0:T(8,128)(2,1)S(1)}, u32[]{:S(2)}, u32[]{:S(2)}) collective-permute-start(bf16[2,2,56,768]{3,2,1,0:T(8,128)(2,1)S(1)} %get-tuple-element.16), channel_id=1, source_target_pairs={{0,24},{4,28},{8,16},{12,20},{16,8},{20,12},{24,0},{28,4},{32,56},... | collective-permute-start | bytes 1032200 | tf_op jit(solution)/shard_map/ppermute | solution.py:12
  143.8 23.0 %collective-permute-start.24 = (bf16[2,2,56,768]{3,2,1,0:T(8,128)(2,1)S(1)}, bf16[2,2,56,768]{3,2,1,0:T(8,128)(2,1)S(1)}, u32[]{:S(2)}, u32[]{:S(2)}) collective-permute-start(bf16[2,2,56,768]{3,2,1,0:T(8,128)(2,1)S(1)} %fusion.32), channel_id=1, source_target_pairs={{0,8},{4,12},{8,0},{12,4},{16,24},{20,28},{24,16},{28,20},{32,40},... | collective-permute-start | bytes 1032200 | tf_op jit(solution)/shard_map/ppermute | solution.py:12
  167.0 19.7 %collective-permute-start.25 = (bf16[2,56,768]{2,1,0:T(8,128)(2,1)S(1)}, bf16[2,56,768]{2,1,0:T(8,128)(2,1)S(1)}, u32[]{:S(2)}, u32[]{:S(2)}) collective-permute-start(bf16[2,56,768]{2,1,0:T(8,128)(2,1)S(1)} %get-tuple-element.27), channel_id=1, source_target_pairs={{0,1},{1,98},{2,83},{3,32},{4,7},{5,100},{6,85},{7,38},{8,89},{9,4... | collective-permute-start | bytes 516104 | tf_op jit(solution)/shard_map/ppermute | solution.py:58
  172.3 19.1 %collective-permute-start.26 = (bf16[2,56,768]{2,1,0:T(8,128)(2,1)S(1)}, bf16[2,56,768]{2,1,0:T(8,128)(2,1)S(1)}, u32[]{:S(2)}, u32[]{:S(2)}) collective-permute-start(bf16[2,56,768]{2,1,0:T(8,128)(2,1)S(1)} %get-tuple-element.28), channel_id=1, source_target_pairs={{0,0},{1,97},{2,82},{3,35},{4,6},{5,103},{6,84},{7,37},{8,88},{9,4... | collective-permute-start | bytes 516104 | tf_op jit(solution)/shard_map/ppermute | solution.py:58
  (7 other events, 113.9 us)
